TPU v7x, 256 devices: a whole 4x4x8 slice. The times are simulated.
256 devices in a mesh: grp: 8 (over x, core), tile: 32 (over z, y).
Axes of the slice: x: 4, y: 4, z: 8, core: 2. Of those that a mesh axis runs over, the one named last changes fastest.
Arguments:
- fwd_start: float32 [8, 4, 256, 64, 256], P('grp', None, 'tile'), may hold values from -0.2 to 0.2
- adj_start: float32 [8, 4, 256, 64, 256], P('grp', None, 'tile'), may hold values from -6 to 6
- adj_rhs: float32 [8, 4, 256, 64, 256], P('grp', None, 'tile'), may hold values from -6 to 6
- src_cell: int32 [8, 4], P('grp'), may hold values from 0 to 4194303
- group_count: int32 [8], P('grp'), may hold values from 1 to 4, as said below
- region_label: int32 [256, 64, 256], P('tile'), may hold values from 0 to 7
- cut_flag: int32 [256, 64, 256], P('tile'), may hold values 0 or 1
- region_sigma: float32 [8], replicated, may hold values from 0.3 to 3
Outputs:
- gradient: float32 [256, 64, 256], P('tile', 'grp')
Inputs may be any that keep to these rules, and one draw needn't show every extreme that they name: `group_count`: some group has all 4 slots live in every draw; which one varies.
All inputs are finite; a program needn't handle non-finite values. No bound on the sum of `cut_flag` on one device may be relied on, other than what follows from the above.
Results may differ from a plain program's by a relative error of at most 0.00021.
Values sent between devices are 32-bit elements; how exact they have to be, the bound alone decides.
No kernel may reach another device: no remote copies, remote signals or barrier semaphores. Data moves between devices by JAX's collectives and lax.ppermute only.
A program may use at most 128 MiB of HBM per device.

v0:
```python
import jax
import jax.numpy as jnp
from jax import lax
from jax.sharding import PartitionSpec as P

ITERS = 2


MASS = 0.05
SOURCE_AMP = 64.0


def extended_2(cells, sides, width):
    for axis, dim in sides:
        count = lax.axis_size(axis)
        ends = count - 1
        head = lax.slice_in_dim(cells, 0, width, axis=dim)
        tail = lax.slice_in_dim(cells, cells.shape[dim] - width, cells.shape[dim], axis=dim)
        cells = jnp.concatenate(
            [
                lax.ppermute(tail, axis, [(i, (i + 1) % count) for i in range(ends)]),
                cells,
                lax.ppermute(head, axis, [((i + 1) % count, i) for i in range(ends)]),
            ],
            axis=dim,
        )
    return cells


def shifted_2(value, axis, by):
    peers = lax.axis_size(axis)
    pairs = [(i, i + by) for i in range(peers) if 0 <= i + by < peers]
    return lax.ppermute(value, axis, pairs)


def harmonic(left, right):
    return 2.0 * left * right / (left + right)


def region_conductivity(region_label, region_sigma):
    sigma = jnp.zeros(region_label.shape, jnp.float32)
    for region in range(region_sigma.shape[0]):
        sigma = sigma + jnp.where(region_label == region, region_sigma[region], 0.0)
    return sigma


def lateral_faces(sigma, factor):
    inner_y = harmonic(sigma[:, :-1], sigma[:, 1:]) * factor[:, :-1]
    inner_z = harmonic(sigma[:, :, :-1], sigma[:, :, 1:]) * factor[:, :, :-1]
    face_y = jnp.pad(inner_y, ((0, 0), (1, 1), (0, 0)))
    face_z = jnp.pad(inner_z, ((0, 0), (0, 0), (1, 1)))
    return (face_y, face_z)


def stencil(field, padded, face_x, face_y, face_z, massive):
    pad_y = jnp.pad(field, ((0, 0), (0, 0), (1, 1), (0, 0)))
    pad_z = jnp.pad(field, ((0, 0), (0, 0), (0, 0), (1, 1)))
    result = massive * field
    result = result + face_x[:-1] * (field - padded[:, :-2]) + face_x[1:] * (field - padded[:, 2:])
    result = (
        result
        + face_y[:, :-1] * (field - pad_y[:, :, :-2])
        + face_y[:, 1:] * (field - pad_y[:, :, 2:])
    )
    result = (
        result
        + face_z[:, :, :-1] * (field - pad_z[:, :, :, :-2])
        + face_z[:, :, 1:] * (field - pad_z[:, :, :, 2:])
    )
    return result


def correlate(forward, adjoint, fwd_next, adj_next, face_x, face_y, face_z, massive, live):
    zero_y = jnp.zeros_like(forward[:, :, :1])
    zero_z = jnp.zeros_like(forward[:, :, :, :1])
    diff_fx = fwd_next - forward
    diff_ax = adj_next - adjoint
    diff_fy = jnp.concatenate([forward[:, :, 1:], zero_y], 2) - forward
    diff_ay = jnp.concatenate([adjoint[:, :, 1:], zero_y], 2) - adjoint
    diff_fz = jnp.concatenate([forward[:, :, :, 1:], zero_z], 3) - forward
    diff_az = jnp.concatenate([adjoint[:, :, :, 1:], zero_z], 3) - adjoint
    corr = face_x[1:] * diff_fx * diff_ax + face_y[:, 1:] * diff_fy * diff_ay
    corr = corr + face_z[:, :, 1:] * diff_fz * diff_az + massive * forward * adjoint
    return jnp.sum(live[:, None, None, None] * corr, axis=0)


def dots(left, right):
    return jnp.sum(left * right, axis=(1, 2, 3))


def residual_sum(resid, precond):
    return lax.psum(dots(resid, precond), "tile")


def local(
    fwd_start, adj_start, adj_rhs, src_cell, group_count, region_label, cut_flag, region_sigma
):
    slots = fwd_start.shape[1]
    planes, rows_y, rows_z = region_label.shape
    sigma = region_conductivity(region_label, region_sigma)
    factor = 1.0 - 0.5 * cut_flag.astype(jnp.float32)
    extended = extended_2(jnp.stack([sigma, factor]), (("tile", 1),), 1)
    face_x = harmonic(extended[0, :-1], extended[0, 1:]) * extended[1, :-1]
    face_y, face_z = lateral_faces(sigma, factor)
    massive = MASS * sigma
    diag = (
        massive
        + face_x[:-1]
        + face_x[1:]
        + face_y[:, :-1]
        + face_y[:, 1:]
        + face_z[:, :, :-1]
        + face_z[:, :, 1:]
    )

    def apply(field):
        padded = extended_2(field, (("tile", 1),), 1)
        return stencil(field, padded, face_x, face_y, face_z, massive)

    offset = lax.axis_index("tile") * (planes * rows_y * rows_z)
    cells = lax.iota(jnp.int32, planes * rows_y * rows_z) + offset
    source = SOURCE_AMP * (cells[None, :] == src_cell[0][:, None]).astype(jnp.float32)
    rhs = jnp.concatenate([source.reshape(slots, planes, rows_y, rows_z), adj_rhs[0]], 0)
    iterate = jnp.concatenate([fwd_start[0], adj_start[0]], 0)
    resid = rhs - apply(iterate)
    precond = resid / diag
    direction = precond
    rz_now = residual_sum(resid, precond)
    for step in range(ITERS):
        image = apply(direction)
        curve = lax.psum(dots(direction, image), "tile")
        alpha = (rz_now / curve)[:, None, None, None]
        iterate = iterate + alpha * direction
        resid = resid - alpha * image
        if step + 1 < ITERS:
            precond = resid / diag
            rz_next = residual_sum(resid, precond)
            direction = precond + (rz_next / rz_now)[:, None, None, None] * direction
            rz_now = rz_next
    following = shifted_2(iterate[:, 0], "tile", -1)
    shifted = jnp.concatenate([iterate[:, 1:], following[:, None]], 1)
    live = (lax.iota(jnp.int32, slots) < group_count[0]).astype(jnp.float32)
    term = correlate(
        iterate[:slots],
        iterate[slots:],
        shifted[:slots],
        shifted[slots:],
        face_x,
        face_y,
        face_z,
        massive,
        live,
    )
    summed = lax.psum(term, "grp")
    block = rows_y // lax.axis_size("grp")
    summed = lax.dynamic_slice_in_dim(summed, lax.axis_index("grp") * block, block, 1)
    return -summed / slots


def solution(mesh):
    in_specs = (
        P("grp", None, "tile", None, None),
        P("grp", None, "tile", None, None),
        P("grp", None, "tile", None, None),
        P("grp", None),
        P("grp"),
        P("tile", None, None),
        P("tile", None, None),
        P(),
    )
    out_specs = P("tile", "grp", None)
    return jax.shard_map(local, mesh=mesh, in_specs=in_specs, out_specs=out_specs, check_vma=False)
```

profile of v0, /device:TPU:1, one launch (start us, length us, event | category | flops | bytes accessed | tf_op | source)
XLA Modules:
  0.0 449.3 jit_solution(13885268476233769980)
XLA Ops:
  6.5 1.6 fusion.79
  8.2 1.1 multiply_subtract_fusion.1
  9.3 7.2 %broadcast_multiply_fusion = (f32[8,64,256]{2,1,0:T(8,128)}, f32[8,64,256]{2,1,0:T(8,128)S(1)}) fusion(f32[]{:T(128)} %bitcast.8, s32[8,64,256]{2,1,0:T(8,128)} %param.13, f32[]{:T(128)} %bitcast.7, f32[]{:T(128)} %bitcast.6, f32[]{:T(128)} %bitcast.5, f32[]{:T(128)} %bitcast.4, f32[]{:T(128)} %bitcast.3, f32[]{:T(128)} %bitcast.2, f32[]{:T(128)} %bitcast.1), kind=kLoop, calls=%fused_computation.123 | loop fusion | flops 3145728 | bytes 1572896 | tf_op jit(solution)/shard_map/mul | solution.py:105
  16.6 4.7 %collective-permute-start = (f32[2,1,64,256]{3,2,1,0:T(8,128)S(1)}, f32[2,1,64,256]{3,2,1,0:T(8,128)}, u32[]{:S(2)}, u32[]{:S(2)}) collective-permute-start(f32[2,1,64,256]{3,2,1,0:T(8,128)S(1)} %get-tuple-element.25), channel_id=1, source_target_pairs={{0,1},{1,2},{2,3},{3,4},{4,5},{5,6},{6,7},{7,8},{8,9},{9,10},{10,1... | collective-permute-start | bytes 393224 | tf_op jit(solution)/shard_map/ppermute | solution.py:21
  21.2 1.3 collective-permute-start.1
  22.6 0.0 copy-start.11
  22.6 1.1 fusion.69
  23.7 4.8 %collective-permute-start.2 = (f32[8,1,64,256]{3,2,1,0:T(8,128)}, f32[8,1,64,256]{3,2,1,0:T(8,128)}, u32[]{:S(2)}, u32[]{:S(2)}) collective-permute-start(f32[8,1,64,256]{3,2,1,0:T(8,128)} %get-tuple-element.22), channel_id=1, source_target_pairs={{0,1},{1,2},{2,3},{3,4},{4,5},{5,6},{6,7},{7,8},{8,9},{9,10},{10,1... | collective-permute-start | bytes 1572872 | tf_op jit(solution)/shard_map/ppermute | solution.py:21
  28.4 1.3 collective-permute-start.3
  29.7 1.1 slice_multiply_fusion
  30.8 0.9 slice_multiply_fusion.1
  31.8 1.7 compare_select_fusion
  33.4 0.4 copy-done.3
  33.8 2.4 pad_maximum_fusion
  36.2 1.1 maximum_maximum_fusion
  37.3 0.0 collective-permute-done.1
  37.3 0.1 fusion.67
  37.5 2.0 fusion.78
  39.4 0.0 collective-permute-done.2
  39.4 3.1 collective-permute-done.3
  42.5 17.9 %broadcast_divide_fusion = (f32[8,8,64,256]{3,2,1,0:T(8,128)}, f32[8,8,64,256]{3,2,1,0:T(8,128)}) fusion(f32[8,64,256]{2,1,0:T(8,128)S(1)} %get-tuple-element.27, f32[8,8,64,256]{3,2,1,0:T(8,128)} %pad_maximum_fusion, f32[8,64,256]{2,1,0:T(8,128)} %get-tuple-element.32, f32[8,64,256]{2,1,0:T(8,128)} %get-tuple-element.31, ...), kind=kLoop, calls=%fused_computation.100 | loop fusion | flops 27262976 | bytes 26214400 | tf_op jit(solution)/shard_map/div | solution.py:126
  60.4 1.3 fusion.77
  61.7 2.6 collective-permute-start.4
  64.3 1.3 collective-permute-start.5
  65.6 6.6 %collective-permute-done.4 = f32[8,1,64,256]{3,2,1,0:T(8,128)} collective-permute-done((f32[8,1,64,256]{3,2,1,0:T(8,128)S(1)}, f32[8,1,64,256]{3,2,1,0:T(8,128)}, u32[]{:S(2)}, u32[]{:S(2)}) %collective-permute-start.4) | collective-permute-done | bytes 524320 | tf_op jit(solution)/shard_map/ppermute | solution.py:21
  72.3 6.3 %collective-permute-done.5 = f32[8,1,64,256]{3,2,1,0:T(8,128)} collective-permute-done((f32[8,1,64,256]{3,2,1,0:T(8,128)S(1)}, f32[8,1,64,256]{3,2,1,0:T(8,128)}, u32[]{:S(2)}, u32[]{:S(2)}) %collective-permute-start.5) | collective-permute-done | bytes 524320 | tf_op jit(solution)/shard_map/ppermute | solution.py:23
  78.5 17.8 %multiply_reduce_fusion.1 = (f32[8]{0:T(128)S(1)}, f32[8]{0:T(128)S(1)}, f32[8,8,64,256]{3,2,1,0:T(8,128)}) fusion(f32[8,8,64,256]{3,2,1,0:T(8,128)} %get-tuple-element.11, f32[8,64,256]{2,1,0:T(8,128)S(1)} %get-tuple-element.27, f32[8,8,64,256]{3,2,1,0:T(8,128)} %get-tuple-element.10, f32[8,64,256]{2,1,0:T(8,128)} %get-tuple-element.32, ...), kind=kLoop, calls=%fused_computation.87 | loop fusion | flops 27262960 | bytes 17825856 | tf_op jit(solution)/shard_map/reduce_sum | solution.py:88
  96.3 60.9 %all-reduce.12 = (f32[8]{0:T(128)S(1)}, f32[8]{0:T(128)S(1)}) all-reduce(f32[8]{0:T(128)S(1)} %get-tuple-element.6, f32[8]{0:T(128)S(1)} %get-tuple-element.5), channel_id=1, replica_groups=mesh['grp'=8,'tile'=32] {'tile'}, use_global_device_ids=true, to_apply=%region_1.2 | all-reduce | flops 16 | bytes 128 | tf_op jit(solution)/shard_map/psum | solution.py:92
  157.2 4.4 multiply_reduce_fusion
  161.6 55.7 %psum.37 = f32[8]{0:T(128)S(1)} all-reduce(f32[8]{0:T(128)S(1)} %multiply_reduce_fusion), channel_id=1, replica_groups=mesh['grp'=8,'tile'=32] {'tile'}, use_global_device_ids=true, to_apply=%region_5.6 | all-reduce | flops 8 | bytes 64 | tf_op jit(solution)/shard_map/psum | solution.py:92
  217.3 4.7 %multiply_add_fusion.1 = f32[8,8,64,256]{3,2,1,0:T(8,128)S(1)} fusion(f32[8]{0:T(128)S(1)} %div.45, f32[8,64,256]{2,1,0:T(8,128)S(1)} %get-tuple-element.27, f32[8,8,64,256]{3,2,1,0:T(8,128)} %get-tuple-element.11, f32[8,8,64,256]{3,2,1,0:T(8,128)} %get-tuple-element.9, f32[8]{0:T(128)S(1)} %div.43), kind=kLoop, calls=%fused_computation.84 | loop fusion | flops 6291456 | bytes 13107264 | tf_op jit(solution)/shard_map/add | solution.py:138
  222.1 0.1 fusion.76
  222.2 4.2 collective-permute-start.6
  226.4 1.5 collective-permute-start.7
  228.5 3.2 collective-permute-done.6
  231.7 5.0 %collective-permute-done.7 = f32[8,1,64,256]{3,2,1,0:T(8,128)} collective-permute-done((f32[8,1,64,256]{3,2,1,0:T(8,128)S(1)}, f32[8,1,64,256]{3,2,1,0:T(8,128)}, u32[]{:S(2)}, u32[]{:S(2)}) %collective-permute-start.7) | collective-permute-done | bytes 524320 | tf_op jit(solution)/shard_map/ppermute | solution.py:23
  236.7 6.7 %fusion.56 = f32[8]{0:T(128)S(1)} fusion(f32[8,8,64,256]{3,2,1,0:T(8,128)S(1)} %multiply_add_fusion.1, f32[8,1,64,256]{3,2,1,0:T(8,128)} %collective-permute-done.7, f32[8,1,64,256]{3,2,1,0:T(8,128)} %collective-permute-done.6, f32[8,64,256]{2,1,0:T(8,128)} %get-tuple-element.32, f32[8,64,256]{2,1,0:T(8,128)} %get-tuple-element.31, ...), kind=kLoop, calls=%fused_computation.89 | loop fusion | flops 24117240 | bytes 8912928 | tf_op jit(solution)/shard_map/reduce_sum | solution.py:88
  243.4 55.7 %psum.38 = f32[8]{0:T(128)S(1)} all-reduce(f32[8]{0:T(128)S(1)} %fusion.56), channel_id=1, replica_groups=mesh['grp'=8,'tile'=32] {'tile'}, use_global_device_ids=true, to_apply=%region_7.8 | all-reduce | flops 8 | bytes 64 | tf_op jit(solution)/shard_map/psum | solution.py:131
  299.1 5.5 %multiply_add_fusion = f32[8,8,64,256]{3,2,1,0:T(8,128)S(1)} fusion(f32[8,8,64,256]{3,2,1,0:T(8,128)} %copy-done, f32[8]{0:T(128)S(1)} %div.46, f32[8]{0:T(128)S(1)} %div.43, f32[4,8,64,256]{3,2,1,0:T(8,128)S(1)} %bitcast.40, f32[4,8,64,256]{3,2,1,0:T(8,128)} %bitcast.42, f32[8,8,64,256]{3,2,1,0:T(8,128)} %get-tuple-element.11, ...), kind=kLoop, calls=%fused_computation.83 | loop fusion | flops 6291456 | bytes 17301568 | tf_op jit(solution)/shard_map/add | solution.py:133
  304.7 1.3 collective-permute-start.8
  306.0 0.6 fusion.74
  306.7 0.4 slice.288
  307.1 1.1 fusion.75
  308.3 6.6 %collective-permute-done.8 = f32[8,64,256]{2,1,0:T(8,128)S(1)} collective-permute-done((f32[8,64,256]{2,1,0:T(8,128)S(1)}, f32[8,64,256]{2,1,0:T(8,128)S(1)}, u32[]{:S(2)}, u32[]{:S(2)}) %collective-permute-start.8) | collective-permute-done | bytes 524320 | tf_op jit(solution)/shard_map/ppermute | solution.py:33
  314.9 3.3 fusion.66
  318.1 0.0 all-reduce.15.cloned.1.call-update
  318.2 122.8 %all-reduce.15.cloned.1.call-done = f32[8,64,256]{2,1,0:T(8,128)} async-done(((f32[8,64,256]{2,1,0:T(8,128)}), f32[8,64,256]{2,1,0:T(8,128)}) %all-reduce.15.cloned.1.call-update) | async-done | bytes 524304 | tf_op jit(solution)/shard_map/psum | solution.py:154
  441.0 1.5 negate_multiply_fusion
  (31 shorter events, 0.2 us)
Async XLA Ops:
  6.5 16.0 %copy-start.1 = (f32[1,4,8,64,256]{4,3,2,1,0:T(8,128)S(1)}, f32[1,4,8,64,256]{4,3,2,1,0:T(8,128)}, u32[]{:S(2)}) copy-start(f32[1,4,8,64,256]{4,3,2,1,0:T(8,128)} %param.9) | copy-start | bytes 6291460
  6.5 434.4 %all-reduce.15.cloned.1.call-start = ((), (), s32[]{:S(2)}) async-start(), calls=%async_computation | async-start | bytes 1048576 | tf_op jit(solution)/shard_map/psum | solution.py:154
  6.5 16.0 %copy-start.2 = (f32[1,4,8,64,256]{4,3,2,1,0:T(8,128)S(1)}, f32[1,4,8,64,256]{4,3,2,1,0:T(8,128)}, u32[]{:S(2)}) copy-start(f32[1,4,8,64,256]{4,3,2,1,0:T(8,128)} %param.8) | copy-start | bytes 6291460
  16.6 19.6 %collective-permute-start = (f32[2,1,64,256]{3,2,1,0:T(8,128)S(1)}, f32[2,1,64,256]{3,2,1,0:T(8,128)}, u32[]{:S(2)}, u32[]{:S(2)}) collective-permute-start(f32[2,1,64,256]{3,2,1,0:T(8,128)S(1)} %get-tuple-element.25), channel_id=1, source_target_pairs={{0,1},{1,2},{2,3},{3,4},{4,5},{5,6},{6,7},{7,8},{8,9},{9,10},{10,1... | collective-permute-start | bytes 393224 | tf_op jit(solution)/shard_map/ppermute | solution.py:21
  21.2 16.1 %collective-permute-start.1 = (f32[2,1,64,256]{3,2,1,0:T(8,128)S(1)}, f32[2,1,64,256]{3,2,1,0:T(8,128)S(1)}, u32[]{:S(2)}, u32[]{:S(2)}) collective-permute-start(f32[2,1,64,256]{3,2,1,0:T(8,128)S(1)} %get-tuple-element.24), channel_id=1, source_target_pairs={{1,0},{2,1},{3,2},{4,3},{5,4},{6,5},{7,6},{8,7},{9,8},{10,9},{11,1... | collective-permute-start | bytes 393224 | tf_op jit(solution)/shard_map/ppermute | solution.py:23
  22.6 9.2 %copy-start.11 = (s32[1,4]{1,0:T(1,128)S(1)}, s32[1,4]{1,0:T(1,128)}, u32[]{:S(2)}) copy-start(s32[1,4]{1,0:T(1,128)} %param.11) | copy-start | bytes 52
  23.7 15.8 %collective-permute-start.2 = (f32[8,1,64,256]{3,2,1,0:T(8,128)}, f32[8,1,64,256]{3,2,1,0:T(8,128)}, u32[]{:S(2)}, u32[]{:S(2)}) collective-permute-start(f32[8,1,64,256]{3,2,1,0:T(8,128)} %get-tuple-element.22), channel_id=1, source_target_pairs={{0,1},{1,2},{2,3},{3,4},{4,5},{5,6},{6,7},{7,8},{8,9},{9,10},{10,1... | collective-permute-start | bytes 1572872 | tf_op jit(solution)/shard_map/ppermute | solution.py:21
  28.4 14.1 %collective-permute-start.3 = (f32[8,1,64,256]{3,2,1,0:T(8,128)}, f32[8,1,64,256]{3,2,1,0:T(8,128)}, u32[]{:S(2)}, u32[]{:S(2)}) collective-permute-start(f32[8,1,64,256]{3,2,1,0:T(8,128)} %get-tuple-element.23), channel_id=1, source_target_pairs={{1,0},{2,1},{3,2},{4,3},{5,4},{6,5},{7,6},{8,7},{9,8},{10,9},{11,1... | collective-permute-start | bytes 1572872 | tf_op jit(solution)/shard_map/ppermute | solution.py:23
  31.7 2.1 copy-start.3
  36.2 1.3 copy-start.9
  36.2 1.3 copy-start.10
  42.5 36.0 %copy-start.4 = (f32[8,64,256]{2,1,0:T(8,128)S(1)}, f32[8,64,256]{2,1,0:T(8,128)}, u32[]{:S(2)}) copy-start(f32[8,64,256]{2,1,0:T(8,128)} %get-tuple-element.12) | copy-start | bytes 1572868
  61.7 10.6 %collective-permute-start.4 = (f32[8,1,64,256]{3,2,1,0:T(8,128)S(1)}, f32[8,1,64,256]{3,2,1,0:T(8,128)}, u32[]{:S(2)}, u32[]{:S(2)}) collective-permute-start(f32[8,1,64,256]{3,2,1,0:T(8,128)S(1)} %get-tuple-element.20), channel_id=1, source_target_pairs={{0,1},{1,2},{2,3},{3,4},{4,5},{5,6},{6,7},{7,8},{8,9},{9,10},{10,1... | collective-permute-start | bytes 1572872 | tf_op jit(solution)/shard_map/ppermute | solution.py:21
  64.3 14.2 %collective-permute-start.5 = (f32[8,1,64,256]{3,2,1,0:T(8,128)S(1)}, f32[8,1,64,256]{3,2,1,0:T(8,128)}, u32[]{:S(2)}, u32[]{:S(2)}) collective-permute-start(f32[8,1,64,256]{3,2,1,0:T(8,128)S(1)} %get-tuple-element.21), channel_id=1, source_target_pairs={{1,0},{2,1},{3,2},{4,3},{5,4},{6,5},{7,6},{8,7},{9,8},{10,9},{11,1... | collective-permute-start | bytes 1572872 | tf_op jit(solution)/shard_map/ppermute | solution.py:23
  217.3 19.4 %copy-start.5 = (f32[8,64,256]{2,1,0:T(8,128)S(1)}, f32[8,64,256]{2,1,0:T(8,128)}, u32[]{:S(2)}) copy-start(f32[8,64,256]{2,1,0:T(8,128)} %get-tuple-element.28) | copy-start | bytes 1572868
  222.1 21.3 %copy-start = (f32[8,8,64,256]{3,2,1,0:T(8,128)}, f32[8,8,64,256]{3,2,1,0:T(8,128)S(1)}, u32[]{:S(2)}) copy-start(f32[8,8,64,256]{3,2,1,0:T(8,128)S(1)} %multiply_add_fusion.1) | copy-start | bytes 12582916
  222.2 9.5 %collective-permute-start.6 = (f32[8,1,64,256]{3,2,1,0:T(8,128)S(1)}, f32[8,1,64,256]{3,2,1,0:T(8,128)}, u32[]{:S(2)}, u32[]{:S(2)}) collective-permute-start(f32[8,1,64,256]{3,2,1,0:T(8,128)S(1)} %get-tuple-element.18), channel_id=1, source_target_pairs={{0,1},{1,2},{2,3},{3,4},{4,5},{5,6},{6,7},{7,8},{8,9},{9,10},{10,1... | collective-permute-start | bytes 1572872 | tf_op jit(solution)/shard_map/ppermute | solution.py:21
  226.4 10.3 %collective-permute-start.7 = (f32[8,1,64,256]{3,2,1,0:T(8,128)S(1)}, f32[8,1,64,256]{3,2,1,0:T(8,128)}, u32[]{:S(2)}, u32[]{:S(2)}) collective-permute-start(f32[8,1,64,256]{3,2,1,0:T(8,128)S(1)} %get-tuple-element.19), channel_id=1, source_target_pairs={{1,0},{2,1},{3,2},{4,3},{5,4},{6,5},{7,6},{8,7},{9,8},{10,9},{11,1... | collective-permute-start | bytes 1572872 | tf_op jit(solution)/shard_map/ppermute | solution.py:23
  304.7 10.2 %collective-permute-start.8 = (f32[8,64,256]{2,1,0:T(8,128)S(1)}, f32[8,64,256]{2,1,0:T(8,128)S(1)}, u32[]{:S(2)}, u32[]{:S(2)}) collective-permute-start(f32[8,64,256]{2,1,0:T(8,128)S(1)} %slice_bitcast_fusion.2), channel_id=1, source_target_pairs={{1,0},{2,1},{3,2},{4,3},{5,4},{6,5},{7,6},{8,7},{9,8},{10,9},{11,1... | collective-permute-start | bytes 1572872 | tf_op jit(solution)/shard_map/ppermute | solution.py:33
  307.1 7.8 %copy-start.6 = (f32[8,64,256]{2,1,0:T(8,128)S(1)}, f32[8,64,256]{2,1,0:T(8,128)}, u32[]{:S(2)}) copy-start(f32[8,64,256]{2,1,0:T(8,128)} %get-tuple-element.28) | copy-start | bytes 1572868
  307.1 7.8 %copy-start.7 = (f32[8,64,256]{2,1,0:T(8,128)S(1)}, f32[8,64,256]{2,1,0:T(8,128)}, u32[]{:S(2)}) copy-start(f32[8,64,256]{2,1,0:T(8,128)} %get-tuple-element.30) | copy-start | bytes 1572868
  307.1 7.8 %copy-start.8 = (f32[8,64,256]{2,1,0:T(8,128)S(1)}, f32[8,64,256]{2,1,0:T(8,128)}, u32[]{:S(2)}) copy-start(f32[8,64,256]{2,1,0:T(8,128)} %get-tuple-element.32) | copy-start | bytes 1572868
Sparse Core Ops, SparseCore 0:
  318.3 122.6 all-reduce.14
where the time goes:
time: 451 us; the launch traced here: 449 us
  blocking collectives  172 us (38%)
  waiting for transfers between devices  154 us (34%)
  other arithmetic  80.5 us (18%)
  starting transfers between devices  22.9 us (5%)
  between operations  14.3 us (3%)
  local copies, waits for them, and re-layouts  5.67 us (1%)
    psum x1, waiting for transfers between devices, local(): summed = lax.psum(term, 'grp')  123 us
    psum x2, blocking collectives, residual_sum(): return lax.psum(dots(resid, precond), 'tile')  117 us
    psum x1, blocking collectives, local(): curve = lax.psum(dots(direction, image), 'tile')  55.7 us
    reduce_sum x3, other arithmetic, dots(): return jnp.sum(left * right, axis=(1, 2, 3))  28.9 us
    div x1, other arithmetic, local(): precond = resid / diag  17.9 us
    ppermute x4, starting transfers between devices, extended_2(): lax.ppermute(tail, axis, [(i, (i + 1) % count) for i in range(ends)])  16.3 us
    ppermute x4, waiting for transfers between devices, extended_2(): lax.ppermute(head, axis, [((i + 1) % count, i) for i in range(ends)])  14.4 us
    ppermute x4, waiting for transfers between devices, extended_2(): lax.ppermute(tail, axis, [(i, (i + 1) % count) for i in range(ends)])  9.83 us
  transfers between devices with their start and end apart: 10, of which 7 were waited for; matrix products, arithmetic and copies ran while one was open for 3% of the time, Pallas kernels for 0%

commit v1 on v0

v1 whole, which is shorter than its diff:
```python
import functools
import jax
import jax.numpy as jnp
from jax import lax
from jax.experimental import pallas as pl
from jax.experimental.pallas import tpu as pltpu
from jax.sharding import PartitionSpec as P

MASS = 0.05
SOURCE_AMP = 64.0
F32 = jnp.float32
VMEM = pltpu.VMEM
IN_SMEM = pl.BlockSpec(memory_space=pltpu.SMEM)
IN_VMEM = pl.BlockSpec(memory_space=pltpu.VMEM)
IN_HBM = pl.BlockSpec(memory_space=pltpu.HBM)
LIMIT = 24 * 1024 * 1024


def next_y(v):
    return pltpu.roll(v, v.shape[0] - 1, 0)


def prev_y(v):
    return pltpu.roll(v, 1, 0)


def next_z(v):
    return pltpu.roll(v, v.shape[1] - 1, 1)


def prev_z(v):
    return pltpu.roll(v, 1, 1)


def harmonic(left, right):
    return 2.0 * left * right / (left + right)


def harmonic_or_zero(left, right):
    return 2.0 * left * right / jnp.maximum(left + right, 1e-30)


def lateral_faces(sigma, factor, mean):
    rows = lax.broadcasted_iota(jnp.int32, sigma.shape, 0)
    lanes = lax.broadcasted_iota(jnp.int32, sigma.shape, 1)
    face_y = jnp.where(rows < sigma.shape[0] - 1, factor * mean(sigma, next_y(sigma)), 0.0)
    face_z = jnp.where(lanes < sigma.shape[1] - 1, factor * mean(sigma, next_z(sigma)), 0.0)
    return face_y, face_z


def lateral(v, face_y, face_z):
    return face_y * next_y(v) + prev_y(face_y * v) + face_z * next_z(v) + prev_z(face_z * v)


def upper_lateral(v, face_y, face_z):
    return face_y * next_y(v) + face_z * next_z(v)


def folded(v):
    rows, lanes = v.shape
    v = v.reshape(rows // 8, 8, lanes).sum(0)
    total = v[:, :128]
    for at in range(128, lanes, 128):
        total = total + v[:, at : at + 128]
    return total


def plane_source(src, slot, plane, shape):
    rows, lanes = shape
    planes = 8
    cell = src[0, slot] - (lax.axis_index("tile") * planes + plane) * (rows * lanes)
    at = lax.broadcasted_iota(jnp.int32, shape, 0) * lanes + lax.broadcasted_iota(jnp.int32, shape, 1)
    return jnp.where(at == cell, SOURCE_AMP, 0.0).astype(F32)


def edges_kernel(
    table_in, src_in, count, fwd, adj, rhs, label, cut,
    up, down, kxf, ky, kz, dd, inv, mass, weight,
    table, src, lab, flag, sig, fac, xs, rs, sems,
):
    slots = fwd.shape[1]
    planes, rows, lanes = label.shape
    last = planes - 1
    copies = [
        pltpu.make_async_copy(label, lab, sems.at[0]),
        pltpu.make_async_copy(cut, flag, sems.at[1]),
        pltpu.make_async_copy(table_in, table, sems.at[12]),
        pltpu.make_async_copy(src_in, src, sems.at[13]),
        pltpu.make_async_copy(fwd.at[0, :, 0], down.at[pl.ds(0, slots)], sems.at[2]),
        pltpu.make_async_copy(adj.at[0, :, 0], down.at[pl.ds(slots, slots)], sems.at[3]),
        pltpu.make_async_copy(fwd.at[0, :, last], up.at[pl.ds(0, slots)], sems.at[4]),
        pltpu.make_async_copy(adj.at[0, :, last], up.at[pl.ds(slots, slots)], sems.at[5]),
        pltpu.make_async_copy(fwd.at[0, :, pl.ds(1, 2)], xs.at[pl.ds(0, slots), pl.ds(0, 2)], sems.at[6]),
        pltpu.make_async_copy(adj.at[0, :, pl.ds(1, 2)], xs.at[pl.ds(slots, slots), pl.ds(0, 2)], sems.at[7]),
        pltpu.make_async_copy(fwd.at[0, :, last - 1], xs.at[pl.ds(0, slots), 2], sems.at[8]),
        pltpu.make_async_copy(adj.at[0, :, last - 1], xs.at[pl.ds(slots, slots), 2], sems.at[9]),
        pltpu.make_async_copy(rhs.at[0, :, pl.ds(0, 2)], rs.at[:, pl.ds(0, 2)], sems.at[10]),
        pltpu.make_async_copy(rhs.at[0, :, last], rs.at[:, 2], sems.at[11]),
    ]
    for copy in copies:
        copy.start()
    for copy in copies[:4]:
        copy.wait()
    slot = lax.broadcasted_iota(jnp.int32, weight.shape, 0)
    weight[...] = jnp.where(slot < count[0], -1.0 / slots, 0.0).astype(F32)

    @pl.loop(0, planes)
    def _(p):
        names = lab[p]
        value = jnp.full((rows, lanes), table[0], F32)
        for region in range(1, table.shape[0]):
            value = jnp.where(names == region, table[region], value)
        factor = 1.0 - 0.5 * flag[p].astype(F32)
        sig[p] = value
        fac[p] = factor
        mass[p] = MASS * value
        face_y, face_z = lateral_faces(value, factor, harmonic)
        ky[p] = face_y
        kz[p] = face_z

    kxf[0] = jnp.zeros((rows, lanes), F32)
    kxf[planes] = jnp.zeros((rows, lanes), F32)

    @pl.loop(1, planes)
    def _(p):
        kxf[p] = harmonic(sig[p - 1], sig[p]) * fac[p - 1]

    @pl.loop(0, planes)
    def _(p):
        face_y, face_z = ky[p], kz[p]
        diag = mass[p] + kxf[p] + kxf[p + 1] + face_y + prev_y(face_y) + face_z + prev_z(face_z)
        dd[p] = diag
        inv[p] = 1.0 / diag

    for copy in copies[4:]:
        copy.wait()
    up[2 * 2 * slots] = sig[last]
    up[2 * 2 * slots + 1] = fac[last]
    up[2 * 2 * slots + 2] = dd[last]
    down[2 * 2 * slots] = sig[0]
    down[2 * 2 * slots + 1] = fac[0]
    down[2 * 2 * slots + 2] = dd[0]
    systems = 2 * slots
    base = 2 * systems + 3

    def one(s, right):
        x0, x1, x2, x6, x7 = down[s], xs[s, 0], xs[s, 1], xs[s, 2], up[s]
        down[systems + s] = right[0] + lateral(x0, ky[0], kz[0]) + kxf[1] * x1
        up[systems + s] = right[2] + lateral(x7, ky[last], kz[last]) + kxf[last] * x6
        z1 = inv[1] * (right[1] + lateral(x1, ky[1], kz[1]) + kxf[1] * x0 + kxf[2] * x2) - x1
        down[base + s] = kxf[1] * z1

    @pl.loop(0, slots)
    def _(s):
        one(s, [plane_source(src, s, p, (rows, lanes)) for p in (0, 1, last)])

    @pl.loop(0, slots)
    def _(s):
        one(slots + s, [rs[s, 0], rs[s, 1], rs[s, 2]])


def interior_kernel(src_in, fwd, adj, rhs, kxf, ky, kz, dd, inv, x, z, n, moments, src, rs, sems):
    slots = fwd.shape[1]
    planes, rows, lanes = x.shape[1:]
    last = planes - 1
    copies = [
        pltpu.make_async_copy(fwd.at[0], x.at[pl.ds(0, slots)], sems.at[0]),
        pltpu.make_async_copy(adj.at[0], x.at[pl.ds(slots, slots)], sems.at[1]),
        pltpu.make_async_copy(rhs.at[0], rs, sems.at[2]),
        pltpu.make_async_copy(src_in, src, sems.at[3]),
    ]
    for copy in copies:
        copy.start()
    for copy in copies:
        copy.wait()

    def one(s, right):
        for p in range(1, last):
            total = right(p) + lateral(x[s, p], ky[p], kz[p])
            total = total + kxf[p] * x[s, p - 1] + kxf[p + 1] * x[s, p + 1]
            z[s, p] = inv[p] * total - x[s, p]
        c0 = jnp.zeros((8, 128), F32)
        c1, c2, c3 = c0, c0, c0
        for p in range(1, last):
            v = z[s, p]
            c0 = c0 + folded(dd[p] * v * v)
            w = lateral(v, ky[p], kz[p])
            if p > 1:
                w = w + kxf[p] * z[s, p - 1]
            if p < last - 1:
                w = w + kxf[p + 1] * z[s, p + 1]
            if p == 1 or p == last - 1:
                n[s, p] = w
                continue
            m = inv[p] * w
            n[s, p] = m
            c1 = c1 + folded(v * w)
            c2 = c2 + folded(m * w)
            near = upper_lateral(m, ky[p], kz[p])
            if p > 2:
                near = near + kxf[p] * n[s, p - 1]
            c3 = c3 + folded(m * near)
        for at, c in enumerate((c0, c1, c2, c3)):
            moments[s, at] = c

    @pl.loop(0, slots)
    def _(s):
        one(s, lambda p: plane_source(src, s, p, (rows, lanes)))

    @pl.loop(0, slots)
    def _(s):
        one(slots + s, lambda p: rs[s, p])


def boundary_kernel(
    below, above, up, down, kxf, ky, kz, dd, inv, z_in, n_in, moments,
    z, n, zx, nx, kch, out,
    coef, sums,
):
    systems, planes, rows, lanes = z.shape
    last = planes - 1
    base = 2 * systems + 3
    sig, fac, deg = 2 * systems, 2 * systems + 1, 2 * systems + 2
    low = harmonic(below[sig], down[sig]) * below[fac]
    high = harmonic(up[sig], above[sig]) * up[fac]
    kch[...] = high
    coef[0] = low
    d0 = dd[0] + low
    d7 = dd[last] + high
    dm = below[deg] + low
    d8 = above[deg] + high
    coef[1] = d0
    coef[2] = d7
    coef[3] = 1.0 / d0
    coef[4] = 1.0 / d7
    coef[5] = jnp.where(dm > 0.0, 1.0 / jnp.where(dm > 0.0, dm, 1.0), 0.0)
    coef[6] = jnp.where(d8 > 0.0, 1.0 / jnp.where(d8 > 0.0, d8, 1.0), 0.0)
    face_y, face_z = lateral_faces(above[sig], above[fac], harmonic_or_zero)
    coef[7] = face_y
    coef[8] = face_z

    @pl.loop(0, systems)
    def _(s):
        c0, c1, c2, c3 = [moments[s, at] for at in range(4)]
        kc, i0, i1 = coef[0], coef[3], inv[1]
        x0, xm = down[s], below[s]
        z0 = i0 * (down[systems + s] + kc * xm) - x0
        zm = coef[5] * (below[systems + s] + kc * x0) - xm
        z1 = z_in[s, 1]
        w0 = lateral(z0, ky[0], kz[0]) + kxf[1] * z1 + kc * zm
        w1 = n_in[s, 1] + kxf[1] * z0
        n0 = i0 * w0
        n1 = i1 * w1
        z[s, 0] = z0
        n[s, 0] = n0
        n[s, 1] = n1
        c0 = c0 + folded(coef[1] * z0 * z0)
        c1 = c1 + folded(z0 * w0 + z1 * w1)
        c2 = c2 + folded(n0 * w0 + n1 * w1)
        near0 = upper_lateral(n0, ky[0], kz[0]) + kxf[1] * n1
        near1 = upper_lateral(n1, ky[1], kz[1]) + kxf[2] * n_in[s, 2]
        c3 = c3 + folded(n0 * near0 + n1 * near1)
        kc, i7, i6 = kch[...], coef[4], inv[last - 1]
        x7, x8 = up[s], above[s]
        z7 = i7 * (up[systems + s] + kc * x8) - x7
        z8 = coef[6] * (above[systems + s] + kc * x7) - x8
        z6 = z_in[s, last - 1]
        w7 = lateral(z7, ky[last], kz[last]) + kxf[last] * z6 + kc * z8
        w6 = n_in[s, last - 1] + kxf[last] * z7
        w8 = lateral(z8, coef[7], coef[8]) + above[base + s] + kc * z7
        n7 = i7 * w7
        n6 = i6 * w6
        n8 = coef[6] * w8
        z[s, last] = z7
        n[s, last] = n7
        n[s, last - 1] = n6
        zx[s] = z8
        nx[s] = n8
        c0 = c0 + folded(coef[2] * z7 * z7)
        c1 = c1 + folded(z7 * w7 + z6 * w6)
        c2 = c2 + folded(n7 * w7 + n6 * w6)
        near7 = upper_lateral(n7, ky[last], kz[last]) + kc * n8
        near6 = upper_lateral(n6, ky[last - 1], kz[last - 1]) + kxf[last] * n7
        near6 = near6 + kxf[last - 1] * n_in[s, last - 2]
        c3 = c3 + folded(n7 * near7 + n6 * near6)
        for at, c in enumerate((c0, c1, c2, c3 + c3)):
            sums[at, pl.ds(s, 1)] = c.sum(0, keepdims=True)

    lanes_at = lax.broadcasted_iota(jnp.int32, (systems, 128), 1)
    packed = jnp.zeros((systems, 128), F32)
    for at in range(4):
        packed = packed + jnp.where(lanes_at == at, sums[at].sum(1, keepdims=True), 0.0)
    out[...] = jnp.broadcast_to(packed[None], out.shape)


def correlate_kernel(weight, parts, x, z, n, above, zx, nx, kxf, kch, ky, kz, mass, out, scale):
    systems, planes, rows, lanes = z.shape
    slots = systems // 2
    last = planes - 1
    total = parts[...].sum(0)
    lanes_at = lax.broadcasted_iota(jnp.int32, total.shape, 1)
    c0, c1, c2, c3 = [
        jnp.where(lanes_at == at, total, 0.0).sum(1, keepdims=True) for at in range(4)
    ]
    alpha = c0 / (c0 - c1)
    keep = 1.0 - alpha
    rz = keep * keep * c0 + 2.0 * alpha * keep * c1 + alpha * alpha * c2
    first = keep + rz / c0
    curve = first * first * (c0 - c1) + 2.0 * first * alpha * (c1 - c2) + alpha * alpha * (c2 - c3)
    step = rz / curve
    scale[0] = jnp.broadcast_to(alpha + step * first, (systems, lanes))
    scale[1] = jnp.broadcast_to(step * alpha, (systems, lanes))
    out[...] = jnp.zeros(out.shape, F32)

    @pl.loop(0, slots)
    def _(s):
        ends = (s, slots + s)
        share = weight[pl.ds(s, 1)]
        on_z = [scale[0, pl.ds(e, 1)] for e in ends]
        on_n = [scale[1, pl.ds(e, 1)] for e in ends]

        def field(p):
            if p < planes:
                return [x[e, p] + on_z[i] * z[e, p] + on_n[i] * n[e, p] for i, e in enumerate(ends)]
            return [above[e] + on_z[i] * zx[e] + on_n[i] * nx[e] for i, e in enumerate(ends)]

        u, v = field(0)
        for p in range(planes):
            u_up, v_up = field(p + 1)
            face_x = kxf[p + 1] if p < last else kch[...]
            corr = face_x * (u_up - u) * (v_up - v)
            corr = corr + ky[p] * (next_y(u) - u) * (next_y(v) - v)
            corr = corr + kz[p] * (next_z(u) - u) * (next_z(v) - v)
            corr = corr + mass[p] * u * v
            out[:, p] = out[:, p] + (share * corr).reshape(out.shape[0], -1, lanes)
            u, v = u_up, v_up


def local(
    fwd_start, adj_start, adj_rhs, src_cell, group_count, region_label, cut_flag, region_sigma
):
    slots = fwd_start.shape[1]
    systems = 2 * slots
    planes, rows, lanes = region_label.shape
    groups = lax.axis_size("grp")
    tiles = lax.axis_size("tile")
    cells = planes * rows * lanes

    def held(*shape):
        return VMEM(shape, F32)

    def in_hbm(*arrays):
        return [pltpu.with_memory_space_constraint(a, pltpu.HBM) for a in arrays]

    def pinned(*arrays):
        return [pltpu.with_memory_space_constraint(a, pltpu.VMEM) for a in arrays]

    def params(**more):
        return pltpu.CompilerParams(vmem_limit_bytes=LIMIT, **more)

    field = held(systems, planes, rows, lanes)
    plane_set = held(planes, rows, lanes)
    up, down, kxf, ky, kz, dd, inv, mass, weight = pl.pallas_call(
        edges_kernel,
        out_shape=[
            held(2 * systems + 3, rows, lanes),
            held(3 * systems + 3, rows, lanes),
            held(planes + 1, rows, lanes),
            plane_set, plane_set, plane_set, plane_set, plane_set,
            held(8, lanes),
        ],
        in_specs=[IN_HBM] * 2 + [IN_SMEM] + [IN_HBM] * 5,
        out_specs=[IN_VMEM] * 9,
        scratch_shapes=[
            pltpu.SMEM(region_sigma.shape, F32),
            pltpu.SMEM(src_cell.shape, jnp.int32),
            VMEM((planes, rows, lanes), jnp.int32),
            VMEM((planes, rows, lanes), jnp.int32),
            VMEM((planes, rows, lanes), F32),
            VMEM((planes, rows, lanes), F32),
            VMEM((systems, 3, rows, lanes), F32),
            VMEM((slots, 3, rows, lanes), F32),
            pltpu.SemaphoreType.DMA((14,)),
        ],
        compiler_params=params(),
        cost_estimate=pl.CostEstimate(flops=20 * cells, bytes_accessed=16 * cells, transcendentals=0),
        name="edges",
    )(
        *in_hbm(region_sigma, src_cell), group_count,
        *in_hbm(fwd_start, adj_start, adj_rhs, region_label, cut_flag),
    )

    below = lax.ppermute(up, "tile", [(i, i + 1) for i in range(tiles - 1)])
    above = lax.ppermute(down, "tile", [(i + 1, i) for i in range(tiles - 1)])

    x, z, n, moments = pl.pallas_call(
        interior_kernel,
        out_shape=[field, field, field, held(systems, 4, 8, 128)],
        in_specs=[IN_HBM] * 4 + [IN_VMEM] * 5,
        out_specs=[IN_VMEM] * 4,
        scratch_shapes=[
            pltpu.SMEM(src_cell.shape, jnp.int32),
            VMEM((slots, planes, rows, lanes), F32),
            pltpu.SemaphoreType.DMA((4,)),
        ],
        compiler_params=params(),
        cost_estimate=pl.CostEstimate(
            flops=60 * systems * cells, bytes_accessed=32 * systems * cells, transcendentals=0
        ),
        name="interior",
    )(*in_hbm(src_cell, fwd_start, adj_start, adj_rhs), *pinned(kxf, ky, kz, dd, inv))

    z, n, zx, nx, kch, moments = pl.pallas_call(
        boundary_kernel,
        out_shape=[
            field, field,
            held(systems, rows, lanes), held(systems, rows, lanes), held(rows, lanes),
            held(tiles, systems, 128),
        ],
        in_specs=[IN_VMEM] * 12,
        out_specs=[IN_VMEM] * 6,
        input_output_aliases={9: 0, 10: 1},
        scratch_shapes=[
            VMEM((9, rows, lanes), F32),
            VMEM((4, systems, 128), F32),
        ],
        compiler_params=params(),
        name="boundary",
    )(*pinned(below, above, up, down, kxf, ky, kz, dd, inv, z, n, moments))

    parts = lax.all_to_all(moments, "tile", 0, 0)

    term = pl.pallas_call(
        correlate_kernel,
        out_shape=held(groups, planes, rows // groups, lanes),
        in_specs=[IN_VMEM] * 13,
        out_specs=IN_VMEM,
        scratch_shapes=[VMEM((2, systems, lanes), F32)],
        compiler_params=params(),
        name="correlate",
    )(*pinned(weight, parts, x, z, n, above, zx, nx, kxf, kch, ky, kz, mass))

    blocks = lax.all_to_all(term, "grp", 0, 0)
    return jnp.sum(blocks, axis=0)


def solution(mesh):
    in_specs = (
        P("grp", None, "tile", None, None),
        P("grp", None, "tile", None, None),
        P("grp", None, "tile", None, None),
        P("grp", None),
        P("grp"),
        P("tile", None, None),
        P("tile", None, None),
        P(),
    )
    out_specs = P("tile", "grp", None)
    return jax.shard_map(local, mesh=mesh, in_specs=in_specs, out_specs=out_specs, check_vma=False)
```

time: 451 us -> 93.4 us (0.21)
  blocking collectives: 172 us -> 40.9 us
  waiting for transfers between devices: 154 us -> 23.6 us
  other arithmetic: 80.5 us -> 0.66 us
  Pallas kernels: 0 us -> 21.2 us
  starting transfers between devices: 22.9 us -> 6.03 us
  between operations: 14.3 us -> 0.7 us
  local copies, waits for them, and re-layouts: 5.67 us -> 0 us
    psum x3 -> x0, blocking collectives: 172 us -> none  [the longest x2 117 us: residual_sum(): return lax.psum(dots(resid, precond), 'tile')]
    psum x1 -> x0, waiting for transfers between devices: 123 us -> none  [local(): summed = lax.psum(term, 'grp')]
    all_to_all x0 -> x2, blocking collectives: none -> 40.9 us  [the longest x1 24.4 us: local(): parts = lax.all_to_all(moments, 'tile', 0, 0)]
    reduce_sum x4 -> x1, other arithmetic: 32.1 us -> 0.66 us  [local(): return jnp.sum(blocks, axis=0)]
    pallas_call x0 -> x4, Pallas kernels: none -> 21.2 us  [the longest x1 10.4 us: local(): pl.pallas_call(interior_kernel, out_shape=[field, field, field, held(syst...]
    div x5 -> x0, other arithmetic: 19.4 us -> none  [the longest x1 17.9 us: local(): precond = resid / diag]
    ppermute x9 -> x2, starting transfers between devices: 22.9 us -> 6.03 us  [the longest x1 4.74 us: local(): below = lax.ppermute(up, 'tile', [(i, i + 1) for i in range(tiles - 1)])]
    mul x5 -> x0, other arithmetic: 11 us -> none  [the longest x1 7.23 us: local(): massive = MASS * sigma]
  transfers between devices with their start and end apart: 10 -> 2, of which waited for: 7 -> 2; matrix products, arithmetic and copies ran while one was open for 3% -> 0% of each run, Pallas kernels for 0% -> 11%
where the time goes in v1:
time: 93.4 us; the launch traced here: 93.2 us
  blocking collectives  40.9 us (44%)
  waiting for transfers between devices  23.6 us (25%)
  Pallas kernels  21.2 us (23%)
  starting transfers between devices  6.03 us (6%)
    all_to_all x1, blocking collectives, local(): parts = lax.all_to_all(moments, 'tile', 0, 0)  24.4 us
    all_to_all x1, blocking collectives, local(): blocks = lax.all_to_all(term, 'grp', 0, 0)  16.6 us
    ppermute x1, waiting for transfers between devices, local(): below = lax.ppermute(up, 'tile', [(i, i + 1) for i in range(tiles - 1)])  13.3 us
    pallas_call x1, Pallas kernels, local(): pl.pallas_call(interior_kernel, out_shape=[field, field, field, held(syst...  10.4 us
    ppermute x1, waiting for transfers between devices, local(): above = lax.ppermute(down, 'tile', [(i + 1, i) for i in range(tiles - 1)])  10.3 us
    pallas_call x1, Pallas kernels, local(): pl.pallas_call(edges_kernel, out_shape=[held(2 * systems + 3, rows, lanes...  4.75 us
    ppermute x1, starting transfers between devices, local(): below = lax.ppermute(up, 'tile', [(i, i + 1) for i in range(tiles - 1)])  4.74 us
    pallas_call x1, Pallas kernels, local(): pl.pallas_call(boundary_kernel, out_shape=[field, field, held(systems, ro...  3.31 us
  transfers between devices with their start and end apart: 2, of which 2 were waited for; matrix products, arithmetic and copies ran while one was open for 0% of the time, Pallas kernels for 11%

profile of v1, /device:TPU:1, one launch (start us, length us, event | category | flops | bytes accessed | tf_op | source)
XLA Modules:
  0.0 93.2 jit_solution(6466521228369320944)
XLA Ops:
  0.7 4.8 %edges.1 = (f32[19,64,256]{2,1,0:T(8,128)S(1)}, f32[27,64,256]{2,1,0:T(8,128)S(1)}, f32[9,64,256]{2,1,0:T(8,128)S(1)}, f32[8,64,256]{2,1,0:T(8,128)S(1)}, f32[8,...) custom-call(f32[8]{0:T(128)} %table_in.1, ...), custom_call_target="tpu_custom_call" | custom-call | flops 2621440 | bytes 2097152 | tf_op jit(solution)/shard_map/edges/pallas_call | solution.py:363
  5.4 1.3 %collective-permute-start.1 = (f32[27,64,256]{2,1,0:T(8,128)S(1)}, f32[27,64,256]{2,1,0:T(8,128)S(1)}, u32[]{:S(2)}, u32[]{:S(2)}) collective-permute-start(f32[27,64,256]{2,1,0:T(8,128)S(1)} %get-tuple-element.26.down), channel_id=1, source_target_pairs={{1,0},{2,1},{3,2},{4,3},{5,4},{6,5},{7,6},{8,7},{9,8},{10,9},{11,1... | collective-permute-start | bytes 5308424 | tf_op jit(solution)/shard_map/ppermute | solution.py:394
  6.7 4.7 %collective-permute-start = (f32[19,64,256]{2,1,0:T(8,128)S(1)}, f32[19,64,256]{2,1,0:T(8,128)S(1)}, u32[]{:S(2)}, u32[]{:S(2)}) collective-permute-start(f32[19,64,256]{2,1,0:T(8,128)S(1)} %get-tuple-element.25.up), channel_id=1, source_target_pairs={{0,1},{1,2},{2,3},{3,4},{4,5},{5,6},{6,7},{7,8},{8,9},{9,10},{10,1... | collective-permute-start | bytes 3735560 | tf_op jit(solution)/shard_map/ppermute | solution.py:393
  11.5 10.4 %interior.1 = (f32[8,8,64,256]{3,2,1,0:T(8,128)S(1)}, f32[8,8,64,256]{3,2,1,0:T(8,128)S(1)}, f32[8,8,64,256]{3,2,1,0:T(8,128)S(1)}, f32[8,4,8,128]{3,2,1,0:T(8,128)S(1)}) custom-call(s32[1,4]{1,0:T(1,128)} %src_in.3, f32[1,4,8,64,256]{4,3,2,1,0:T(8,128)} %fwd.3, f32[1,4,8,64,256]{4,3,2,1,0:T(8,128)} %adj.3, f32[1,4,8,64,256]{4,3,2,1,0:T(8,128)} %rhs.3, ...), custom_call_target="tpu_custom_call" | custom-call | flops 62914560 | bytes 33554432 | tf_op jit(solution)/shard_map/interior/pallas_call | solution.py:396
  21.9 13.3 %collective-permute-done.below = f32[19,64,256]{2,1,0:T(8,128)S(1)} collective-permute-done((f32[19,64,256]{2,1,0:T(8,128)S(1)}, f32[19,64,256]{2,1,0:T(8,128)S(1)}, u32[]{:S(2)}, u32[]{:S(2)}) %collective-permute-start) | collective-permute-done | bytes 1245216 | tf_op jit(solution)/shard_map/ppermute | solution.py:393
  35.2 10.3 %collective-permute-done.1.above = f32[27,64,256]{2,1,0:T(8,128)S(1)} collective-permute-done((f32[27,64,256]{2,1,0:T(8,128)S(1)}, f32[27,64,256]{2,1,0:T(8,128)S(1)}, u32[]{:S(2)}, u32[]{:S(2)}) %collective-permute-start.1) | collective-permute-done | bytes 1769504 | tf_op jit(solution)/shard_map/ppermute | solution.py:394
  45.5 3.3 %boundary.1 = (f32[8,8,64,256]{3,2,1,0:T(8,128)S(1)}, f32[8,8,64,256]{3,2,1,0:T(8,128)S(1)}, f32[8,64,256]{2,1,0:T(8,128)S(1)}, f32[8,64,256]{2,1,0:T(8,128)S(1)...) custom-call(f32[19,64,256]{2,1,0:T(8,128)S(1)} %collective-permute-done.below, ...), custom_call_target="tpu_custom_call", output_to_operand_aliasing={{0}: (9, {}), {1}: (10, {})} | custom-call | tf_op jit(solution)/shard_map/boundary/pallas_call | solution.py:413
  48.8 24.4 %all_to_all.10.parts = f32[32,8,128]{2,1,0:T(8,128)S(1)} all-to-all(f32[32,8,128]{2,1,0:T(8,128)S(1)} %get-tuple-element.35), channel_id=1, replica_groups=mesh['grp'=8,'tile'=32] {'tile'}, dimensions={0} | all-to-all | bytes 262144 | tf_op jit(solution)/shard_map/all_to_all | solution.py:431
  73.2 2.8 %correlate.1 = f32[8,8,8,256]{3,2,1,0:T(8,128)S(1)} custom-call(f32[8,256]{1,0:T(8,128)S(1)} %get-tuple-element.24.weight, f32[32,8,128]{2,1,0:T(8,128)S(1)} %all_to_all.10.parts, f32[8,8,64,256]{3,2,1,0:T(8,128)S(1)} %get-tuple-element.36.x, f32[8,8,64,256]{3,2,1,0:T(8,128)S(1)} %get-tuple-element.37.z, f32[8,8,64,256]{3,2,1,0:T(8,128)S(1)} %get-tuple-element.38.n, ...), custom_call_target="tpu_custom_call" | custom-call | tf_op jit(solution)/shard_map/correlate/pallas_call | solution.py:433
  76.0 16.6 %all_to_all.11 = f32[8,8,8,256]{3,2,1,0:T(8,128)S(1)} all-to-all(f32[8,8,8,256]{3,2,1,0:T(8,128)S(1)} %correlate.1), channel_id=1, replica_groups=mesh['grp'=8,'tile'=32] {'grp'}, dimensions={0} | all-to-all | bytes 1048576 | tf_op jit(solution)/shard_map/all_to_all | solution.py:443
  92.5 0.7 reduce_sum.9
Async XLA Ops:
  5.4 40.1 %collective-permute-start.1 = (f32[27,64,256]{2,1,0:T(8,128)S(1)}, f32[27,64,256]{2,1,0:T(8,128)S(1)}, u32[]{:S(2)}, u32[]{:S(2)}) collective-permute-start(f32[27,64,256]{2,1,0:T(8,128)S(1)} %get-tuple-element.26.down), channel_id=1, source_target_pairs={{1,0},{2,1},{3,2},{4,3},{5,4},{6,5},{7,6},{8,7},{9,8},{10,9},{11,1... | collective-permute-start | bytes 5308424 | tf_op jit(solution)/shard_map/ppermute | solution.py:394
  6.7 28.5 %collective-permute-start = (f32[19,64,256]{2,1,0:T(8,128)S(1)}, f32[19,64,256]{2,1,0:T(8,128)S(1)}, u32[]{:S(2)}, u32[]{:S(2)}) collective-permute-start(f32[19,64,256]{2,1,0:T(8,128)S(1)} %get-tuple-element.25.up), channel_id=1, source_target_pairs={{0,1},{1,2},{2,3},{3,4},{4,5},{5,6},{6,7},{7,8},{8,9},{9,10},{10,1... | collective-permute-start | bytes 3735560 | tf_op jit(solution)/shard_map/ppermute | solution.py:393

commit v2 on v1

v2 whole, which is shorter than its diff:
```python
import functools
import jax
import jax.numpy as jnp
from jax import lax
from jax.experimental import pallas as pl
from jax.experimental.pallas import tpu as pltpu
from jax.sharding import PartitionSpec as P

MASS = 0.05
SOURCE_AMP = 64.0
F32 = jnp.float32
VMEM = pltpu.VMEM
IN_SMEM = pl.BlockSpec(memory_space=pltpu.SMEM)
IN_VMEM = pl.BlockSpec(memory_space=pltpu.VMEM)
IN_HBM = pl.BlockSpec(memory_space=pltpu.HBM)
LIMIT = 24 * 1024 * 1024


def next_y(v):
    return pltpu.roll(v, v.shape[0] - 1, 0)


def prev_y(v):
    return pltpu.roll(v, 1, 0)


def next_z(v):
    return pltpu.roll(v, v.shape[1] - 1, 1)


def prev_z(v):
    return pltpu.roll(v, 1, 1)


def harmonic(left, right):
    return 2.0 * left * right / (left + right)


def harmonic_or_zero(left, right):
    return 2.0 * left * right / jnp.maximum(left + right, 1e-30)


def lateral_faces(sigma, factor, mean):
    rows = lax.broadcasted_iota(jnp.int32, sigma.shape, 0)
    lanes = lax.broadcasted_iota(jnp.int32, sigma.shape, 1)
    face_y = jnp.where(rows < sigma.shape[0] - 1, factor * mean(sigma, next_y(sigma)), 0.0)
    face_z = jnp.where(lanes < sigma.shape[1] - 1, factor * mean(sigma, next_z(sigma)), 0.0)
    return face_y, face_z


def lateral(v, face_y, face_z):
    return face_y * next_y(v) + prev_y(face_y * v) + face_z * next_z(v) + prev_z(face_z * v)


def upper_lateral(v, face_y, face_z):
    return face_y * next_y(v) + face_z * next_z(v)


def folded(v):
    rows, lanes = v.shape
    v = v.reshape(rows // 8, 8, lanes).sum(0)
    total = v[:, :128]
    for at in range(128, lanes, 128):
        total = total + v[:, at : at + 128]
    return total


def plane_source(src, slot, plane, shape):
    rows, lanes = shape
    planes = 8
    cell = src[0, slot] - (lax.axis_index("tile") * planes + plane) * (rows * lanes)
    at = lax.broadcasted_iota(jnp.int32, shape, 0) * lanes + lax.broadcasted_iota(jnp.int32, shape, 1)
    return jnp.where(at == cell, SOURCE_AMP, 0.0).astype(F32)


def head_kernel(
    table_in, count, fwd, adj, label, cut,
    msg_a, msg_b, kxf, ky, kz, dd, inv, mass, weight,
    table, lab, flag, sig, fac, sems,
):
    slots = fwd.shape[1]
    planes, rows, lanes = label.shape
    last = planes - 1
    systems = 2 * slots
    core = lax.rem(lax.axis_index("grp"), 2)
    copies = [
        pltpu.make_async_copy(label, lab, sems.at[0]),
        pltpu.make_async_copy(cut, flag, sems.at[1]),
        pltpu.make_async_copy(table_in, table, sems.at[2]),
    ]
    edges = [(msg_a, jnp.where(core == 0, last, 0)), (msg_b, jnp.where(core == 1, last, 0))]
    for at, (msg, edge) in enumerate(edges):
        for half, source in enumerate((fwd, adj)):
            copies.append(
                pltpu.make_async_copy(
                    source.at[0, :, edge], msg.at[pl.ds(half * slots, slots)], sems.at[3 + 2 * at + half]
                )
            )
    for copy in copies:
        copy.start()
    slot = lax.broadcasted_iota(jnp.int32, weight.shape, 0)
    weight[...] = jnp.where(slot < count[0], -1.0 / slots, 0.0).astype(F32)
    for copy in copies[:3]:
        copy.wait()

    @pl.loop(0, planes)
    def _(p):
        names = lab[p]
        value = jnp.full((rows, lanes), table[0], F32)
        for region in range(1, table.shape[0]):
            value = jnp.where(names == region, table[region], value)
        factor = 1.0 - 0.5 * flag[p].astype(F32)
        sig[p] = value
        fac[p] = factor
        mass[p] = MASS * value
        face_y, face_z = lateral_faces(value, factor, harmonic)
        ky[p] = face_y
        kz[p] = face_z

    kxf[0] = jnp.zeros((rows, lanes), F32)
    kxf[planes] = jnp.zeros((rows, lanes), F32)

    @pl.loop(1, planes)
    def _(p):
        kxf[p] = harmonic(sig[p - 1], sig[p]) * fac[p - 1]

    @pl.loop(0, planes)
    def _(p):
        face_y, face_z = ky[p], kz[p]
        diag = mass[p] + kxf[p] + kxf[p + 1] + face_y + prev_y(face_y) + face_z + prev_z(face_z)
        dd[p] = diag
        inv[p] = 1.0 / diag

    for msg, edge in edges:
        msg[systems] = sig[edge]
        msg[systems + 1] = fac[edge]
        msg[systems + 2] = dd[edge]
    for copy in copies[3:]:
        copy.wait()


def edges_kernel(
    src_in, fwd, adj, rhs, head_a, head_b, kxf, ky, kz, inv, msg_a, msg_b, src, xs, rs, sems
):
    slots = fwd.shape[1]
    systems = 2 * slots
    planes, rows, lanes = ky.shape
    last = planes - 1
    first, other = pl.ds(0, slots), pl.ds(slots, slots)
    copies = [
        pltpu.make_async_copy(src_in, src, sems.at[0]),
        pltpu.make_async_copy(fwd.at[0, :, pl.ds(1, 2)], xs.at[first, pl.ds(0, 2)], sems.at[1]),
        pltpu.make_async_copy(adj.at[0, :, pl.ds(1, 2)], xs.at[other, pl.ds(0, 2)], sems.at[2]),
        pltpu.make_async_copy(fwd.at[0, :, pl.ds(planes - 3, 2)], xs.at[first, pl.ds(2, 2)], sems.at[3]),
        pltpu.make_async_copy(adj.at[0, :, pl.ds(planes - 3, 2)], xs.at[other, pl.ds(2, 2)], sems.at[4]),
        pltpu.make_async_copy(rhs.at[0, :, pl.ds(0, 2)], rs.at[:, pl.ds(0, 2)], sems.at[5]),
        pltpu.make_async_copy(rhs.at[0, :, pl.ds(planes - 2, 2)], rs.at[:, pl.ds(2, 2)], sems.at[6]),
    ]
    for copy in copies:
        copy.start()
    for copy in copies:
        copy.wait()
    core = lax.rem(lax.axis_index("grp"), 2)
    half = slots // 2
    for head, msg, up in ((head_a, msg_a, core == 0), (head_b, msg_b, core == 1)):
        edge, inner = jnp.where(up, last, 0), jnp.where(up, last - 1, 1)
        at_inner, at_next = jnp.where(up, 3, 0), jnp.where(up, 2, 1)
        rs_edge, rs_inner = jnp.where(up, 3, 0), jnp.where(up, 2, 1)
        face, face_next = jnp.where(up, last, 1), jnp.where(up, last - 1, 2)
        lead = jnp.where(up, half, 0)

        def partial(s, right):
            msg[s] = right + lateral(head[s], ky[edge], kz[edge]) + kxf[face] * xs[s, at_inner]

        def onward(at, s, right):
            x1 = xs[s, at_inner]
            total = right + lateral(x1, ky[inner], kz[inner])
            total = total + kxf[face] * head[s] + kxf[face_next] * xs[s, at_next]
            msg[systems + at] = kxf[face] * (inv[inner] * total - x1)

        @pl.loop(0, slots)
        def _(s):
            partial(s, plane_source(src, s, edge, (rows, lanes)))
            partial(slots + s, rs[s, rs_edge])

        @pl.loop(0, half)
        def _(s):
            slot = lead + s
            onward(s, slot, plane_source(src, slot, inner, (rows, lanes)))
            onward(half + s, slots + slot, rs[slot, rs_inner])


def interior_kernel(src_in, fwd, adj, rhs, kxf, ky, kz, dd, inv, x, z, n, moments, extra, src, rs, sems):
    slots = fwd.shape[1]
    planes, rows, lanes = x.shape[1:]
    last = planes - 1
    copies = [
        pltpu.make_async_copy(fwd.at[0], x.at[pl.ds(0, slots)], sems.at[0]),
        pltpu.make_async_copy(adj.at[0], x.at[pl.ds(slots, slots)], sems.at[1]),
        pltpu.make_async_copy(rhs.at[0], rs, sems.at[2]),
        pltpu.make_async_copy(src_in, src, sems.at[3]),
    ]
    for copy in copies:
        copy.start()
    for copy in copies:
        copy.wait()

    def one(s, right):
        for p in range(1, last):
            total = right(p) + lateral(x[s, p], ky[p], kz[p])
            total = total + kxf[p] * x[s, p - 1] + kxf[p + 1] * x[s, p + 1]
            z[s, p] = inv[p] * total - x[s, p]
        c0 = jnp.zeros((8, 128), F32)
        c1, c2, c3 = c0, c0, c0
        for p in range(1, last):
            v = z[s, p]
            c0 = c0 + folded(dd[p] * v * v)
            w = lateral(v, ky[p], kz[p])
            if p > 1:
                w = w + kxf[p] * z[s, p - 1]
            if p < last - 1:
                w = w + kxf[p + 1] * z[s, p + 1]
            if p == 1 or p == last - 1:
                n[s, p] = w
                continue
            m = inv[p] * w
            n[s, p] = m
            c1 = c1 + folded(v * w)
            c2 = c2 + folded(m * w)
            near = upper_lateral(m, ky[p], kz[p])
            if p > 2:
                near = near + kxf[p] * n[s, p - 1]
            c3 = c3 + folded(m * near)
        for at, c in enumerate((c0, c1, c2, c3)):
            moments[s, at] = c

    @pl.loop(0, slots)
    def _(s):
        one(s, lambda p: plane_source(src, s, p, (rows, lanes)))

    @pl.loop(0, slots)
    def _(s):
        one(slots + s, lambda p: rs[s, p])

    half = slots // 2
    for at in range(half):
        extra[at] = kxf[1] * z[half + at, 1]
        extra[half + at] = kxf[1] * z[slots + half + at, 1]


def both_sides(planes, slots, pairs):
    last, half = planes - 1, slots // 2
    core = lax.rem(lax.axis_index("grp"), 2)
    found = []
    for at, pair in enumerate(pairs):
        low = core == at
        found.append(
            (
                at, pair, low, jnp.where(low, 0, 1),
                jnp.where(low, 0, last), jnp.where(low, 1, last - 1), jnp.where(low, 2, last - 2),
                jnp.where(low, 1, last), jnp.where(low, 2, last - 1), jnp.where(low, half, 0),
            )
        )
    return found


def near_kernel(
    got_a, got_b, head_a, head_b, msg_a, msg_b, kxf, ky, kz, dd, inv, z_in, n_in, moments_in,
    z, n, part, ext_x, far, moments,
    coef,
):
    systems, planes, rows, lanes = z.shape
    sides = both_sides(planes, systems // 2, ((got_a, head_b, msg_b), (got_b, head_a, msg_a)))
    for at, (got, head, _), low, side, edge, _, _, _, _, _ in sides:
        cross = harmonic(got[systems], head[systems])
        cross = cross * jnp.where(low, got[systems + 1], head[systems + 1])
        here = dd[edge] + cross
        there = got[systems + 2] + cross
        real = there > 0.0
        coef[at] = here
        far[side, 0] = cross
        far[side, 1] = jnp.where(real, 1.0 / jnp.where(real, there, 1.0), 0.0)
        face_y, face_z = lateral_faces(got[systems], got[systems + 1], harmonic_or_zero)
        far[side, 2] = face_y
        far[side, 3] = face_z
        far[side, 4] = 1.0 / here

    @pl.loop(0, systems)
    def _(s):
        c0, c1, c2, c3 = [moments_in[s, at] for at in range(4)]
        for at, (got, head, msg), _, side, edge, inner, third, face, face_next, _ in sides:
            xm = got[s]
            z0 = far[side, 4] * (msg[s] + far[side, 0] * xm) - head[s]
            z1 = z_in[s, inner]
            w0 = lateral(z0, ky[edge], kz[edge]) + kxf[face] * z1
            w1 = n_in[s, inner] + kxf[face] * z0
            n1 = inv[inner] * w1
            z[s, edge] = z0
            n[s, inner] = n1
            part[side, s] = w0
            ext_x[side, s] = xm
            c0 = c0 + folded(coef[at] * z0 * z0)
            c1 = c1 + folded(z0 * w0 + z1 * w1)
            c2 = c2 + folded(n1 * w1)
            near1 = upper_lateral(n1, ky[inner], kz[inner]) + kxf[face_next] * n_in[s, third]
            c3 = c3 + folded(n1 * near1)
        for at, c in enumerate((c0, c1, c2, c3)):
            moments[s, at] = c


def boundary_kernel(
    got_a, got_b, head_a, head_b, kxf, ky, kz, far, ext_x, part, z, n_in, moments,
    n, ext_z, ext_n, out,
    sums,
):
    systems, planes, rows, lanes = n.shape
    slots = systems // 2
    half = slots // 2
    sides = both_sides(planes, slots, ((got_a, head_b), (got_b, head_a)))

    @pl.loop(0, systems)
    def _(s):
        c0, c1, c2, c3 = [moments[s, at] for at in range(4)]
        for _, (got, head), _, side, edge, inner, _, face, _, _ in sides:
            cross = far[side, 0]
            z0 = z[s, edge]
            zm = far[side, 1] * (got[s] + cross * head[s]) - ext_x[side, s]
            over = cross * zm
            w0 = part[side, s] + over
            n0 = far[side, 4] * w0
            n[s, edge] = n0
            ext_z[side, s] = zm
            c1 = c1 + folded(z0 * over)
            c2 = c2 + folded(n0 * w0)
            near0 = upper_lateral(n0, ky[edge], kz[edge]) + kxf[face] * n_in[s, inner]
            c3 = c3 + folded(n0 * near0)
        for at, c in enumerate((c0, c1, c2, c3 + c3)):
            sums[at, pl.ds(s, 1)] = c.sum(0, keepdims=True)

    @pl.loop(0, half)
    def _(at):
        for _, (got, _), _, side, edge, _, _, _, _, lead in sides:
            for place, s in ((at, lead + at), (half + at, slots + lead + at)):
                cross = far[side, 0]
                w = lateral(ext_z[side, s], far[side, 2], far[side, 3])
                w = w + got[systems + place] + cross * z[s, edge]
                nm = far[side, 1] * w
                ext_n[side, s] = nm
                pair = folded(cross * nm * n[s, edge])
                sums[3, pl.ds(s, 1)] = sums[3, pl.ds(s, 1)] + 2.0 * pair.sum(0, keepdims=True)

    lanes_at = lax.broadcasted_iota(jnp.int32, (systems, 128), 1)
    packed = jnp.zeros((systems, 128), F32)
    for at in range(4):
        packed = packed + jnp.where(lanes_at == at, sums[at].sum(1, keepdims=True), 0.0)
    out[...] = jnp.broadcast_to(packed[None], out.shape)


def correlate_kernel(
    weight, parts, x, z, n, ext_x, ext_z, ext_n, far, extra, kxf, ky, kz, mass, keep, give, scale, total
):
    systems, planes, rows, lanes = z.shape
    slots = systems // 2
    half = slots // 2
    last = planes - 1
    summed = parts[...].sum(0)
    lanes_at = lax.broadcasted_iota(jnp.int32, summed.shape, 1)
    c0, c1, c2, c3 = [
        jnp.where(lanes_at == at, summed, 0.0).sum(1, keepdims=True) for at in range(4)
    ]
    alpha = c0 / (c0 - c1)
    rest = 1.0 - alpha
    rz = rest * rest * c0 + 2.0 * alpha * rest * c1 + alpha * alpha * c2
    first = rest + rz / c0
    curve = first * first * (c0 - c1) + 2.0 * first * alpha * (c1 - c2) + alpha * alpha * (c2 - c3)
    step = rz / curve
    scale[0] = jnp.broadcast_to(alpha + step * first, (systems, lanes))
    scale[1] = jnp.broadcast_to(step * alpha, (systems, lanes))

    def slot_terms(s, fresh):
        ends = (s, slots + s)
        share = weight[pl.ds(s, 1)]
        on_z = [scale[0, pl.ds(e, 1)] for e in ends]
        on_n = [scale[1, pl.ds(e, 1)] for e in ends]

        def field(p):
            return [x[e, p] + on_z[i] * z[e, p] + on_n[i] * n[e, p] for i, e in enumerate(ends)]

        def outside():
            found = []
            for i, e in enumerate(ends):
                zm = ext_z[1, e]
                if s < half:
                    nm = ext_n[1, e]
                else:
                    w = lateral(zm, far[1, 2], far[1, 3]) + extra[s - half + i * half]
                    nm = far[1, 1] * (w + far[1, 0] * z[e, last])
                found.append(ext_x[1, e] + on_z[i] * zm + on_n[i] * nm)
            return found

        u, v = field(0)
        for p in range(planes):
            u_up, v_up = field(p + 1) if p < last else outside()
            face_x = kxf[p + 1] if p < last else far[1, 0]
            corr = face_x * (u_up - u) * (v_up - v)
            corr = corr + ky[p] * (next_y(u) - u) * (next_y(v) - v)
            corr = corr + kz[p] * (next_z(u) - u) * (next_z(v) - v)
            corr = corr + mass[p] * u * v
            total[p] = share * corr if fresh else total[p] + share * corr
            u, v = u_up, v_up

    for s in range(slots):
        slot_terms(s, s == 0)
    core = lax.rem(lax.axis_index("grp"), 2)
    deep = keep.shape[2]
    for at in range(keep.shape[0]):
        keep[at] = total[:, pl.ds(pl.multiple_of((2 * at + core) * deep, 8), deep)]
        give[at] = total[:, pl.ds(pl.multiple_of((2 * at + 1 - core) * deep, 8), deep)]


def merge_kernel(keep, got, own, to_1, to_2, to_3):
    mine = lax.div(lax.axis_index("grp"), 2)
    for at, out in enumerate((own, to_1, to_2, to_3)):
        block = jnp.bitwise_xor(mine, at)
        out[...] = keep[block] + got[block]


def total_kernel(own, one, two, three, out):
    out[...] = (own[...] + one[...]) + (two[...] + three[...])


def local(
    fwd_start, adj_start, adj_rhs, src_cell, group_count, region_label, cut_flag, region_sigma
):
    slots = fwd_start.shape[1]
    systems = 2 * slots
    planes, rows, lanes = region_label.shape
    groups = lax.axis_size("grp")
    tiles = lax.axis_size("tile")
    cells = planes * rows * lanes

    def held(*shape):
        return VMEM(shape, F32)

    def in_hbm(*arrays):
        return [pltpu.with_memory_space_constraint(a, pltpu.HBM) for a in arrays]

    def pinned(*arrays):
        return [pltpu.with_memory_space_constraint(a, pltpu.VMEM) for a in arrays]

    def params(**more):
        return pltpu.CompilerParams(vmem_limit_bytes=LIMIT, **more)

    half = slots // 2
    field = held(systems, planes, rows, lanes)
    plane_set = held(planes, rows, lanes)
    head = held(systems + 3, rows, lanes)
    message = held(systems + 2 * half, rows, lanes)
    HEAD, EDGES, INTERIOR, NEAR = 20, 20, 1, 10000

    def cost(scale):
        return pl.CostEstimate(flops=scale * cells, bytes_accessed=scale * cells, transcendentals=0)


    def opposite(value, parity):
        pairs = []
        for g in range(groups):
            by = 1 if g % 2 == parity else -1
            pairs += [(g * tiles + t, g * tiles + t + by) for t in range(tiles) if 0 <= t + by < tiles]
        return lax.ppermute(value, ("grp", "tile"), pairs)

    head_a, head_b, kxf, ky, kz, dd, inv, mass, weight = pl.pallas_call(
        head_kernel,
        out_shape=[
            head, head,
            held(planes + 1, rows, lanes),
            plane_set, plane_set, plane_set, plane_set, plane_set,
            held(8, lanes),
        ],
        in_specs=[IN_HBM, IN_SMEM] + [IN_HBM] * 4,
        out_specs=[IN_VMEM] * 9,
        scratch_shapes=[
            pltpu.SMEM(region_sigma.shape, F32),
            VMEM((planes, rows, lanes), jnp.int32),
            VMEM((planes, rows, lanes), jnp.int32),
            VMEM((planes, rows, lanes), F32),
            VMEM((planes, rows, lanes), F32),
            pltpu.SemaphoreType.DMA((7,)),
        ],
        compiler_params=params(),
        cost_estimate=cost(HEAD),
        name="head",
    )(
        *in_hbm(region_sigma), group_count,
        *in_hbm(fwd_start, adj_start, region_label, cut_flag),
    )
    near_a = opposite(head_a, 0)
    near_b = opposite(head_b, 1)

    msg_a, msg_b = pl.pallas_call(
        edges_kernel,
        out_shape=[message, message],
        in_specs=[IN_HBM] * 4 + [IN_VMEM] * 6,
        out_specs=[IN_VMEM] * 2,
        scratch_shapes=[
            pltpu.SMEM(src_cell.shape, jnp.int32),
            VMEM((systems, 4, rows, lanes), F32),
            VMEM((slots, 4, rows, lanes), F32),
            pltpu.SemaphoreType.DMA((7,)),
        ],
        compiler_params=params(),
        cost_estimate=cost(EDGES),
        name="edges",
    )(
        *in_hbm(src_cell, fwd_start, adj_start, adj_rhs),
        *pinned(head_a, head_b, kxf, ky, kz, inv),
    )
    got_a = opposite(msg_a, 0)
    got_b = opposite(msg_b, 1)

    x, z, n, moments, extra = pl.pallas_call(
        interior_kernel,
        out_shape=[field, field, field, held(systems, 4, 8, 128), held(2 * half, rows, lanes)],
        in_specs=[IN_HBM] * 4 + [IN_VMEM] * 5,
        out_specs=[IN_VMEM] * 5,
        scratch_shapes=[
            pltpu.SMEM(src_cell.shape, jnp.int32),
            VMEM((slots, planes, rows, lanes), F32),
            pltpu.SemaphoreType.DMA((4,)),
        ],
        compiler_params=params(),
        cost_estimate=cost(INTERIOR),
        name="interior",
    )(*in_hbm(src_cell, fwd_start, adj_start, adj_rhs), *pinned(kxf, ky, kz, dd, inv))

    pair_of = held(2, systems, rows, lanes)
    z, n, part, ext_x, far, moments = pl.pallas_call(
        near_kernel,
        out_shape=[field, field, pair_of, pair_of, held(2, 5, rows, lanes), held(systems, 4, 8, 128)],
        in_specs=[IN_VMEM] * 14,
        out_specs=[IN_VMEM] * 6,
        input_output_aliases={11: 0, 12: 1},
        scratch_shapes=[VMEM((2, rows, lanes), F32)],
        compiler_params=params(),
        cost_estimate=cost(NEAR),
        name="near",
    )(*pinned(near_a, near_b, head_a, head_b, msg_a, msg_b, kxf, ky, kz, dd, inv, z, n, moments))

    n, ext_z, ext_n, moments = pl.pallas_call(
        boundary_kernel,
        out_shape=[field, pair_of, pair_of, held(tiles, systems, 128)],
        in_specs=[IN_VMEM] * 13,
        out_specs=[IN_VMEM] * 4,
        input_output_aliases={11: 0},
        scratch_shapes=[VMEM((4, systems, 128), F32)],
        compiler_params=params(),
        name="boundary",
    )(*pinned(got_a, got_b, head_a, head_b, kxf, ky, kz, far, ext_x, part, z, n, moments))

    moments, extra = lax.optimization_barrier((moments, extra))
    late = lax.ppermute(extra, "tile", [(i + 1, i) for i in range(tiles - 1)])
    parts = lax.all_to_all(moments, "tile", 0, 0)

    blocks = held(groups // 2, planes, rows // groups, lanes)
    block = held(planes, rows // groups, lanes)
    keep, give = pl.pallas_call(
        correlate_kernel,
        out_shape=[blocks, blocks],
        in_specs=[IN_VMEM] * 14,
        out_specs=[IN_VMEM] * 2,
        scratch_shapes=[VMEM((2, systems, lanes), F32), VMEM((planes, rows, lanes), F32)],
        compiler_params=params(),
        name="correlate",
    )(*pinned(weight, parts, x, z, n, ext_x, ext_z, ext_n, far, late, kxf, ky, kz, mass))

    def swapped(value, by):
        return lax.ppermute(value, "grp", [(g, g ^ by) for g in range(groups)])

    got = swapped(give, 1)
    own, *sent = pl.pallas_call(
        merge_kernel,
        out_shape=[block] * 4,
        in_specs=[IN_VMEM] * 2,
        out_specs=[IN_VMEM] * 4,
        compiler_params=params(),
        name="merge",
    )(*pinned(keep, got))
    came = [swapped(value, 2 * (at + 1)) for at, value in enumerate(sent)]
    return pl.pallas_call(
        total_kernel,
        out_shape=jax.ShapeDtypeStruct((planes, rows // groups, lanes), F32),
        in_specs=[IN_VMEM] * 4,
        out_specs=IN_VMEM,
        compiler_params=params(),
        name="total",
    )(*pinned(own, *came))


def solution(mesh):
    in_specs = (
        P("grp", None, "tile", None, None),
        P("grp", None, "tile", None, None),
        P("grp", None, "tile", None, None),
        P("grp", None),
        P("grp"),
        P("tile", None, None),
        P("tile", None, None),
        P(),
    )
    out_specs = P("tile", "grp", None)
    return jax.shard_map(local, mesh=mesh, in_specs=in_specs, out_specs=out_specs, check_vma=False)
```

time: 93.4 us -> 84.6 us (0.906)
  blocking collectives: 40.9 us -> 23.4 us
  starting transfers between devices: 6.03 us -> 19 us
  waiting for transfers between devices: 23.6 us -> 14.7 us
  Pallas kernels: 21.2 us -> 26.4 us
    all_to_all x1 -> x0, blocking collectives: 16.6 us -> none  [local(): blocks = lax.all_to_all(term, 'grp', 0, 0)]
    ppermute x2 -> x9, starting transfers between devices: 6.03 us -> 19 us  [the longest x4 11.3 us: opposite(): return lax.ppermute(value, ('grp', 'tile'), pairs)]
    ppermute x2 -> x9, waiting for transfers between devices: 23.6 us -> 14.7 us  [the longest x4 9.28 us: opposite(): return lax.ppermute(value, ('grp', 'tile'), pairs)]
    pallas_call x3 -> x7, Pallas kernels: 10.8 us -> 15.1 us  [the longest x1 3.67 us: local(): pl.pallas_call(edges_kernel, out_shape=[message, message], in_specs=[IN_H...]
    all_to_all x1, blocking collectives: 24.4 us -> 23.4 us  [local(): parts = lax.all_to_all(moments, 'tile', 0, 0)]
  transfers between devices with their start and end apart: 2 -> 9, of which waited for: 2 -> 5; matrix products, arithmetic and copies ran while one was open for 0% -> 0% of each run, Pallas kernels for 11% -> 21%
where the time goes in v2:
time: 84.6 us; the launch traced here: 84.3 us
  Pallas kernels  26.4 us (31%)
  blocking collectives  23.4 us (28%)
  starting transfers between devices  19 us (22%)
  waiting for transfers between devices  14.7 us (17%)
    all_to_all x1, blocking collectives, local(): parts = lax.all_to_all(moments, 'tile', 0, 0)  23.4 us
    ppermute x4, starting transfers between devices, opposite(): return lax.ppermute(value, ('grp', 'tile'), pairs)  11.3 us
    pallas_call x1, Pallas kernels, local(): pl.pallas_call(interior_kernel, out_shape=[field, field, field, held(syst...  11.3 us
    ppermute x4, waiting for transfers between devices, opposite(): return lax.ppermute(value, ('grp', 'tile'), pairs)  9.28 us
    ppermute x4, starting transfers between devices, swapped(): return lax.ppermute(value, 'grp', [(g, g ^ by) for g in range(groups)])  6.42 us
    ppermute x4, waiting for transfers between devices, swapped(): return lax.ppermute(value, 'grp', [(g, g ^ by) for g in range(groups)])  5.42 us
    pallas_call x1, Pallas kernels, local(): pl.pallas_call(edges_kernel, out_shape=[message, message], in_specs=[IN_H...  3.67 us
    pallas_call x1, Pallas kernels, local(): pl.pallas_call(correlate_kernel, out_shape=[blocks, blocks], in_specs=[IN...  3.41 us
  transfers between devices with their start and end apart: 9, of which 5 were waited for; matrix products, arithmetic and copies ran while one was open for 0% of the time, Pallas kernels for 21%

profile of v2, /device:TPU:1, one launch (start us, length us, event | category | flops | bytes accessed | tf_op | source)
XLA Modules:
  0.0 84.3 jit_solution(1637857636681087052)
XLA Ops:
  0.7 3.1 %head.1 = (f32[11,64,256]{2,1,0:T(8,128)S(1)}, f32[11,64,256]{2,1,0:T(8,128)S(1)}, f32[9,64,256]{2,1,0:T(8,128)S(1)}, f32[8,64,256]{2,1,0:T(8,128)S(1)}, f32[8,6...) custom-call(f32[8]{0:T(128)} %table_in.1, ...), custom_call_target="tpu_custom_call" | custom-call | flops 2621440 | bytes 2621440 | tf_op jit(solution)/shard_map/head/pallas_call | solution.py:472
  3.8 1.3 %collective-permute-start.2 = (f32[11,64,256]{2,1,0:T(8,128)S(1)}, f32[11,64,256]{2,1,0:T(8,128)S(1)}, u32[]{:S(2)}, u32[]{:S(2)}) collective-permute-start(f32[11,64,256]{2,1,0:T(8,128)S(1)} %get-tuple-element.40.head_a), channel_id=1, source_target_pairs={{0,1},{1,2},{2,3},{3,4},{4,5},{5,6},{6,7},{7,8},{8,9},{9,10},{10,1... | collective-permute-start | bytes 2162696 | tf_op jit(solution)/shard_map/ppermute | solution.py:470
  5.1 4.7 %collective-permute-start.3 = (f32[11,64,256]{2,1,0:T(8,128)S(1)}, f32[11,64,256]{2,1,0:T(8,128)S(1)}, u32[]{:S(2)}, u32[]{:S(2)}) collective-permute-start(f32[11,64,256]{2,1,0:T(8,128)S(1)} %get-tuple-element.41.head_b), channel_id=1, source_target_pairs={{1,0},{2,1},{3,2},{4,3},{5,4},{6,5},{7,6},{8,7},{9,8},{10,9},{11,1... | collective-permute-start | bytes 2162696 | tf_op jit(solution)/shard_map/ppermute | solution.py:470
  9.8 3.7 %edges.1 = (f32[12,64,256]{2,1,0:T(8,128)S(1)}, f32[12,64,256]{2,1,0:T(8,128)S(1)}) custom-call(s32[1,4]{1,0:T(1,128)} %src_in.3, f32[1,4,8,64,256]{4,3,2,1,0:T(8,128)} %fwd.5, f32[1,4,8,64,256]{4,3,2,1,0:T(8,128)} %adj.5, f32[1,4,8,64,256]{4,3,2,1,0:T(8,128)} %rhs.3, f32[11,64,256]{2,1,0:T(8,128)S(1)} %get-tuple-element.40.head_a, ...), custom_call_target="tpu_custom_call" | custom-call | flops 2621440 | bytes 2621440 | tf_op jit(solution)/shard_map/edges/pallas_call | solution.py:500
  13.4 1.3 %collective-permute-start = (f32[12,64,256]{2,1,0:T(8,128)S(1)}, f32[12,64,256]{2,1,0:T(8,128)S(1)}, u32[]{:S(2)}, u32[]{:S(2)}) collective-permute-start(f32[12,64,256]{2,1,0:T(8,128)S(1)} %get-tuple-element.46.msg_a), channel_id=1, source_target_pairs={{0,1},{1,2},{2,3},{3,4},{4,5},{5,6},{6,7},{7,8},{8,9},{9,10},{10,1... | collective-permute-start | bytes 2359304 | tf_op jit(solution)/shard_map/ppermute | solution.py:470
  14.7 4.0 %collective-permute-start.1 = (f32[12,64,256]{2,1,0:T(8,128)S(1)}, f32[12,64,256]{2,1,0:T(8,128)S(1)}, u32[]{:S(2)}, u32[]{:S(2)}) collective-permute-start(f32[12,64,256]{2,1,0:T(8,128)S(1)} %get-tuple-element.47.msg_b), channel_id=1, source_target_pairs={{1,0},{2,1},{3,2},{4,3},{5,4},{6,5},{7,6},{8,7},{9,8},{10,9},{11,1... | collective-permute-start | bytes 2359304 | tf_op jit(solution)/shard_map/ppermute | solution.py:470
  18.8 11.3 %interior.1 = (f32[8,8,64,256]{3,2,1,0:T(8,128)S(1)}, f32[8,8,64,256]{3,2,1,0:T(8,128)S(1)}, f32[8,8,64,256]{3,2,1,0:T(8,128)S(1)}, f32[8,4,8,128]{3,2,1,0:T(8,128)S(1)}, f32[4,64,256]{2,1,0:T(8,128)S(1)}) custom-call(s32[1,4]{1,0:T(1,128)} %src_in.3, f32[1,4,8,64,256]{4,3,2,1,0:T(8,128)} %fwd.5, f32[1,4,8,64,256]{4,3,2,1,0:T(8,128)} %adj.5, ...), custom_call_target="tpu_custom_call" | custom-call | flops 131072 | bytes 131072 | tf_op jit(solution)/shard_map/interior/pallas_call | solution.py:521
  30.1 0.0 collective-permute-done.2.got_a
  30.1 0.0 collective-permute-done.3.got_b
  30.1 2.3 %near.1 = (f32[8,8,64,256]{3,2,1,0:T(8,128)S(1)}, f32[8,8,64,256]{3,2,1,0:T(8,128)S(1)}, f32[2,8,64,256]{3,2,1,0:T(8,128)S(1)}, f32[2,8,64,256]{3,2,1,0:T(8,128)...) custom-call(f32[11,64,256]{2,1,0:T(8,128)S(1)} %collective-permute-d, ...), custom_call_target="tpu_custom_call", output_to_operand_aliasing={{0}: (11, {}), {1}: (12, {})} | custom-call | flops 1310720000 | bytes 1310720000 | tf_op jit(solution)/shard_map/near/pallas_call | solution.py:537
  32.5 4.0 %collective-permute-done.got_a = f32[12,64,256]{2,1,0:T(8,128)S(1)} collective-permute-done((f32[12,64,256]{2,1,0:T(8,128)S(1)}, f32[12,64,256]{2,1,0:T(8,128)S(1)}, u32[]{:S(2)}, u32[]{:S(2)}) %collective-permute-start) | collective-permute-done | bytes 786464 | tf_op jit(solution)/shard_map/ppermute | solution.py:470
  36.4 5.3 %collective-permute-done.1.got_b = f32[12,64,256]{2,1,0:T(8,128)S(1)} collective-permute-done((f32[12,64,256]{2,1,0:T(8,128)S(1)}, f32[12,64,256]{2,1,0:T(8,128)S(1)}, u32[]{:S(2)}, u32[]{:S(2)}) %collective-permute-start.1) | collective-permute-done | bytes 786464 | tf_op jit(solution)/shard_map/ppermute | solution.py:470
  41.7 1.9 %boundary.1 = (f32[8,8,64,256]{3,2,1,0:T(8,128)S(1)}, f32[2,8,64,256]{3,2,1,0:T(8,128)S(1)}, f32[2,8,64,256]{3,2,1,0:T(8,128)S(1)}, f32[32,8,128]{2,1,0:T(8,128)S(1)}) custom-call(f32[12,64,256]{2,1,0:T(8,128)S(1)} %collective-permute-done.got_a, f32[12,64,256]{2,1,0:T(8,128)S(1)} %collective-permute-done.1.got_b, ...), custom_call_target="tpu_custom_call", output_to_operand_aliasing={{0}: (11, {})} | custom-call | tf_op jit(solution)/shard_map/boundary/pallas_call | solution.py:549
  43.7 1.3 %collective-permute-start.4 = (f32[4,64,256]{2,1,0:T(8,128)S(1)}, f32[4,64,256]{2,1,0:T(8,128)S(1)}, u32[]{:S(2)}, u32[]{:S(2)}) collective-permute-start(f32[4,64,256]{2,1,0:T(8,128)S(1)} %get-tuple-element.65), channel_id=1, source_target_pairs={{1,0},{2,1},{3,2},{4,3},{5,4},{6,5},{7,6},{8,7},{9,8},{10,9},{11,1... | collective-permute-start | bytes 786440 | tf_op jit(solution)/shard_map/ppermute | solution.py:561
  45.0 23.4 %all_to_all.5.parts = f32[32,8,128]{2,1,0:T(8,128)S(1)} all-to-all(f32[32,8,128]{2,1,0:T(8,128)S(1)} %get-tuple-element.60), channel_id=1, replica_groups=mesh['grp'=8,'tile'=32] {'tile'}, dimensions={0} | all-to-all | bytes 262144 | tf_op jit(solution)/shard_map/all_to_all | solution.py:562
  68.4 0.0 collective-permute-done.4.extra
  68.4 3.4 %correlate.1 = (f32[4,8,8,256]{3,2,1,0:T(8,128)S(1)}, f32[4,8,8,256]{3,2,1,0:T(8,128)S(1)}) custom-call(f32[8,256]{1,0:T(8,128)S(1)} %get-tuple-element.39.weight, f32[32,8,128]{2,1,0:T(8,128)S(1)} %all_to_all.5.parts, f32[8,8,64,256]{3,2,1,0:T(8,128)S(1)} %get-tuple-element.61.x, f32[8,8,64,256]{3,2,1,0:T(8,128)S(1)} %get-tuple-element.55.z, ...), custom_call_target="tpu_custom_call" | custom-call | tf_op jit(solution)/shard_map/correlate/pallas_call | solution.py:566
  71.8 2.5 %collective-permute-start.5 = (f32[4,8,8,256]{3,2,1,0:T(8,128)S(1)}, f32[4,8,8,256]{3,2,1,0:T(8,128)S(1)}, u32[]{:S(2)}, u32[]{:S(2)}) collective-permute-start(f32[4,8,8,256]{3,2,1,0:T(8,128)S(1)} %get-tuple-element.68), channel_id=1, source_target_pairs={{0,32},{32,0},{64,96},{96,64},{128,160},{160,128},{192,224},{224,1... | collective-permute-start | bytes 786440 | tf_op jit(solution)/shard_map/ppermute | solution.py:577
  74.3 1.2 %collective-permute-done.5.got = f32[4,8,8,256]{3,2,1,0:T(8,128)S(1)} collective-permute-done((f32[4,8,8,256]{3,2,1,0:T(8,128)S(1)}, f32[4,8,8,256]{3,2,1,0:T(8,128)S(1)}, u32[]{:S(2)}, u32[]{:S(2)}) %collective-permute-start.5) | collective-permute-done | bytes 262176 | tf_op jit(solution)/shard_map/ppermute | solution.py:577
  75.5 1.3 %collective-permute-start.6 = (f32[8,8,256]{2,1,0:T(8,128)S(1)}, f32[8,8,256]{2,1,0:T(8,128)S(1)}, u32[]{:S(2)}, u32[]{:S(2)}) collective-permute-start(f32[8,8,256]{2,1,0:T(8,128)S(1)} %get-tuple-element.70), channel_id=1, source_target_pairs={{0,64},{32,96},{64,0},{96,32},{128,192},{160,224},{192,128},{224,1... | collective-permute-start | bytes 196616 | tf_op jit(solution)/shard_map/ppermute | solution.py:577
  76.8 2.5 %collective-permute-start.7 = (f32[8,8,256]{2,1,0:T(8,128)S(1)}, f32[8,8,256]{2,1,0:T(8,128)S(1)}, u32[]{:S(2)}, u32[]{:S(2)}) collective-permute-start(f32[8,8,256]{2,1,0:T(8,128)S(1)} %get-tuple-element.71), channel_id=1, source_target_pairs={{0,128},{32,160},{64,192},{96,224},{128,0},{160,32},{192,64},{224,... | collective-permute-start | bytes 196616 | tf_op jit(solution)/shard_map/ppermute | solution.py:577
  79.2 0.2 collective-permute-start.8
  79.4 0.0 collective-permute-done.6.one
  79.4 2.7 %collective-permute-done.7.two = f32[8,8,256]{2,1,0:T(8,128)S(1)} collective-permute-done((f32[8,8,256]{2,1,0:T(8,128)S(1)}, f32[8,8,256]{2,1,0:T(8,128)S(1)}, u32[]{:S(2)}, u32[]{:S(2)}) %collective-permute-start.7) | collective-permute-done | bytes 65568 | tf_op jit(solution)/shard_map/ppermute | solution.py:577
  82.2 1.5 %collective-permute-done.8.three = f32[8,8,256]{2,1,0:T(8,128)S(1)} collective-permute-done((f32[8,8,256]{2,1,0:T(8,128)S(1)}, f32[8,8,256]{2,1,0:T(8,128)S(1)}, u32[]{:S(2)}, u32[]{:S(2)}) %collective-permute-start.8) | collective-permute-done | bytes 65568 | tf_op jit(solution)/shard_map/ppermute | solution.py:577
  83.7 0.6 total.1
  (1 shorter events, 0.0 us)
Async XLA Ops:
  3.8 26.4 %collective-permute-start.2 = (f32[11,64,256]{2,1,0:T(8,128)S(1)}, f32[11,64,256]{2,1,0:T(8,128)S(1)}, u32[]{:S(2)}, u32[]{:S(2)}) collective-permute-start(f32[11,64,256]{2,1,0:T(8,128)S(1)} %get-tuple-element.40.head_a), channel_id=1, source_target_pairs={{0,1},{1,2},{2,3},{3,4},{4,5},{5,6},{6,7},{7,8},{8,9},{9,10},{10,1... | collective-permute-start | bytes 2162696 | tf_op jit(solution)/shard_map/ppermute | solution.py:470
  5.1 25.1 %collective-permute-start.3 = (f32[11,64,256]{2,1,0:T(8,128)S(1)}, f32[11,64,256]{2,1,0:T(8,128)S(1)}, u32[]{:S(2)}, u32[]{:S(2)}) collective-permute-start(f32[11,64,256]{2,1,0:T(8,128)S(1)} %get-tuple-element.41.head_b), channel_id=1, source_target_pairs={{1,0},{2,1},{3,2},{4,3},{5,4},{6,5},{7,6},{8,7},{9,8},{10,9},{11,1... | collective-permute-start | bytes 2162696 | tf_op jit(solution)/shard_map/ppermute | solution.py:470
  13.4 23.0 %collective-permute-start = (f32[12,64,256]{2,1,0:T(8,128)S(1)}, f32[12,64,256]{2,1,0:T(8,128)S(1)}, u32[]{:S(2)}, u32[]{:S(2)}) collective-permute-start(f32[12,64,256]{2,1,0:T(8,128)S(1)} %get-tuple-element.46.msg_a), channel_id=1, source_target_pairs={{0,1},{1,2},{2,3},{3,4},{4,5},{5,6},{6,7},{7,8},{8,9},{9,10},{10,1... | collective-permute-start | bytes 2359304 | tf_op jit(solution)/shard_map/ppermute | solution.py:470
  14.7 27.0 %collective-permute-start.1 = (f32[12,64,256]{2,1,0:T(8,128)S(1)}, f32[12,64,256]{2,1,0:T(8,128)S(1)}, u32[]{:S(2)}, u32[]{:S(2)}) collective-permute-start(f32[12,64,256]{2,1,0:T(8,128)S(1)} %get-tuple-element.47.msg_b), channel_id=1, source_target_pairs={{1,0},{2,1},{3,2},{4,3},{5,4},{6,5},{7,6},{8,7},{9,8},{10,9},{11,1... | collective-permute-start | bytes 2359304 | tf_op jit(solution)/shard_map/ppermute | solution.py:470
  43.7 24.8 %collective-permute-start.4 = (f32[4,64,256]{2,1,0:T(8,128)S(1)}, f32[4,64,256]{2,1,0:T(8,128)S(1)}, u32[]{:S(2)}, u32[]{:S(2)}) collective-permute-start(f32[4,64,256]{2,1,0:T(8,128)S(1)} %get-tuple-element.65), channel_id=1, source_target_pairs={{1,0},{2,1},{3,2},{4,3},{5,4},{6,5},{7,6},{8,7},{9,8},{10,9},{11,1... | collective-permute-start | bytes 786440 | tf_op jit(solution)/shard_map/ppermute | solution.py:561
  71.8 3.6 %collective-permute-start.5 = (f32[4,8,8,256]{3,2,1,0:T(8,128)S(1)}, f32[4,8,8,256]{3,2,1,0:T(8,128)S(1)}, u32[]{:S(2)}, u32[]{:S(2)}) collective-permute-start(f32[4,8,8,256]{3,2,1,0:T(8,128)S(1)} %get-tuple-element.68), channel_id=1, source_target_pairs={{0,32},{32,0},{64,96},{96,64},{128,160},{160,128},{192,224},{224,1... | collective-permute-start | bytes 786440 | tf_op jit(solution)/shard_map/ppermute | solution.py:577
  75.5 3.9 %collective-permute-start.6 = (f32[8,8,256]{2,1,0:T(8,128)S(1)}, f32[8,8,256]{2,1,0:T(8,128)S(1)}, u32[]{:S(2)}, u32[]{:S(2)}) collective-permute-start(f32[8,8,256]{2,1,0:T(8,128)S(1)} %get-tuple-element.70), channel_id=1, source_target_pairs={{0,64},{32,96},{64,0},{96,32},{128,192},{160,224},{192,128},{224,1... | collective-permute-start | bytes 196616 | tf_op jit(solution)/shard_map/ppermute | solution.py:577
  76.8 5.4 %collective-permute-start.7 = (f32[8,8,256]{2,1,0:T(8,128)S(1)}, f32[8,8,256]{2,1,0:T(8,128)S(1)}, u32[]{:S(2)}, u32[]{:S(2)}) collective-permute-start(f32[8,8,256]{2,1,0:T(8,128)S(1)} %get-tuple-element.71), channel_id=1, source_target_pairs={{0,128},{32,160},{64,192},{96,224},{128,0},{160,32},{192,64},{224,... | collective-permute-start | bytes 196616 | tf_op jit(solution)/shard_map/ppermute | solution.py:577
  79.2 4.5 %collective-permute-start.8 = (f32[8,8,256]{2,1,0:T(8,128)S(1)}, f32[8,8,256]{2,1,0:T(8,128)S(1)}, u32[]{:S(2)}, u32[]{:S(2)}) collective-permute-start(f32[8,8,256]{2,1,0:T(8,128)S(1)} %get-tuple-element.72), channel_id=1, source_target_pairs={{0,192},{32,224},{64,128},{96,160},{128,64},{160,96},{192,0},{224,... | collective-permute-start | bytes 196616 | tf_op jit(solution)/shard_map/ppermute | solution.py:577

commit v3 on v2

--- a/solution.py
+++ b/solution.py
@@ -73,137 +73,153 @@
     return jnp.where(at == cell, SOURCE_AMP, 0.0).astype(F32)
 
 
-def head_kernel(
-    table_in, count, fwd, adj, label, cut,
-    msg_a, msg_b, kxf, ky, kz, dd, inv, mass, weight,
-    table, lab, flag, sig, fac, sems,
-):
+def conductivity(table, names):
+    value = jnp.full(names.shape, table[0], F32)
+    for region in range(1, table.shape[0]):
+        value = jnp.where(names == region, table[region], value)
+    return value
+
+
+def cut_factor(flags):
+    return 1.0 - 0.5 * flags.astype(F32)
+
+
+def head_kernel(table_in, fwd, adj, label, cut, msg_a, msg_b, table, lab, flag, shared, sems):
     slots = fwd.shape[1]
-    planes, rows, lanes = label.shape
+    planes = label.shape[0]
     last = planes - 1
     systems = 2 * slots
     core = lax.rem(lax.axis_index("grp"), 2)
+    front, back = pl.ds(0, 2), pl.ds(planes - 2, 2)
     copies = [
-        pltpu.make_async_copy(label, lab, sems.at[0]),
-        pltpu.make_async_copy(cut, flag, sems.at[1]),
-        pltpu.make_async_copy(table_in, table, sems.at[2]),
+        pltpu.make_async_copy(table_in, table, sems.at[0]),
+        pltpu.make_async_copy(label.at[front], lab.at[pl.ds(0, 2)], sems.at[1]),
+        pltpu.make_async_copy(label.at[back], lab.at[pl.ds(2, 2)], sems.at[2]),
+        pltpu.make_async_copy(cut.at[front], flag.at[pl.ds(0, 2)], sems.at[3]),
+        pltpu.make_async_copy(cut.at[back], flag.at[pl.ds(2, 2)], sems.at[4]),
     ]
-    edges = [(msg_a, jnp.where(core == 0, last, 0)), (msg_b, jnp.where(core == 1, last, 0))]
-    for at, (msg, edge) in enumerate(edges):
+    edges = [(msg_a, core == 0), (msg_b, core == 1)]
+    for at, (msg, up) in enumerate(edges):
+        edge = jnp.where(up, last, 0)
         for half, source in enumerate((fwd, adj)):
             copies.append(
                 pltpu.make_async_copy(
-                    source.at[0, :, edge], msg.at[pl.ds(half * slots, slots)], sems.at[3 + 2 * at + half]
+                    source.at[0, :, edge], msg.at[pl.ds(half * slots, slots)], sems.at[5 + 2 * at + half]
                 )
             )
     for copy in copies:
         copy.start()
-    slot = lax.broadcasted_iota(jnp.int32, weight.shape, 0)
-    weight[...] = jnp.where(slot < count[0], -1.0 / slots, 0.0).astype(F32)
-    for copy in copies[:3]:
+    for copy in copies[:5]:
         copy.wait()
-
-    @pl.loop(0, planes)
-    def _(p):
-        names = lab[p]
-        value = jnp.full((rows, lanes), table[0], F32)
-        for region in range(1, table.shape[0]):
-            value = jnp.where(names == region, table[region], value)
-        factor = 1.0 - 0.5 * flag[p].astype(F32)
-        sig[p] = value
-        fac[p] = factor
-        mass[p] = MASS * value
-        face_y, face_z = lateral_faces(value, factor, harmonic)
-        ky[p] = face_y
-        kz[p] = face_z
-
-    kxf[0] = jnp.zeros((rows, lanes), F32)
-    kxf[planes] = jnp.zeros((rows, lanes), F32)
-
-    @pl.loop(1, planes)
-    def _(p):
-        kxf[p] = harmonic(sig[p - 1], sig[p]) * fac[p - 1]
-
-    @pl.loop(0, planes)
-    def _(p):
-        face_y, face_z = ky[p], kz[p]
-        diag = mass[p] + kxf[p] + kxf[p + 1] + face_y + prev_y(face_y) + face_z + prev_z(face_z)
-        dd[p] = diag
-        inv[p] = 1.0 / diag
-
-    for msg, edge in edges:
-        msg[systems] = sig[edge]
-        msg[systems + 1] = fac[edge]
-        msg[systems + 2] = dd[edge]
-    for copy in copies[3:]:
+    sigma = [conductivity(table, lab[at]) for at in range(4)]
+    factor = [cut_factor(flag[at]) for at in range(4)]
+    faces = [harmonic(sigma[at], sigma[at + 1]) * factor[at] for at in (0, 2)]
+    for side, at in enumerate((0, 3)):
+        face_y, face_z = lateral_faces(sigma[at], factor[at], harmonic)
+        shared[side, 0] = sigma[at]
+        shared[side, 1] = factor[at]
+        diag = MASS * sigma[at] + faces[side] + face_y + prev_y(face_y) + face_z + prev_z(face_z)
+        shared[side, 2] = diag
+    for msg, up in edges:
+        side = jnp.where(up, 1, 0)
+        for at in range(3):
+            msg[systems + at] = shared[side, at]
+    for copy in copies[5:]:
         copy.wait()
 
 
 def edges_kernel(
-    src_in, fwd, adj, rhs, head_a, head_b, kxf, ky, kz, inv, msg_a, msg_b, src, xs, rs, sems
+    table_in, src_in, count, fwd, adj, rhs_in, label, cut, head_a, head_b,
+    msg_a, msg_b, x, rhs, kxf, ky, kz, dd, inv, sig, fac, weight,
+    table, src, lab, flag, sems,
 ):
     slots = fwd.shape[1]
     systems = 2 * slots
     planes, rows, lanes = ky.shape
     last = planes - 1
-    first, other = pl.ds(0, slots), pl.ds(slots, slots)
     copies = [
-        pltpu.make_async_copy(src_in, src, sems.at[0]),
-        pltpu.make_async_copy(fwd.at[0, :, pl.ds(1, 2)], xs.at[first, pl.ds(0, 2)], sems.at[1]),
-        pltpu.make_async_copy(adj.at[0, :, pl.ds(1, 2)], xs.at[other, pl.ds(0, 2)], sems.at[2]),
-        pltpu.make_async_copy(fwd.at[0, :, pl.ds(planes - 3, 2)], xs.at[first, pl.ds(2, 2)], sems.at[3]),
-        pltpu.make_async_copy(adj.at[0, :, pl.ds(planes - 3, 2)], xs.at[other, pl.ds(2, 2)], sems.at[4]),
-        pltpu.make_async_copy(rhs.at[0, :, pl.ds(0, 2)], rs.at[:, pl.ds(0, 2)], sems.at[5]),
-        pltpu.make_async_copy(rhs.at[0, :, pl.ds(planes - 2, 2)], rs.at[:, pl.ds(2, 2)], sems.at[6]),
+        pltpu.make_async_copy(table_in, table, sems.at[0]),
+        pltpu.make_async_copy(src_in, src, sems.at[1]),
+        pltpu.make_async_copy(label, lab, sems.at[2]),
+        pltpu.make_async_copy(cut, flag, sems.at[3]),
     ]
+    spans = (pl.ds(0, 3), pl.ds(planes - 3, 3), pl.ds(3, planes - 6))
+    for at, span in enumerate(spans):
+        for half, source in enumerate((fwd, adj)):
+            into = x.at[pl.ds(half * slots, slots), span]
+            copies.append(pltpu.make_async_copy(source.at[0, :, span], into, sems.at[4 + 3 * at + half]))
+        copies.append(pltpu.make_async_copy(rhs_in.at[0, :, span], rhs.at[:, span], sems.at[6 + 3 * at]))
     for copy in copies:
         copy.start()
-    for copy in copies:
+    slot = lax.broadcasted_iota(jnp.int32, weight.shape, 0)
+    weight[...] = jnp.where(slot < count[0], -1.0 / slots, 0.0).astype(F32)
+    for copy in copies[:4]:
+        copy.wait()
+
+    @pl.loop(0, planes)
+    def _(p):
+        value = conductivity(table, lab[p])
+        factor = cut_factor(flag[p])
+        sig[p] = value
+        fac[p] = factor
+        face_y, face_z = lateral_faces(value, factor, harmonic)
+        ky[p] = face_y
+        kz[p] = face_z
+
+    kxf[0] = jnp.zeros((rows, lanes), F32)
+    kxf[planes] = jnp.zeros((rows, lanes), F32)
+
+    @pl.loop(1, planes)
+    def _(p):
+        kxf[p] = harmonic(sig[p - 1], sig[p]) * fac[p - 1]
+
+    @pl.loop(0, planes)
+    def _(p):
+        face_y, face_z = ky[p], kz[p]
+        diag = MASS * sig[p] + kxf[p] + kxf[p + 1] + face_y + prev_y(face_y) + face_z + prev_z(face_z)
+        dd[p] = diag
+        inv[p] = 1.0 / diag
+
+    for copy in copies[4:10]:
         copy.wait()
     core = lax.rem(lax.axis_index("grp"), 2)
     half = slots // 2
-    for head, msg, up in ((head_a, msg_a, core == 0), (head_b, msg_b, core == 1)):
-        edge, inner = jnp.where(up, last, 0), jnp.where(up, last - 1, 1)
-        at_inner, at_next = jnp.where(up, 3, 0), jnp.where(up, 2, 1)
-        rs_edge, rs_inner = jnp.where(up, 3, 0), jnp.where(up, 2, 1)
+    for msg, up in ((msg_a, core == 0), (msg_b, core == 1)):
+        edge, inner, third = jnp.where(up, last, 0), jnp.where(up, last - 1, 1), jnp.where(up, last - 2, 2)
         face, face_next = jnp.where(up, last, 1), jnp.where(up, last - 1, 2)
         lead = jnp.where(up, half, 0)
 
         def partial(s, right):
-            msg[s] = right + lateral(head[s], ky[edge], kz[edge]) + kxf[face] * xs[s, at_inner]
+            msg[s] = right + lateral(x[s, edge], ky[edge], kz[edge]) + kxf[face] * x[s, inner]
 
         def onward(at, s, right):
-            x1 = xs[s, at_inner]
+            x1 = x[s, inner]
             total = right + lateral(x1, ky[inner], kz[inner])
-            total = total + kxf[face] * head[s] + kxf[face_next] * xs[s, at_next]
+            total = total + kxf[face] * x[s, edge] + kxf[face_next] * x[s, third]
             msg[systems + at] = kxf[face] * (inv[inner] * total - x1)
 
         @pl.loop(0, slots)
         def _(s):
             partial(s, plane_source(src, s, edge, (rows, lanes)))
-            partial(slots + s, rs[s, rs_edge])
+            partial(slots + s, rhs[s, edge])
 
         @pl.loop(0, half)
         def _(s):
             slot = lead + s
             onward(s, slot, plane_source(src, slot, inner, (rows, lanes)))
-            onward(half + s, slots + slot, rs[slot, rs_inner])
-
-
-def interior_kernel(src_in, fwd, adj, rhs, kxf, ky, kz, dd, inv, x, z, n, moments, extra, src, rs, sems):
-    slots = fwd.shape[1]
-    planes, rows, lanes = x.shape[1:]
+            onward(half + s, slots + slot, rhs[slot, inner])
+
+    for copy in copies[10:]:
+        copy.wait()
+
+
+def interior_kernel(src_in, x, rs, kxf, ky, kz, dd, inv, z, n, moments, extra, src, sem):
+    systems, planes, rows, lanes = x.shape
+    slots = systems // 2
     last = planes - 1
-    copies = [
-        pltpu.make_async_copy(fwd.at[0], x.at[pl.ds(0, slots)], sems.at[0]),
-        pltpu.make_async_copy(adj.at[0], x.at[pl.ds(slots, slots)], sems.at[1]),
-        pltpu.make_async_copy(rhs.at[0], rs, sems.at[2]),
-        pltpu.make_async_copy(src_in, src, sems.at[3]),
-    ]
-    for copy in copies:
-        copy.start()
-    for copy in copies:
-        copy.wait()
+    fetch = pltpu.make_async_copy(src_in, src, sem)
+    fetch.start()
+    fetch.wait()
 
     def one(s, right):
         for p in range(1, last):
@@ -356,13 +372,7 @@
     out[...] = jnp.broadcast_to(packed[None], out.shape)
 
 
-def correlate_kernel(
-    weight, parts, x, z, n, ext_x, ext_z, ext_n, far, extra, kxf, ky, kz, mass, keep, give, scale, total
-):
-    systems, planes, rows, lanes = z.shape
-    slots = systems // 2
-    half = slots // 2
-    last = planes - 1
+def steps_kernel(parts, scale):
     summed = parts[...].sum(0)
     lanes_at = lax.broadcasted_iota(jnp.int32, summed.shape, 1)
     c0, c1, c2, c3 = [
@@ -374,8 +384,17 @@
     first = rest + rz / c0
     curve = first * first * (c0 - c1) + 2.0 * first * alpha * (c1 - c2) + alpha * alpha * (c2 - c3)
     step = rz / curve
-    scale[0] = jnp.broadcast_to(alpha + step * first, (systems, lanes))
-    scale[1] = jnp.broadcast_to(step * alpha, (systems, lanes))
+    scale[0] = jnp.broadcast_to(alpha + step * first, scale.shape[1:])
+    scale[1] = jnp.broadcast_to(step * alpha, scale.shape[1:])
+
+
+def correlate_kernel(
+    weight, scale, x, z, n, ext_x, ext_z, ext_n, far, extra, kxf, ky, kz, sig, keep, give, total
+):
+    systems, planes, rows, lanes = z.shape
+    slots = systems // 2
+    half = slots // 2
+    last = planes - 1
 
     def slot_terms(s, fresh):
         ends = (s, slots + s)
@@ -405,7 +424,7 @@
             corr = face_x * (u_up - u) * (v_up - v)
             corr = corr + ky[p] * (next_y(u) - u) * (next_y(v) - v)
             corr = corr + kz[p] * (next_z(u) - u) * (next_z(v) - v)
-            corr = corr + mass[p] * u * v
+            corr = corr + (MASS * sig[p]) * u * v
             total[p] = share * corr if fresh else total[p] + share * corr
             u, v = u_up, v_up
 
@@ -456,7 +475,7 @@
     plane_set = held(planes, rows, lanes)
     head = held(systems + 3, rows, lanes)
     message = held(systems + 2 * half, rows, lanes)
-    HEAD, EDGES, INTERIOR, NEAR = 20, 20, 1, 10000
+    HEAD, EDGES, INTERIOR, NEAR, STEPS = 20, 20, 1, 10000, 1
 
     def cost(scale):
         return pl.CostEstimate(flops=scale * cells, bytes_accessed=scale * cells, transcendentals=0)
@@ -469,69 +488,63 @@
             pairs += [(g * tiles + t, g * tiles + t + by) for t in range(tiles) if 0 <= t + by < tiles]
         return lax.ppermute(value, ("grp", "tile"), pairs)
 
-    head_a, head_b, kxf, ky, kz, dd, inv, mass, weight = pl.pallas_call(
+    head_a, head_b = pl.pallas_call(
         head_kernel,
+        out_shape=[head, head],
+        in_specs=[IN_HBM] * 5,
+        out_specs=[IN_VMEM] * 2,
+        scratch_shapes=[
+            pltpu.SMEM(region_sigma.shape, F32),
+            VMEM((4, rows, lanes), jnp.int32),
+            VMEM((4, rows, lanes), jnp.int32),
+            VMEM((2, 3, rows, lanes), F32),
+            pltpu.SemaphoreType.DMA((9,)),
+        ],
+        compiler_params=params(),
+        cost_estimate=cost(HEAD),
+        name="head",
+    )(*in_hbm(region_sigma, fwd_start, adj_start, region_label, cut_flag))
+    near_a = opposite(head_a, 0)
+    near_b = opposite(head_b, 1)
+
+    msg_a, msg_b, x, rhs, kxf, ky, kz, dd, inv, sig, fac, weight = pl.pallas_call(
+        edges_kernel,
         out_shape=[
-            head, head,
+            message, message, field, held(slots, planes, rows, lanes),
             held(planes + 1, rows, lanes),
-            plane_set, plane_set, plane_set, plane_set, plane_set,
+            plane_set, plane_set, plane_set, plane_set, plane_set, plane_set,
             held(8, lanes),
         ],
-        in_specs=[IN_HBM, IN_SMEM] + [IN_HBM] * 4,
-        out_specs=[IN_VMEM] * 9,
+        in_specs=[IN_HBM] * 2 + [IN_SMEM] + [IN_HBM] * 5 + [IN_VMEM] * 2,
+        out_specs=[IN_VMEM] * 12,
         scratch_shapes=[
             pltpu.SMEM(region_sigma.shape, F32),
+            pltpu.SMEM(src_cell.shape, jnp.int32),
             VMEM((planes, rows, lanes), jnp.int32),
             VMEM((planes, rows, lanes), jnp.int32),
-            VMEM((planes, rows, lanes), F32),
-            VMEM((planes, rows, lanes), F32),
-            pltpu.SemaphoreType.DMA((7,)),
-        ],
-        compiler_params=params(),
-        cost_estimate=cost(HEAD),
-        name="head",
-    )(
-        *in_hbm(region_sigma), group_count,
-        *in_hbm(fwd_start, adj_start, region_label, cut_flag),
-    )
-    near_a = opposite(head_a, 0)
-    near_b = opposite(head_b, 1)
-
-    msg_a, msg_b = pl.pallas_call(
-        edges_kernel,
-        out_shape=[message, message],
-        in_specs=[IN_HBM] * 4 + [IN_VMEM] * 6,
-        out_specs=[IN_VMEM] * 2,
-        scratch_shapes=[
-            pltpu.SMEM(src_cell.shape, jnp.int32),
-            VMEM((systems, 4, rows, lanes), F32),
-            VMEM((slots, 4, rows, lanes), F32),
-            pltpu.SemaphoreType.DMA((7,)),
+            pltpu.SemaphoreType.DMA((13,)),
         ],
         compiler_params=params(),
         cost_estimate=cost(EDGES),
         name="edges",
     )(
-        *in_hbm(src_cell, fwd_start, adj_start, adj_rhs),
-        *pinned(head_a, head_b, kxf, ky, kz, inv),
+        *in_hbm(region_sigma, src_cell), group_count,
+        *in_hbm(fwd_start, adj_start, adj_rhs, region_label, cut_flag),
+        *pinned(head_a, head_b),
     )
     got_a = opposite(msg_a, 0)
     got_b = opposite(msg_b, 1)
 
-    x, z, n, moments, extra = pl.pallas_call(
+    z, n, moments, extra = pl.pallas_call(
         interior_kernel,
-        out_shape=[field, field, field, held(systems, 4, 8, 128), held(2 * half, rows, lanes)],
-        in_specs=[IN_HBM] * 4 + [IN_VMEM] * 5,
-        out_specs=[IN_VMEM] * 5,
-        scratch_shapes=[
-            pltpu.SMEM(src_cell.shape, jnp.int32),
-            VMEM((slots, planes, rows, lanes), F32),
-            pltpu.SemaphoreType.DMA((4,)),
-        ],
+        out_shape=[field, field, held(systems, 4, 8, 128), held(2 * half, rows, lanes)],
+        in_specs=[IN_HBM] + [IN_VMEM] * 7,
+        out_specs=[IN_VMEM] * 4,
+        scratch_shapes=[pltpu.SMEM(src_cell.shape, jnp.int32), pltpu.SemaphoreType.DMA],
         compiler_params=params(),
         cost_estimate=cost(INTERIOR),
         name="interior",
-    )(*in_hbm(src_cell, fwd_start, adj_start, adj_rhs), *pinned(kxf, ky, kz, dd, inv))
+    )(*in_hbm(src_cell), *pinned(x, rhs, kxf, ky, kz, dd, inv))
 
     pair_of = held(2, systems, rows, lanes)
     z, n, part, ext_x, far, moments = pl.pallas_call(
@@ -546,6 +559,9 @@
         name="near",
     )(*pinned(near_a, near_b, head_a, head_b, msg_a, msg_b, kxf, ky, kz, dd, inv, z, n, moments))
 
+    moments, extra = lax.optimization_barrier((moments, extra))
+    late = lax.ppermute(extra, "tile", [(i + 1, i) for i in range(tiles - 1)])
+
     n, ext_z, ext_n, moments = pl.pallas_call(
         boundary_kernel,
         out_shape=[field, pair_of, pair_of, held(tiles, systems, 128)],
@@ -557,21 +573,28 @@
         name="boundary",
     )(*pinned(got_a, got_b, head_a, head_b, kxf, ky, kz, far, ext_x, part, z, n, moments))
 
-    moments, extra = lax.optimization_barrier((moments, extra))
-    late = lax.ppermute(extra, "tile", [(i + 1, i) for i in range(tiles - 1)])
     parts = lax.all_to_all(moments, "tile", 0, 0)
 
     blocks = held(groups // 2, planes, rows // groups, lanes)
     block = held(planes, rows // groups, lanes)
+    scale = pl.pallas_call(
+        steps_kernel,
+        out_shape=held(2, systems, lanes),
+        in_specs=[IN_VMEM],
+        out_specs=IN_VMEM,
+        compiler_params=params(),
+        cost_estimate=cost(STEPS),
+        name="steps",
+    )(*pinned(parts))
     keep, give = pl.pallas_call(
         correlate_kernel,
         out_shape=[blocks, blocks],
         in_specs=[IN_VMEM] * 14,
         out_specs=[IN_VMEM] * 2,
-        scratch_shapes=[VMEM((2, systems, lanes), F32), VMEM((planes, rows, lanes), F32)],
+        scratch_shapes=[VMEM((planes, rows, lanes), F32)],
         compiler_params=params(),
         name="correlate",
-    )(*pinned(weight, parts, x, z, n, ext_x, ext_z, ext_n, far, late, kxf, ky, kz, mass))
+    )(*pinned(weight, scale, x, z, n, ext_x, ext_z, ext_n, far, late, kxf, ky, kz, sig))
 
     def swapped(value, by):
         return lax.ppermute(value, "grp", [(g, g ^ by) for g in range(groups)])

time: 84.6 us -> 78.8 us (0.931)
  Pallas kernels: 26.4 us -> 24.2 us
  waiting for transfers between devices: 14.7 us -> 13 us
  blocking collectives: 23.4 us -> 21.8 us
    ppermute x4, waiting for transfers between devices: 9.28 us -> 7.57 us  [opposite(): return lax.ppermute(value, ('grp', 'tile'), pairs)]
    all_to_all x1, blocking collectives: 23.4 us -> 21.8 us  [local(): parts = lax.all_to_all(moments, 'tile', 0, 0)]
    pallas_call x3 -> x4, Pallas kernels: 18.1 us -> 16.5 us  [the longest x1 9.08 us: local(): pl.pallas_call(interior_kernel, out_shape=[field, field, held(systems, 4,...]
  transfers between devices with their start and end apart: 9 -> 9, of which waited for: 5 -> 5; matrix products, arithmetic and copies ran while one was open for 0% -> 0% of each run, Pallas kernels for 21% -> 24%
where the time goes in v3:
time: 78.8 us; the launch traced here: 78.5 us
  Pallas kernels  24.2 us (31%)
  blocking collectives  21.8 us (28%)
  starting transfers between devices  18.7 us (24%)
  waiting for transfers between devices  13 us (16%)
    all_to_all x1, blocking collectives, local(): parts = lax.all_to_all(moments, 'tile', 0, 0)  21.8 us
    ppermute x4, starting transfers between devices, opposite(): return lax.ppermute(value, ('grp', 'tile'), pairs)  11.3 us
    pallas_call x1, Pallas kernels, local(): pl.pallas_call(interior_kernel, out_shape=[field, field, held(systems, 4,...  9.08 us
    ppermute x4, waiting for transfers between devices, opposite(): return lax.ppermute(value, ('grp', 'tile'), pairs)  7.57 us
    ppermute x4, starting transfers between devices, swapped(): return lax.ppermute(value, 'grp', [(g, g ^ by) for g in range(groups)])  6.07 us
    pallas_call x1, Pallas kernels, local(): pl.pallas_call(edges_kernel, out_shape=[message, message, field, held(slo...  5.79 us
    ppermute x4, waiting for transfers between devices, swapped(): return lax.ppermute(value, 'grp', [(g, g ^ by) for g in range(groups)])  5.42 us
    pallas_call x1, Pallas kernels, local(): pl.pallas_call(correlate_kernel, out_shape=[blocks, blocks], in_specs=[IN...  3.05 us
  transfers between devices with their start and end apart: 9, of which 5 were waited for; matrix products, arithmetic and copies ran while one was open for 0% of the time, Pallas kernels for 24%

profile of v3, /device:TPU:1, one launch (start us, length us, event | category | flops | bytes accessed | tf_op | source)
XLA Modules:
  0.0 78.5 jit_solution(5131097332375344188)
XLA Ops:
  0.0 1.5 %head.1 = (f32[11,64,256]{2,1,0:T(8,128)S(1)}, f32[11,64,256]{2,1,0:T(8,128)S(1)}) custom-call(f32[8]{0:T(128)} %table_in.3, f32[1,4,8,64,256]{4,3,2,1,0:T(8,128)} %fwd.3, f32[1,4,8,64,256]{4,3,2,1,0:T(8,128)} %adj.3, s32[8,64,256]{2,1,0:T(8,128)} %label.3, s32[8,64,256]{2,1,0:T(8,128)} %cut.3), custom_call_target="tpu_custom_call" | custom-call | flops 2621440 | bytes 2621440 | tf_op jit(solution)/shard_map/head/pallas_call | solution.py:491
  1.5 1.3 %collective-permute-start.2 = (f32[11,64,256]{2,1,0:T(8,128)S(1)}, f32[11,64,256]{2,1,0:T(8,128)S(1)}, u32[]{:S(2)}, u32[]{:S(2)}) collective-permute-start(f32[11,64,256]{2,1,0:T(8,128)S(1)} %get-tuple-element.40.head_a), channel_id=1, source_target_pairs={{0,1},{1,2},{2,3},{3,4},{4,5},{5,6},{6,7},{7,8},{8,9},{9,10},{10,1... | collective-permute-start | bytes 2162696 | tf_op jit(solution)/shard_map/ppermute | solution.py:489
  2.8 4.7 %collective-permute-start.3 = (f32[11,64,256]{2,1,0:T(8,128)S(1)}, f32[11,64,256]{2,1,0:T(8,128)S(1)}, u32[]{:S(2)}, u32[]{:S(2)}) collective-permute-start(f32[11,64,256]{2,1,0:T(8,128)S(1)} %get-tuple-element.41.head_b), channel_id=1, source_target_pairs={{1,0},{2,1},{3,2},{4,3},{5,4},{6,5},{7,6},{8,7},{9,8},{10,9},{11,1... | collective-permute-start | bytes 2162696 | tf_op jit(solution)/shard_map/ppermute | solution.py:489
  8.2 5.8 %edges.1 = (f32[12,64,256]{2,1,0:T(8,128)S(1)}, f32[12,64,256]{2,1,0:T(8,128)S(1)}, f32[8,8,64,256]{3,2,1,0:T(8,128)S(1)}, f32[4,8,64,256]{3,2,1,0:T(8,128)S(1)}...) custom-call(f32[8]{0:T(128)} %table_in.3, ...), custom_call_target="tpu_custom_call" | custom-call | flops 2621440 | bytes 2621440 | tf_op jit(solution)/shard_map/edges/pallas_call | solution.py:510
  14.0 1.3 %collective-permute-start = (f32[12,64,256]{2,1,0:T(8,128)S(1)}, f32[12,64,256]{2,1,0:T(8,128)S(1)}, u32[]{:S(2)}, u32[]{:S(2)}) collective-permute-start(f32[12,64,256]{2,1,0:T(8,128)S(1)} %get-tuple-element.43.msg_a), channel_id=1, source_target_pairs={{0,1},{1,2},{2,3},{3,4},{4,5},{5,6},{6,7},{7,8},{8,9},{9,10},{10,1... | collective-permute-start | bytes 2359304 | tf_op jit(solution)/shard_map/ppermute | solution.py:489
  15.3 4.0 %collective-permute-start.1 = (f32[12,64,256]{2,1,0:T(8,128)S(1)}, f32[12,64,256]{2,1,0:T(8,128)S(1)}, u32[]{:S(2)}, u32[]{:S(2)}) collective-permute-start(f32[12,64,256]{2,1,0:T(8,128)S(1)} %get-tuple-element.44.msg_b), channel_id=1, source_target_pairs={{1,0},{2,1},{3,2},{4,3},{5,4},{6,5},{7,6},{8,7},{9,8},{10,9},{11,1... | collective-permute-start | bytes 2359304 | tf_op jit(solution)/shard_map/ppermute | solution.py:489
  19.3 9.1 %interior.1 = (f32[8,8,64,256]{3,2,1,0:T(8,128)S(1)}, f32[8,8,64,256]{3,2,1,0:T(8,128)S(1)}, f32[8,4,8,128]{3,2,1,0:T(8,128)S(1)}, f32[4,64,256]{2,1,0:T(8,128)S(1)}) custom-call(s32[1,4]{1,0:T(1,128)} %src_in.3, f32[8,8,64,256]{3,2,1,0:T(8,128)S(1)} %get-tuple-element.50.x, f32[4,8,64,256]{3,2,1,0:T(8,128)S(1)} %get-tuple-element.51.rs, ...), custom_call_target="tpu_custom_call" | custom-call | flops 131072 | bytes 131072 | tf_op jit(solution)/shard_map/interior/pallas_call | solution.py:538
  28.4 0.0 collective-permute-done.2.got_a
  28.4 0.0 collective-permute-done.3.got_b
  28.4 2.2 %near.1 = (f32[8,8,64,256]{3,2,1,0:T(8,128)S(1)}, f32[8,8,64,256]{3,2,1,0:T(8,128)S(1)}, f32[2,8,64,256]{3,2,1,0:T(8,128)S(1)}, f32[2,8,64,256]{3,2,1,0:T(8,128)...) custom-call(f32[11,64,256]{2,1,0:T(8,128)S(1)} %collective-permute-d, ...), custom_call_target="tpu_custom_call", output_to_operand_aliasing={{0}: (11, {}), {1}: (12, {})} | custom-call | flops 1310720000 | bytes 1310720000 | tf_op jit(solution)/shard_map/near/pallas_call | solution.py:550
  30.6 1.3 %collective-permute-start.4 = (f32[4,64,256]{2,1,0:T(8,128)S(1)}, f32[4,64,256]{2,1,0:T(8,128)S(1)}, u32[]{:S(2)}, u32[]{:S(2)}) collective-permute-start(f32[4,64,256]{2,1,0:T(8,128)S(1)} %get-tuple-element.67), channel_id=1, source_target_pairs={{1,0},{2,1},{3,2},{4,3},{5,4},{6,5},{7,6},{8,7},{9,8},{10,9},{11,1... | collective-permute-start | bytes 786440 | tf_op jit(solution)/shard_map/ppermute | solution.py:563
  31.9 3.6 %collective-permute-done.got_a = f32[12,64,256]{2,1,0:T(8,128)S(1)} collective-permute-done((f32[12,64,256]{2,1,0:T(8,128)S(1)}, f32[12,64,256]{2,1,0:T(8,128)S(1)}, u32[]{:S(2)}, u32[]{:S(2)}) %collective-permute-start) | collective-permute-done | bytes 786464 | tf_op jit(solution)/shard_map/ppermute | solution.py:489
  35.5 4.0 %collective-permute-done.1.got_b = f32[12,64,256]{2,1,0:T(8,128)S(1)} collective-permute-done((f32[12,64,256]{2,1,0:T(8,128)S(1)}, f32[12,64,256]{2,1,0:T(8,128)S(1)}, u32[]{:S(2)}, u32[]{:S(2)}) %collective-permute-start.1) | collective-permute-done | bytes 786464 | tf_op jit(solution)/shard_map/ppermute | solution.py:489
  39.5 1.8 %boundary.1 = (f32[8,8,64,256]{3,2,1,0:T(8,128)S(1)}, f32[2,8,64,256]{3,2,1,0:T(8,128)S(1)}, f32[2,8,64,256]{3,2,1,0:T(8,128)S(1)}, f32[32,8,128]{2,1,0:T(8,128)S(1)}) custom-call(f32[12,64,256]{2,1,0:T(8,128)S(1)} %collective-permute-done.got_a, f32[12,64,256]{2,1,0:T(8,128)S(1)} %collective-permute-done.1.got_b, ...), custom_call_target="tpu_custom_call", output_to_operand_aliasing={{0}: (11, {})} | custom-call | tf_op jit(solution)/shard_map/boundary/pallas_call | solution.py:565
  41.3 21.8 %all_to_all.5.parts = f32[32,8,128]{2,1,0:T(8,128)S(1)} all-to-all(f32[32,8,128]{2,1,0:T(8,128)S(1)} %get-tuple-element.63), channel_id=1, replica_groups=mesh['grp'=8,'tile'=32] {'tile'}, dimensions={0} | all-to-all | bytes 262144 | tf_op jit(solution)/shard_map/all_to_all | solution.py:576
  63.1 0.1 steps.1.scale
  63.2 0.0 collective-permute-done.4.extra
  63.3 3.1 %correlate.1 = (f32[4,8,8,256]{3,2,1,0:T(8,128)S(1)}, f32[4,8,8,256]{3,2,1,0:T(8,128)S(1)}) custom-call(f32[8,256]{1,0:T(8,128)S(1)} %get-tuple-element.42.weight, f32[2,8,256]{2,1,0:T(8,128)S(1)} %steps.1.scale, f32[8,8,64,256]{3,2,1,0:T(8,128)S(1)} %get-tuple-element.50.x, f32[8,8,64,256]{3,2,1,0:T(8,128)S(1)} %get-tuple-element.58.z, ...), custom_call_target="tpu_custom_call" | custom-call | tf_op jit(solution)/shard_map/correlate/pallas_call | solution.py:589
  66.3 2.1 %collective-permute-start.5 = (f32[4,8,8,256]{3,2,1,0:T(8,128)S(1)}, f32[4,8,8,256]{3,2,1,0:T(8,128)S(1)}, u32[]{:S(2)}, u32[]{:S(2)}) collective-permute-start(f32[4,8,8,256]{3,2,1,0:T(8,128)S(1)} %get-tuple-element.70), channel_id=1, source_target_pairs={{0,32},{32,0},{64,96},{96,64},{128,160},{160,128},{192,224},{224,1... | collective-permute-start | bytes 786440 | tf_op jit(solution)/shard_map/ppermute | solution.py:600
  68.4 1.2 %collective-permute-done.5.got = f32[4,8,8,256]{3,2,1,0:T(8,128)S(1)} collective-permute-done((f32[4,8,8,256]{3,2,1,0:T(8,128)S(1)}, f32[4,8,8,256]{3,2,1,0:T(8,128)S(1)}, u32[]{:S(2)}, u32[]{:S(2)}) %collective-permute-start.5) | collective-permute-done | bytes 262176 | tf_op jit(solution)/shard_map/ppermute | solution.py:600
  69.6 1.3 %collective-permute-start.6 = (f32[8,8,256]{2,1,0:T(8,128)S(1)}, f32[8,8,256]{2,1,0:T(8,128)S(1)}, u32[]{:S(2)}, u32[]{:S(2)}) collective-permute-start(f32[8,8,256]{2,1,0:T(8,128)S(1)} %get-tuple-element.72), channel_id=1, source_target_pairs={{0,64},{32,96},{64,0},{96,32},{128,192},{160,224},{192,128},{224,1... | collective-permute-start | bytes 196616 | tf_op jit(solution)/shard_map/ppermute | solution.py:600
  70.9 2.5 %collective-permute-start.7 = (f32[8,8,256]{2,1,0:T(8,128)S(1)}, f32[8,8,256]{2,1,0:T(8,128)S(1)}, u32[]{:S(2)}, u32[]{:S(2)}) collective-permute-start(f32[8,8,256]{2,1,0:T(8,128)S(1)} %get-tuple-element.73), channel_id=1, source_target_pairs={{0,128},{32,160},{64,192},{96,224},{128,0},{160,32},{192,64},{224,... | collective-permute-start | bytes 196616 | tf_op jit(solution)/shard_map/ppermute | solution.py:600
  73.4 0.2 collective-permute-start.8
  73.6 0.0 collective-permute-done.6.one
  73.6 2.7 %collective-permute-done.7.two = f32[8,8,256]{2,1,0:T(8,128)S(1)} collective-permute-done((f32[8,8,256]{2,1,0:T(8,128)S(1)}, f32[8,8,256]{2,1,0:T(8,128)S(1)}, u32[]{:S(2)}, u32[]{:S(2)}) %collective-permute-start.7) | collective-permute-done | bytes 65568 | tf_op jit(solution)/shard_map/ppermute | solution.py:600
  76.3 1.5 %collective-permute-done.8.three = f32[8,8,256]{2,1,0:T(8,128)S(1)} collective-permute-done((f32[8,8,256]{2,1,0:T(8,128)S(1)}, f32[8,8,256]{2,1,0:T(8,128)S(1)}, u32[]{:S(2)}, u32[]{:S(2)}) %collective-permute-start.8) | collective-permute-done | bytes 65568 | tf_op jit(solution)/shard_map/ppermute | solution.py:600
  77.8 0.6 total.1
  (1 shorter events, 0.0 us)
Async XLA Ops:
  1.5 26.9 %collective-permute-start.2 = (f32[11,64,256]{2,1,0:T(8,128)S(1)}, f32[11,64,256]{2,1,0:T(8,128)S(1)}, u32[]{:S(2)}, u32[]{:S(2)}) collective-permute-start(f32[11,64,256]{2,1,0:T(8,128)S(1)} %get-tuple-element.40.head_a), channel_id=1, source_target_pairs={{0,1},{1,2},{2,3},{3,4},{4,5},{5,6},{6,7},{7,8},{8,9},{9,10},{10,1... | collective-permute-start | bytes 2162696 | tf_op jit(solution)/shard_map/ppermute | solution.py:489
  2.8 25.6 %collective-permute-start.3 = (f32[11,64,256]{2,1,0:T(8,128)S(1)}, f32[11,64,256]{2,1,0:T(8,128)S(1)}, u32[]{:S(2)}, u32[]{:S(2)}) collective-permute-start(f32[11,64,256]{2,1,0:T(8,128)S(1)} %get-tuple-element.41.head_b), channel_id=1, source_target_pairs={{1,0},{2,1},{3,2},{4,3},{5,4},{6,5},{7,6},{8,7},{9,8},{10,9},{11,1... | collective-permute-start | bytes 2162696 | tf_op jit(solution)/shard_map/ppermute | solution.py:489
  14.0 21.5 %collective-permute-start = (f32[12,64,256]{2,1,0:T(8,128)S(1)}, f32[12,64,256]{2,1,0:T(8,128)S(1)}, u32[]{:S(2)}, u32[]{:S(2)}) collective-permute-start(f32[12,64,256]{2,1,0:T(8,128)S(1)} %get-tuple-element.43.msg_a), channel_id=1, source_target_pairs={{0,1},{1,2},{2,3},{3,4},{4,5},{5,6},{6,7},{7,8},{8,9},{9,10},{10,1... | collective-permute-start | bytes 2359304 | tf_op jit(solution)/shard_map/ppermute | solution.py:489
  15.3 24.2 %collective-permute-start.1 = (f32[12,64,256]{2,1,0:T(8,128)S(1)}, f32[12,64,256]{2,1,0:T(8,128)S(1)}, u32[]{:S(2)}, u32[]{:S(2)}) collective-permute-start(f32[12,64,256]{2,1,0:T(8,128)S(1)} %get-tuple-element.44.msg_b), channel_id=1, source_target_pairs={{1,0},{2,1},{3,2},{4,3},{5,4},{6,5},{7,6},{8,7},{9,8},{10,9},{11,1... | collective-permute-start | bytes 2359304 | tf_op jit(solution)/shard_map/ppermute | solution.py:489
  30.6 32.6 %collective-permute-start.4 = (f32[4,64,256]{2,1,0:T(8,128)S(1)}, f32[4,64,256]{2,1,0:T(8,128)S(1)}, u32[]{:S(2)}, u32[]{:S(2)}) collective-permute-start(f32[4,64,256]{2,1,0:T(8,128)S(1)} %get-tuple-element.67), channel_id=1, source_target_pairs={{1,0},{2,1},{3,2},{4,3},{5,4},{6,5},{7,6},{8,7},{9,8},{10,9},{11,1... | collective-permute-start | bytes 786440 | tf_op jit(solution)/shard_map/ppermute | solution.py:563
  66.3 3.3 %collective-permute-start.5 = (f32[4,8,8,256]{3,2,1,0:T(8,128)S(1)}, f32[4,8,8,256]{3,2,1,0:T(8,128)S(1)}, u32[]{:S(2)}, u32[]{:S(2)}) collective-permute-start(f32[4,8,8,256]{3,2,1,0:T(8,128)S(1)} %get-tuple-element.70), channel_id=1, source_target_pairs={{0,32},{32,0},{64,96},{96,64},{128,160},{160,128},{192,224},{224,1... | collective-permute-start | bytes 786440 | tf_op jit(solution)/shard_map/ppermute | solution.py:600
  69.6 3.9 %collective-permute-start.6 = (f32[8,8,256]{2,1,0:T(8,128)S(1)}, f32[8,8,256]{2,1,0:T(8,128)S(1)}, u32[]{:S(2)}, u32[]{:S(2)}) collective-permute-start(f32[8,8,256]{2,1,0:T(8,128)S(1)} %get-tuple-element.72), channel_id=1, source_target_pairs={{0,64},{32,96},{64,0},{96,32},{128,192},{160,224},{192,128},{224,1... | collective-permute-start | bytes 196616 | tf_op jit(solution)/shard_map/ppermute | solution.py:600
  70.9 5.4 %collective-permute-start.7 = (f32[8,8,256]{2,1,0:T(8,128)S(1)}, f32[8,8,256]{2,1,0:T(8,128)S(1)}, u32[]{:S(2)}, u32[]{:S(2)}) collective-permute-start(f32[8,8,256]{2,1,0:T(8,128)S(1)} %get-tuple-element.73), channel_id=1, source_target_pairs={{0,128},{32,160},{64,192},{96,224},{128,0},{160,32},{192,64},{224,... | collective-permute-start | bytes 196616 | tf_op jit(solution)/shard_map/ppermute | solution.py:600
  73.4 4.5 %collective-permute-start.8 = (f32[8,8,256]{2,1,0:T(8,128)S(1)}, f32[8,8,256]{2,1,0:T(8,128)S(1)}, u32[]{:S(2)}, u32[]{:S(2)}) collective-permute-start(f32[8,8,256]{2,1,0:T(8,128)S(1)} %get-tuple-element.74), channel_id=1, source_target_pairs={{0,192},{32,224},{64,128},{96,160},{128,64},{160,96},{192,0},{224,... | collective-permute-start | bytes 196616 | tf_op jit(solution)/shard_map/ppermute | solution.py:600

commit v4 on v3

--- a/solution.py
+++ b/solution.py
@@ -48,8 +48,10 @@
     return face_y, face_z
 
 
-def lateral(v, face_y, face_z):
-    return face_y * next_y(v) + prev_y(face_y * v) + face_z * next_z(v) + prev_z(face_z * v)
+def lateral(v, face_y, face_z, back_z):
+    flow_y = face_y * (next_y(v) - v)
+    along_z = face_z * (next_z(v) - v) + back_z * (prev_z(v) - v)
+    return (flow_y - prev_y(flow_y)) + along_z
 
 
 def upper_lateral(v, face_y, face_z):
@@ -115,11 +117,9 @@
     factor = [cut_factor(flag[at]) for at in range(4)]
     faces = [harmonic(sigma[at], sigma[at + 1]) * factor[at] for at in (0, 2)]
     for side, at in enumerate((0, 3)):
-        face_y, face_z = lateral_faces(sigma[at], factor[at], harmonic)
         shared[side, 0] = sigma[at]
         shared[side, 1] = factor[at]
-        diag = MASS * sigma[at] + faces[side] + face_y + prev_y(face_y) + face_z + prev_z(face_z)
-        shared[side, 2] = diag
+        shared[side, 2] = faces[side]
     for msg, up in edges:
         side = jnp.where(up, 1, 0)
         for at in range(3):
@@ -130,8 +130,8 @@
 
 def edges_kernel(
     table_in, src_in, count, fwd, adj, rhs_in, label, cut, head_a, head_b,
-    msg_a, msg_b, x, rhs, kxf, ky, kz, dd, inv, sig, fac, weight,
-    table, src, lab, flag, sems,
+    msg_a, msg_b, x, rhs, kxf, ky, kz, dd, inv, mass, kzb, weight,
+    table, src, lab, flag, sig, fac, sems,
 ):
     slots = fwd.shape[1]
     systems = 2 * slots
@@ -162,9 +162,11 @@
         factor = cut_factor(flag[p])
         sig[p] = value
         fac[p] = factor
+        mass[p] = MASS * value
         face_y, face_z = lateral_faces(value, factor, harmonic)
         ky[p] = face_y
         kz[p] = face_z
+        kzb[p] = prev_z(face_z)
 
     kxf[0] = jnp.zeros((rows, lanes), F32)
     kxf[planes] = jnp.zeros((rows, lanes), F32)
@@ -175,8 +177,8 @@
 
     @pl.loop(0, planes)
     def _(p):
-        face_y, face_z = ky[p], kz[p]
-        diag = MASS * sig[p] + kxf[p] + kxf[p + 1] + face_y + prev_y(face_y) + face_z + prev_z(face_z)
+        face_y = ky[p]
+        diag = mass[p] + kxf[p] + kxf[p + 1] + face_y + prev_y(face_y) + kz[p] + kzb[p]
         dd[p] = diag
         inv[p] = 1.0 / diag
 
@@ -190,13 +192,15 @@
         lead = jnp.where(up, half, 0)
 
         def partial(s, right):
-            msg[s] = right + lateral(x[s, edge], ky[edge], kz[edge]) + kxf[face] * x[s, inner]
+            x0 = x[s, edge]
+            total = right - mass[edge] * x0 + lateral(x0, ky[edge], kz[edge], kzb[edge])
+            msg[s] = total + kxf[face] * (x[s, inner] - x0)
 
         def onward(at, s, right):
             x1 = x[s, inner]
-            total = right + lateral(x1, ky[inner], kz[inner])
-            total = total + kxf[face] * x[s, edge] + kxf[face_next] * x[s, third]
-            msg[systems + at] = kxf[face] * (inv[inner] * total - x1)
+            total = right - mass[inner] * x1 + lateral(x1, ky[inner], kz[inner], kzb[inner])
+            total = total + kxf[face] * (x[s, edge] - x1) + kxf[face_next] * (x[s, third] - x1)
+            msg[systems + at] = inv[inner] * total
 
         @pl.loop(0, slots)
         def _(s):
@@ -213,7 +217,7 @@
         copy.wait()
 
 
-def interior_kernel(src_in, x, rs, kxf, ky, kz, dd, inv, z, n, moments, extra, src, sem):
+def interior_kernel(src_in, x, rs, kxf, ky, kz, mass, inv, kzb, z, n, moments, extra, src, sem):
     systems, planes, rows, lanes = x.shape
     slots = systems // 2
     last = planes - 1
@@ -222,20 +226,22 @@
     fetch.wait()
 
     def one(s, right):
+        zero = jnp.zeros((8, 128), F32)
+        c0, c1, c2, c3 = zero, zero, zero, zero
         for p in range(1, last):
-            total = right(p) + lateral(x[s, p], ky[p], kz[p])
-            total = total + kxf[p] * x[s, p - 1] + kxf[p + 1] * x[s, p + 1]
-            z[s, p] = inv[p] * total - x[s, p]
-        c0 = jnp.zeros((8, 128), F32)
-        c1, c2, c3 = c0, c0, c0
+            v = x[s, p]
+            total = right(p) - mass[p] * v + lateral(v, ky[p], kz[p], kzb[p])
+            total = total + kxf[p + 1] * (x[s, p + 1] - v) + kxf[p] * (x[s, p - 1] - v)
+            fresh = inv[p] * total
+            z[s, p] = fresh
+            c0 = c0 + folded(fresh * total)
         for p in range(1, last):
             v = z[s, p]
-            c0 = c0 + folded(dd[p] * v * v)
-            w = lateral(v, ky[p], kz[p])
+            w = mass[p] * v - lateral(v, ky[p], kz[p], kzb[p])
+            if p < last - 1:
+                w = w - kxf[p + 1] * (z[s, p + 1] - v)
             if p > 1:
-                w = w + kxf[p] * z[s, p - 1]
-            if p < last - 1:
-                w = w + kxf[p + 1] * z[s, p + 1]
+                w = w - kxf[p] * (z[s, p - 1] - v)
             if p == 1 or p == last - 1:
                 n[s, p] = w
                 continue
@@ -260,8 +266,8 @@
 
     half = slots // 2
     for at in range(half):
-        extra[at] = kxf[1] * z[half + at, 1]
-        extra[half + at] = kxf[1] * z[slots + half + at, 1]
+        extra[at] = z[half + at, 1]
+        extra[half + at] = z[slots + half + at, 1]
 
 
 def both_sides(planes, slots, pairs):
@@ -281,47 +287,57 @@
 
 
 def near_kernel(
-    got_a, got_b, head_a, head_b, msg_a, msg_b, kxf, ky, kz, dd, inv, z_in, n_in, moments_in,
+    got_a, got_b, head_a, head_b, msg_a, msg_b, kxf, ky, kz, dd, inv, z_in, n_in, moments_in, mass, kzb,
     z, n, part, ext_x, far, moments,
-    coef,
 ):
     systems, planes, rows, lanes = z.shape
     sides = both_sides(planes, systems // 2, ((got_a, head_b, msg_b), (got_b, head_a, msg_a)))
     for at, (got, head, _), low, side, edge, _, _, _, _, _ in sides:
-        cross = harmonic(got[systems], head[systems])
-        cross = cross * jnp.where(low, got[systems + 1], head[systems + 1])
-        here = dd[edge] + cross
-        there = got[systems + 2] + cross
+        sigma, factor, beyond = got[systems], got[systems + 1], got[systems + 2]
+        cross = harmonic(sigma, head[systems]) * jnp.where(low, factor, head[systems + 1])
+        face_y, face_z = lateral_faces(sigma, factor, harmonic_or_zero)
+        there = MASS * sigma + beyond + cross
+        back_z = prev_z(face_z)
+        there = there + face_y + prev_y(face_y) + face_z + back_z
         real = there > 0.0
-        coef[at] = here
         far[side, 0] = cross
         far[side, 1] = jnp.where(real, 1.0 / jnp.where(real, there, 1.0), 0.0)
-        face_y, face_z = lateral_faces(got[systems], got[systems + 1], harmonic_or_zero)
         far[side, 2] = face_y
         far[side, 3] = face_z
-        far[side, 4] = 1.0 / here
+        far[side, 4] = 1.0 / (dd[edge] + cross)
+        far[side, 5] = MASS * sigma
+        far[side, 6] = beyond
+        far[side, 7] = back_z
 
     @pl.loop(0, systems)
     def _(s):
         c0, c1, c2, c3 = [moments_in[s, at] for at in range(4)]
         for at, (got, head, msg), _, side, edge, inner, third, face, face_next, _ in sides:
             xm = got[s]
-            z0 = far[side, 4] * (msg[s] + far[side, 0] * xm) - head[s]
+            total = msg[s] + far[side, 0] * (xm - head[s])
+            z0 = far[side, 4] * total
             z1 = z_in[s, inner]
-            w0 = lateral(z0, ky[edge], kz[edge]) + kxf[face] * z1
-            w1 = n_in[s, inner] + kxf[face] * z0
+            flow = kxf[face] * (z1 - z0)
+            w0 = mass[edge] * z0 - lateral(z0, ky[edge], kz[edge], kzb[edge]) - flow
+            w1 = n_in[s, inner] + flow
             n1 = inv[inner] * w1
             z[s, edge] = z0
             n[s, inner] = n1
             part[side, s] = w0
             ext_x[side, s] = xm
-            c0 = c0 + folded(coef[at] * z0 * z0)
+            c0 = c0 + folded(total * z0)
             c1 = c1 + folded(z0 * w0 + z1 * w1)
             c2 = c2 + folded(n1 * w1)
-            near1 = upper_lateral(n1, ky[inner], kz[inner]) + kxf[face_next] * n_in[s, third]
-            c3 = c3 + folded(n1 * near1)
+            near = upper_lateral(n1, ky[inner], kz[inner]) + kxf[face_next] * n_in[s, third]
+            c3 = c3 + folded(n1 * near)
         for at, c in enumerate((c0, c1, c2, c3)):
             moments[s, at] = c
+
+
+def outer_slope(v, beyond, edge, far, side):
+    w = far[side, 5] * v - lateral(v, far[side, 2], far[side, 3], far[side, 7])
+    w = w - far[side, 6] * (beyond - v) - far[side, 0] * (edge - v)
+    return far[side, 1] * w
 
 
 def boundary_kernel(
@@ -340,16 +356,16 @@
         for _, (got, head), _, side, edge, inner, _, face, _, _ in sides:
             cross = far[side, 0]
             z0 = z[s, edge]
-            zm = far[side, 1] * (got[s] + cross * head[s]) - ext_x[side, s]
-            over = cross * zm
-            w0 = part[side, s] + over
+            zm = far[side, 1] * (got[s] + cross * (head[s] - ext_x[side, s]))
+            over = cross * (zm - z0)
+            w0 = part[side, s] - over
             n0 = far[side, 4] * w0
             n[s, edge] = n0
             ext_z[side, s] = zm
-            c1 = c1 + folded(z0 * over)
+            c1 = c1 - folded(z0 * over)
             c2 = c2 + folded(n0 * w0)
-            near0 = upper_lateral(n0, ky[edge], kz[edge]) + kxf[face] * n_in[s, inner]
-            c3 = c3 + folded(n0 * near0)
+            near = upper_lateral(n0, ky[edge], kz[edge]) + kxf[face] * n_in[s, inner]
+            c3 = c3 + folded(n0 * near)
         for at, c in enumerate((c0, c1, c2, c3 + c3)):
             sums[at, pl.ds(s, 1)] = c.sum(0, keepdims=True)
 
@@ -357,12 +373,9 @@
     def _(at):
         for _, (got, _), _, side, edge, _, _, _, _, lead in sides:
             for place, s in ((at, lead + at), (half + at, slots + lead + at)):
-                cross = far[side, 0]
-                w = lateral(ext_z[side, s], far[side, 2], far[side, 3])
-                w = w + got[systems + place] + cross * z[s, edge]
-                nm = far[side, 1] * w
+                nm = outer_slope(ext_z[side, s], got[systems + place], z[s, edge], far, side)
                 ext_n[side, s] = nm
-                pair = folded(cross * nm * n[s, edge])
+                pair = folded(far[side, 0] * nm * n[s, edge])
                 sums[3, pl.ds(s, 1)] = sums[3, pl.ds(s, 1)] + 2.0 * pair.sum(0, keepdims=True)
 
     lanes_at = lax.broadcasted_iota(jnp.int32, (systems, 128), 1)
@@ -375,21 +388,23 @@
 def steps_kernel(parts, scale):
     summed = parts[...].sum(0)
     lanes_at = lax.broadcasted_iota(jnp.int32, summed.shape, 1)
-    c0, c1, c2, c3 = [
+    m0, m1, m2, c3 = [
         jnp.where(lanes_at == at, summed, 0.0).sum(1, keepdims=True) for at in range(4)
     ]
-    alpha = c0 / (c0 - c1)
-    rest = 1.0 - alpha
-    rz = rest * rest * c0 + 2.0 * alpha * rest * c1 + alpha * alpha * c2
-    first = rest + rz / c0
-    curve = first * first * (c0 - c1) + 2.0 * first * alpha * (c1 - c2) + alpha * alpha * (c2 - c3)
-    step = rz / curve
-    scale[0] = jnp.broadcast_to(alpha + step * first, scale.shape[1:])
-    scale[1] = jnp.broadcast_to(step * alpha, scale.shape[1:])
+    unit = 1.0 / m1
+    m0, m1, m2, c3 = m0 * unit, m1 * unit, m2 * unit, c3 * unit
+    alpha = m0 / m1
+    top = m0 * (m2 - m1) + m1 * (m0 - m1)
+    low = -m1 * c3 - m2 * (m2 - m1)
+    real = jnp.logical_and(top > 0.0, low > 0.0)
+    step = jnp.where(real, top * m1 / jnp.where(real, m0 * low, 1.0), 0.0)
+    grown = 1.0 + top / (m1 * m1)
+    scale[0] = jnp.broadcast_to(alpha + step * grown, scale.shape[1:])
+    scale[1] = jnp.broadcast_to(-step * alpha, scale.shape[1:])
 
 
 def correlate_kernel(
-    weight, scale, x, z, n, ext_x, ext_z, ext_n, far, extra, kxf, ky, kz, sig, keep, give, total
+    weight, scale, x, z, n, ext_x, ext_z, ext_n, far, extra, kxf, ky, kz, mass, keep, give, total
 ):
     systems, planes, rows, lanes = z.shape
     slots = systems // 2
@@ -412,8 +427,7 @@
                 if s < half:
                     nm = ext_n[1, e]
                 else:
-                    w = lateral(zm, far[1, 2], far[1, 3]) + extra[s - half + i * half]
-                    nm = far[1, 1] * (w + far[1, 0] * z[e, last])
+                    nm = outer_slope(zm, extra[s - half + i * half], z[e, last], far, 1)
                 found.append(ext_x[1, e] + on_z[i] * zm + on_n[i] * nm)
             return found
 
@@ -424,7 +438,7 @@
             corr = face_x * (u_up - u) * (v_up - v)
             corr = corr + ky[p] * (next_y(u) - u) * (next_y(v) - v)
             corr = corr + kz[p] * (next_z(u) - u) * (next_z(v) - v)
-            corr = corr + (MASS * sig[p]) * u * v
+            corr = corr + mass[p] * u * v
             total[p] = share * corr if fresh else total[p] + share * corr
             u, v = u_up, v_up
 
@@ -437,9 +451,9 @@
         give[at] = total[:, pl.ds(pl.multiple_of((2 * at + 1 - core) * deep, 8), deep)]
 
 
-def merge_kernel(keep, got, own, to_1, to_2, to_3):
+def merge_kernel(keep, got, own, to_2, to_1, to_3):
     mine = lax.div(lax.axis_index("grp"), 2)
-    for at, out in enumerate((own, to_1, to_2, to_3)):
+    for at, out in ((0, own), (1, to_1), (2, to_2), (3, to_3)):
         block = jnp.bitwise_xor(mine, at)
         out[...] = keep[block] + got[block]
 
@@ -507,7 +521,7 @@
     near_a = opposite(head_a, 0)
     near_b = opposite(head_b, 1)
 
-    msg_a, msg_b, x, rhs, kxf, ky, kz, dd, inv, sig, fac, weight = pl.pallas_call(
+    msg_a, msg_b, x, rhs, kxf, ky, kz, dd, inv, mass, kzb, weight = pl.pallas_call(
         edges_kernel,
         out_shape=[
             message, message, field, held(slots, planes, rows, lanes),
@@ -522,6 +536,8 @@
             pltpu.SMEM(src_cell.shape, jnp.int32),
             VMEM((planes, rows, lanes), jnp.int32),
             VMEM((planes, rows, lanes), jnp.int32),
+            VMEM((planes, rows, lanes), F32),
+            VMEM((planes, rows, lanes), F32),
             pltpu.SemaphoreType.DMA((13,)),
         ],
         compiler_params=params(),
@@ -538,26 +554,25 @@
     z, n, moments, extra = pl.pallas_call(
         interior_kernel,
         out_shape=[field, field, held(systems, 4, 8, 128), held(2 * half, rows, lanes)],
-        in_specs=[IN_HBM] + [IN_VMEM] * 7,
+        in_specs=[IN_HBM] + [IN_VMEM] * 8,
         out_specs=[IN_VMEM] * 4,
         scratch_shapes=[pltpu.SMEM(src_cell.shape, jnp.int32), pltpu.SemaphoreType.DMA],
         compiler_params=params(),
         cost_estimate=cost(INTERIOR),
         name="interior",
-    )(*in_hbm(src_cell), *pinned(x, rhs, kxf, ky, kz, dd, inv))
+    )(*in_hbm(src_cell), *pinned(x, rhs, kxf, ky, kz, mass, inv, kzb))
 
     pair_of = held(2, systems, rows, lanes)
     z, n, part, ext_x, far, moments = pl.pallas_call(
         near_kernel,
-        out_shape=[field, field, pair_of, pair_of, held(2, 5, rows, lanes), held(systems, 4, 8, 128)],
-        in_specs=[IN_VMEM] * 14,
+        out_shape=[field, field, pair_of, pair_of, held(2, 8, rows, lanes), held(systems, 4, 8, 128)],
+        in_specs=[IN_VMEM] * 16,
         out_specs=[IN_VMEM] * 6,
         input_output_aliases={11: 0, 12: 1},
-        scratch_shapes=[VMEM((2, rows, lanes), F32)],
         compiler_params=params(),
         cost_estimate=cost(NEAR),
         name="near",
-    )(*pinned(near_a, near_b, head_a, head_b, msg_a, msg_b, kxf, ky, kz, dd, inv, z, n, moments))
+    )(*pinned(near_a, near_b, head_a, head_b, msg_a, msg_b, kxf, ky, kz, dd, inv, z, n, moments, mass, kzb))
 
     moments, extra = lax.optimization_barrier((moments, extra))
     late = lax.ppermute(extra, "tile", [(i + 1, i) for i in range(tiles - 1)])
@@ -594,7 +609,7 @@
         scratch_shapes=[VMEM((planes, rows, lanes), F32)],
         compiler_params=params(),
         name="correlate",
-    )(*pinned(weight, scale, x, z, n, ext_x, ext_z, ext_n, far, late, kxf, ky, kz, sig))
+    )(*pinned(weight, scale, x, z, n, ext_x, ext_z, ext_n, far, late, kxf, ky, kz, mass))
 
     def swapped(value, by):
         return lax.ppermute(value, "grp", [(g, g ^ by) for g in range(groups)])
@@ -608,7 +623,7 @@
         compiler_params=params(),
         name="merge",
     )(*pinned(keep, got))
-    came = [swapped(value, 2 * (at + 1)) for at, value in enumerate(sent)]
+    came = [swapped(value, by) for value, by in zip(sent, (4, 2, 6))]
     return pl.pallas_call(
         total_kernel,
         out_shape=jax.ShapeDtypeStruct((planes, rows // groups, lanes), F32),

time: 78.8 us -> 78.3 us (level)
  Pallas kernels: 24.2 us -> 23.4 us
  transfers between devices with their start and end apart: 9 -> 9, of which waited for: 5 -> 6; matrix products, arithmetic and copies ran while one was open for 0% -> 0% of each run, Pallas kernels for 24% -> 24%
where the time goes in v4:
time: 78.3 us; the launch traced here: 78 us
  Pallas kernels  23.4 us (30%)
  blocking collectives  21.8 us (28%)
  starting transfers between devices  18.9 us (24%)
  waiting for transfers between devices  13.2 us (17%)
    all_to_all x1, blocking collectives, local(): parts = lax.all_to_all(moments, 'tile', 0, 0)  21.8 us
    ppermute x4, starting transfers between devices, opposite(): return lax.ppermute(value, ('grp', 'tile'), pairs)  11.3 us
    pallas_call x1, Pallas kernels, local(): pl.pallas_call(interior_kernel, out_shape=[field, field, held(systems, 4,...  8.94 us
    ppermute x4, waiting for transfers between devices, opposite(): return lax.ppermute(value, ('grp', 'tile'), pairs)  8.23 us
    ppermute x4, starting transfers between devices, swapped(): return lax.ppermute(value, 'grp', [(g, g ^ by) for g in range(groups)])  6.3 us
    pallas_call x1, Pallas kernels, local(): pl.pallas_call(edges_kernel, out_shape=[message, message, field, held(slo...  5.22 us
    ppermute x4, waiting for transfers between devices, swapped(): return lax.ppermute(value, 'grp', [(g, g ^ by) for g in range(groups)])  4.94 us
    pallas_call x1, Pallas kernels, local(): pl.pallas_call(correlate_kernel, out_shape=[blocks, blocks], in_specs=[IN...  2.82 us
  transfers between devices with their start and end apart: 9, of which 6 were waited for; matrix products, arithmetic and copies ran while one was open for 0% of the time, Pallas kernels for 24%

profile of v4, /device:TPU:1, one launch (start us, length us, event | category | flops | bytes accessed | tf_op | source)
XLA Modules:
  0.0 78.0 jit_solution(15254498623833680740)
XLA Ops:
  0.0 1.5 %head.1 = (f32[11,64,256]{2,1,0:T(8,128)S(1)}, f32[11,64,256]{2,1,0:T(8,128)S(1)}) custom-call(f32[8]{0:T(128)} %table_in.3, f32[1,4,8,64,256]{4,3,2,1,0:T(8,128)} %fwd.3, f32[1,4,8,64,256]{4,3,2,1,0:T(8,128)} %adj.3, s32[8,64,256]{2,1,0:T(8,128)} %label.3, s32[8,64,256]{2,1,0:T(8,128)} %cut.3), custom_call_target="tpu_custom_call" | custom-call | flops 2621440 | bytes 2621440 | tf_op jit(solution)/shard_map/head/pallas_call | solution.py:505
  1.5 1.3 %collective-permute-start.2 = (f32[11,64,256]{2,1,0:T(8,128)S(1)}, f32[11,64,256]{2,1,0:T(8,128)S(1)}, u32[]{:S(2)}, u32[]{:S(2)}) collective-permute-start(f32[11,64,256]{2,1,0:T(8,128)S(1)} %get-tuple-element.41.head_a), channel_id=1, source_target_pairs={{0,1},{1,2},{2,3},{3,4},{4,5},{5,6},{6,7},{7,8},{8,9},{9,10},{10,1... | collective-permute-start | bytes 2162696 | tf_op jit(solution)/shard_map/ppermute | solution.py:503
  2.8 4.7 %collective-permute-start.3 = (f32[11,64,256]{2,1,0:T(8,128)S(1)}, f32[11,64,256]{2,1,0:T(8,128)S(1)}, u32[]{:S(2)}, u32[]{:S(2)}) collective-permute-start(f32[11,64,256]{2,1,0:T(8,128)S(1)} %get-tuple-element.42.head_b), channel_id=1, source_target_pairs={{1,0},{2,1},{3,2},{4,3},{5,4},{6,5},{7,6},{8,7},{9,8},{10,9},{11,1... | collective-permute-start | bytes 2162696 | tf_op jit(solution)/shard_map/ppermute | solution.py:503
  8.2 5.2 %edges.1 = (f32[12,64,256]{2,1,0:T(8,128)S(1)}, f32[12,64,256]{2,1,0:T(8,128)S(1)}, f32[8,8,64,256]{3,2,1,0:T(8,128)S(1)}, f32[4,8,64,256]{3,2,1,0:T(8,128)S(1)}...) custom-call(f32[8]{0:T(128)} %table_in.3, ...), custom_call_target="tpu_custom_call" | custom-call | flops 2621440 | bytes 2621440 | tf_op jit(solution)/shard_map/edges/pallas_call | solution.py:524
  13.4 1.3 %collective-permute-start = (f32[12,64,256]{2,1,0:T(8,128)S(1)}, f32[12,64,256]{2,1,0:T(8,128)S(1)}, u32[]{:S(2)}, u32[]{:S(2)}) collective-permute-start(f32[12,64,256]{2,1,0:T(8,128)S(1)} %get-tuple-element.44.msg_a), channel_id=1, source_target_pairs={{0,1},{1,2},{2,3},{3,4},{4,5},{5,6},{6,7},{7,8},{8,9},{9,10},{10,1... | collective-permute-start | bytes 2359304 | tf_op jit(solution)/shard_map/ppermute | solution.py:503
  14.7 4.0 %collective-permute-start.1 = (f32[12,64,256]{2,1,0:T(8,128)S(1)}, f32[12,64,256]{2,1,0:T(8,128)S(1)}, u32[]{:S(2)}, u32[]{:S(2)}) collective-permute-start(f32[12,64,256]{2,1,0:T(8,128)S(1)} %get-tuple-element.45.msg_b), channel_id=1, source_target_pairs={{1,0},{2,1},{3,2},{4,3},{5,4},{6,5},{7,6},{8,7},{9,8},{10,9},{11,1... | collective-permute-start | bytes 2359304 | tf_op jit(solution)/shard_map/ppermute | solution.py:503
  18.8 8.9 %interior.1 = (f32[8,8,64,256]{3,2,1,0:T(8,128)S(1)}, f32[8,8,64,256]{3,2,1,0:T(8,128)S(1)}, f32[8,4,8,128]{3,2,1,0:T(8,128)S(1)}, f32[4,64,256]{2,1,0:T(8,128)S(1)}) custom-call(s32[1,4]{1,0:T(1,128)} %src_in.3, f32[8,8,64,256]{3,2,1,0:T(8,128)S(1)} %get-tuple-element.51.x, f32[4,8,64,256]{3,2,1,0:T(8,128)S(1)} %get-tuple-element.52.rs, ...), custom_call_target="tpu_custom_call" | custom-call | flops 131072 | bytes 131072 | tf_op jit(solution)/shard_map/interior/pallas_call | solution.py:554
  27.7 0.0 collective-permute-done.2.got_a
  27.7 0.0 collective-permute-done.3.got_b
  27.7 2.2 %near.1 = (f32[8,8,64,256]{3,2,1,0:T(8,128)S(1)}, f32[8,8,64,256]{3,2,1,0:T(8,128)S(1)}, f32[2,8,64,256]{3,2,1,0:T(8,128)S(1)}, f32[2,8,64,256]{3,2,1,0:T(8,128)...) custom-call(f32[11,64,256]{2,1,0:T(8,128)S(1)} %collective-permute-d, ...), custom_call_target="tpu_custom_call", output_to_operand_aliasing={{0}: (11, {}), {1}: (12, {})} | custom-call | flops 1310720000 | bytes 1310720000 | tf_op jit(solution)/shard_map/near/pallas_call | solution.py:566
  30.0 1.3 %collective-permute-start.4 = (f32[4,64,256]{2,1,0:T(8,128)S(1)}, f32[4,64,256]{2,1,0:T(8,128)S(1)}, u32[]{:S(2)}, u32[]{:S(2)}) collective-permute-start(f32[4,64,256]{2,1,0:T(8,128)S(1)} %get-tuple-element.70), channel_id=1, source_target_pairs={{1,0},{2,1},{3,2},{4,3},{5,4},{6,5},{7,6},{8,7},{9,8},{10,9},{11,1... | collective-permute-start | bytes 786440 | tf_op jit(solution)/shard_map/ppermute | solution.py:578
  31.3 3.7 %collective-permute-done.got_a = f32[12,64,256]{2,1,0:T(8,128)S(1)} collective-permute-done((f32[12,64,256]{2,1,0:T(8,128)S(1)}, f32[12,64,256]{2,1,0:T(8,128)S(1)}, u32[]{:S(2)}, u32[]{:S(2)}) %collective-permute-start) | collective-permute-done | bytes 786464 | tf_op jit(solution)/shard_map/ppermute | solution.py:503
  34.9 4.6 %collective-permute-done.1.got_b = f32[12,64,256]{2,1,0:T(8,128)S(1)} collective-permute-done((f32[12,64,256]{2,1,0:T(8,128)S(1)}, f32[12,64,256]{2,1,0:T(8,128)S(1)}, u32[]{:S(2)}, u32[]{:S(2)}) %collective-permute-start.1) | collective-permute-done | bytes 786464 | tf_op jit(solution)/shard_map/ppermute | solution.py:503
  39.5 1.9 %boundary.1 = (f32[8,8,64,256]{3,2,1,0:T(8,128)S(1)}, f32[2,8,64,256]{3,2,1,0:T(8,128)S(1)}, f32[2,8,64,256]{3,2,1,0:T(8,128)S(1)}, f32[32,8,128]{2,1,0:T(8,128)S(1)}) custom-call(f32[12,64,256]{2,1,0:T(8,128)S(1)} %collective-permute-done.got_a, f32[12,64,256]{2,1,0:T(8,128)S(1)} %collective-permute-done.1.got_b, ...), custom_call_target="tpu_custom_call", output_to_operand_aliasing={{0}: (11, {})} | custom-call | tf_op jit(solution)/shard_map/boundary/pallas_call | solution.py:580
  41.4 21.8 %all_to_all.5.parts = f32[32,8,128]{2,1,0:T(8,128)S(1)} all-to-all(f32[32,8,128]{2,1,0:T(8,128)S(1)} %get-tuple-element.66), channel_id=1, replica_groups=mesh['grp'=8,'tile'=32] {'tile'}, dimensions={0} | all-to-all | bytes 262144 | tf_op jit(solution)/shard_map/all_to_all | solution.py:591
  63.1 0.1 steps.1.scale
  63.3 0.0 collective-permute-done.4.extra
  63.3 2.8 %correlate.1 = (f32[4,8,8,256]{3,2,1,0:T(8,128)S(1)}, f32[4,8,8,256]{3,2,1,0:T(8,128)S(1)}) custom-call(f32[8,256]{1,0:T(8,128)S(1)} %get-tuple-element.43.weight, f32[2,8,256]{2,1,0:T(8,128)S(1)} %steps.1.scale, f32[8,8,64,256]{3,2,1,0:T(8,128)S(1)} %get-tuple-element.51.x, f32[8,8,64,256]{3,2,1,0:T(8,128)S(1)} %get-tuple-element.61.z, ...), custom_call_target="tpu_custom_call" | custom-call | tf_op jit(solution)/shard_map/correlate/pallas_call | solution.py:604
  66.1 2.6 %collective-permute-start.5 = (f32[4,8,8,256]{3,2,1,0:T(8,128)S(1)}, f32[4,8,8,256]{3,2,1,0:T(8,128)S(1)}, u32[]{:S(2)}, u32[]{:S(2)}) collective-permute-start(f32[4,8,8,256]{3,2,1,0:T(8,128)S(1)} %get-tuple-element.72), channel_id=1, source_target_pairs={{0,32},{32,0},{64,96},{96,64},{128,160},{160,128},{192,224},{224,1... | collective-permute-start | bytes 786440 | tf_op jit(solution)/shard_map/ppermute | solution.py:615
  68.7 1.2 %collective-permute-done.5.got = f32[4,8,8,256]{3,2,1,0:T(8,128)S(1)} collective-permute-done((f32[4,8,8,256]{3,2,1,0:T(8,128)S(1)}, f32[4,8,8,256]{3,2,1,0:T(8,128)S(1)}, u32[]{:S(2)}, u32[]{:S(2)}) %collective-permute-start.5) | collective-permute-done | bytes 262176 | tf_op jit(solution)/shard_map/ppermute | solution.py:615
  69.9 2.8 %collective-permute-start.6 = (f32[8,8,256]{2,1,0:T(8,128)S(1)}, f32[8,8,256]{2,1,0:T(8,128)S(1)}, u32[]{:S(2)}, u32[]{:S(2)}) collective-permute-start(f32[8,8,256]{2,1,0:T(8,128)S(1)} %get-tuple-element.74), channel_id=1, source_target_pairs={{0,128},{32,160},{64,192},{96,224},{128,0},{160,32},{192,64},{224,... | collective-permute-start | bytes 196616 | tf_op jit(solution)/shard_map/ppermute | solution.py:615
  72.7 0.3 collective-permute-start.7
  73.0 0.6 collective-permute-start.8
  73.6 1.0 %collective-permute-done.6.one = f32[8,8,256]{2,1,0:T(8,128)S(1)} collective-permute-done((f32[8,8,256]{2,1,0:T(8,128)S(1)}, f32[8,8,256]{2,1,0:T(8,128)S(1)}, u32[]{:S(2)}, u32[]{:S(2)}) %collective-permute-start.6) | collective-permute-done | bytes 65568 | tf_op jit(solution)/shard_map/ppermute | solution.py:615
  74.6 1.6 %collective-permute-done.7.two = f32[8,8,256]{2,1,0:T(8,128)S(1)} collective-permute-done((f32[8,8,256]{2,1,0:T(8,128)S(1)}, f32[8,8,256]{2,1,0:T(8,128)S(1)}, u32[]{:S(2)}, u32[]{:S(2)}) %collective-permute-start.7) | collective-permute-done | bytes 65568 | tf_op jit(solution)/shard_map/ppermute | solution.py:615
  76.2 1.1 %collective-permute-done.8.three = f32[8,8,256]{2,1,0:T(8,128)S(1)} collective-permute-done((f32[8,8,256]{2,1,0:T(8,128)S(1)}, f32[8,8,256]{2,1,0:T(8,128)S(1)}, u32[]{:S(2)}, u32[]{:S(2)}) %collective-permute-start.8) | collective-permute-done | bytes 65568 | tf_op jit(solution)/shard_map/ppermute | solution.py:615
  77.4 0.6 total.1
  (1 shorter events, 0.0 us)
Async XLA Ops:
  1.5 26.2 %collective-permute-start.2 = (f32[11,64,256]{2,1,0:T(8,128)S(1)}, f32[11,64,256]{2,1,0:T(8,128)S(1)}, u32[]{:S(2)}, u32[]{:S(2)}) collective-permute-start(f32[11,64,256]{2,1,0:T(8,128)S(1)} %get-tuple-element.41.head_a), channel_id=1, source_target_pairs={{0,1},{1,2},{2,3},{3,4},{4,5},{5,6},{6,7},{7,8},{8,9},{9,10},{10,1... | collective-permute-start | bytes 2162696 | tf_op jit(solution)/shard_map/ppermute | solution.py:503
  2.8 24.9 %collective-permute-start.3 = (f32[11,64,256]{2,1,0:T(8,128)S(1)}, f32[11,64,256]{2,1,0:T(8,128)S(1)}, u32[]{:S(2)}, u32[]{:S(2)}) collective-permute-start(f32[11,64,256]{2,1,0:T(8,128)S(1)} %get-tuple-element.42.head_b), channel_id=1, source_target_pairs={{1,0},{2,1},{3,2},{4,3},{5,4},{6,5},{7,6},{8,7},{9,8},{10,9},{11,1... | collective-permute-start | bytes 2162696 | tf_op jit(solution)/shard_map/ppermute | solution.py:503
  13.4 21.5 %collective-permute-start = (f32[12,64,256]{2,1,0:T(8,128)S(1)}, f32[12,64,256]{2,1,0:T(8,128)S(1)}, u32[]{:S(2)}, u32[]{:S(2)}) collective-permute-start(f32[12,64,256]{2,1,0:T(8,128)S(1)} %get-tuple-element.44.msg_a), channel_id=1, source_target_pairs={{0,1},{1,2},{2,3},{3,4},{4,5},{5,6},{6,7},{7,8},{8,9},{9,10},{10,1... | collective-permute-start | bytes 2359304 | tf_op jit(solution)/shard_map/ppermute | solution.py:503
  14.7 24.8 %collective-permute-start.1 = (f32[12,64,256]{2,1,0:T(8,128)S(1)}, f32[12,64,256]{2,1,0:T(8,128)S(1)}, u32[]{:S(2)}, u32[]{:S(2)}) collective-permute-start(f32[12,64,256]{2,1,0:T(8,128)S(1)} %get-tuple-element.45.msg_b), channel_id=1, source_target_pairs={{1,0},{2,1},{3,2},{4,3},{5,4},{6,5},{7,6},{8,7},{9,8},{10,9},{11,1... | collective-permute-start | bytes 2359304 | tf_op jit(solution)/shard_map/ppermute | solution.py:503
  30.0 33.3 %collective-permute-start.4 = (f32[4,64,256]{2,1,0:T(8,128)S(1)}, f32[4,64,256]{2,1,0:T(8,128)S(1)}, u32[]{:S(2)}, u32[]{:S(2)}) collective-permute-start(f32[4,64,256]{2,1,0:T(8,128)S(1)} %get-tuple-element.70), channel_id=1, source_target_pairs={{1,0},{2,1},{3,2},{4,3},{5,4},{6,5},{7,6},{8,7},{9,8},{10,9},{11,1... | collective-permute-start | bytes 786440 | tf_op jit(solution)/shard_map/ppermute | solution.py:578
  66.1 3.8 %collective-permute-start.5 = (f32[4,8,8,256]{3,2,1,0:T(8,128)S(1)}, f32[4,8,8,256]{3,2,1,0:T(8,128)S(1)}, u32[]{:S(2)}, u32[]{:S(2)}) collective-permute-start(f32[4,8,8,256]{3,2,1,0:T(8,128)S(1)} %get-tuple-element.72), channel_id=1, source_target_pairs={{0,32},{32,0},{64,96},{96,64},{128,160},{160,128},{192,224},{224,1... | collective-permute-start | bytes 786440 | tf_op jit(solution)/shard_map/ppermute | solution.py:615
  69.9 4.7 %collective-permute-start.6 = (f32[8,8,256]{2,1,0:T(8,128)S(1)}, f32[8,8,256]{2,1,0:T(8,128)S(1)}, u32[]{:S(2)}, u32[]{:S(2)}) collective-permute-start(f32[8,8,256]{2,1,0:T(8,128)S(1)} %get-tuple-element.74), channel_id=1, source_target_pairs={{0,128},{32,160},{64,192},{96,224},{128,0},{160,32},{192,64},{224,... | collective-permute-start | bytes 196616 | tf_op jit(solution)/shard_map/ppermute | solution.py:615
  72.7 3.5 %collective-permute-start.7 = (f32[8,8,256]{2,1,0:T(8,128)S(1)}, f32[8,8,256]{2,1,0:T(8,128)S(1)}, u32[]{:S(2)}, u32[]{:S(2)}) collective-permute-start(f32[8,8,256]{2,1,0:T(8,128)S(1)} %get-tuple-element.75), channel_id=1, source_target_pairs={{0,64},{32,96},{64,0},{96,32},{128,192},{160,224},{192,128},{224,1... | collective-permute-start | bytes 196616 | tf_op jit(solution)/shard_map/ppermute | solution.py:615
  73.0 4.3 %collective-permute-start.8 = (f32[8,8,256]{2,1,0:T(8,128)S(1)}, f32[8,8,256]{2,1,0:T(8,128)S(1)}, u32[]{:S(2)}, u32[]{:S(2)}) collective-permute-start(f32[8,8,256]{2,1,0:T(8,128)S(1)} %get-tuple-element.76), channel_id=1, source_target_pairs={{0,192},{32,224},{64,128},{96,160},{128,64},{160,96},{192,0},{224,... | collective-permute-start | bytes 196616 | tf_op jit(solution)/shard_map/ppermute | solution.py:615

commit v5 on v4

--- a/solution.py
+++ b/solution.py
@@ -309,7 +309,7 @@
         far[side, 6] = beyond
         far[side, 7] = back_z
 
-    @pl.loop(0, systems)
+    @pl.loop(0, systems, unroll=2)
     def _(s):
         c0, c1, c2, c3 = [moments_in[s, at] for at in range(4)]
         for at, (got, head, msg), _, side, edge, inner, third, face, face_next, _ in sides:
@@ -334,6 +334,12 @@
             moments[s, at] = c
 
 
+def moment_lanes(systems):
+    lane = lax.broadcasted_iota(jnp.int32, (systems, 128), 1)
+    row = lax.broadcasted_iota(jnp.int32, (systems, 128), 0)
+    return [lane == 4 * row + at for at in range(4)]
+
+
 def outer_slope(v, beyond, edge, far, side):
     w = far[side, 5] * v - lateral(v, far[side, 2], far[side, 3], far[side, 7])
     w = w - far[side, 6] * (beyond - v) - far[side, 0] * (edge - v)
@@ -350,7 +356,7 @@
     half = slots // 2
     sides = both_sides(planes, slots, ((got_a, head_b), (got_b, head_a)))
 
-    @pl.loop(0, systems)
+    @pl.loop(0, systems, unroll=2)
     def _(s):
         c0, c1, c2, c3 = [moments[s, at] for at in range(4)]
         for _, (got, head), _, side, edge, inner, _, face, _, _ in sides:
@@ -369,7 +375,7 @@
         for at, c in enumerate((c0, c1, c2, c3 + c3)):
             sums[at, pl.ds(s, 1)] = c.sum(0, keepdims=True)
 
-    @pl.loop(0, half)
+    @pl.loop(0, half, unroll=2)
     def _(at):
         for _, (got, _), _, side, edge, _, _, _, _, lead in sides:
             for place, s in ((at, lead + at), (half + at, slots + lead + at)):
@@ -378,18 +384,17 @@
                 pair = folded(far[side, 0] * nm * n[s, edge])
                 sums[3, pl.ds(s, 1)] = sums[3, pl.ds(s, 1)] + 2.0 * pair.sum(0, keepdims=True)
 
-    lanes_at = lax.broadcasted_iota(jnp.int32, (systems, 128), 1)
     packed = jnp.zeros((systems, 128), F32)
-    for at in range(4):
-        packed = packed + jnp.where(lanes_at == at, sums[at].sum(1, keepdims=True), 0.0)
-    out[...] = jnp.broadcast_to(packed[None], out.shape)
+    for at, here in enumerate(moment_lanes(systems)):
+        packed = packed + jnp.where(here, sums[at].sum(1, keepdims=True), 0.0)
+    out[...] = jnp.broadcast_to(packed.sum(0, keepdims=True)[None], out.shape)
 
 
 def steps_kernel(parts, scale):
-    summed = parts[...].sum(0)
-    lanes_at = lax.broadcasted_iota(jnp.int32, summed.shape, 1)
+    systems = scale.shape[1]
+    summed = jnp.broadcast_to(parts[...].sum(0), (systems, 128))
     m0, m1, m2, c3 = [
-        jnp.where(lanes_at == at, summed, 0.0).sum(1, keepdims=True) for at in range(4)
+        jnp.where(here, summed, 0.0).sum(1, keepdims=True) for here in moment_lanes(systems)
     ]
     unit = 1.0 / m1
     m0, m1, m2, c3 = m0 * unit, m1 * unit, m2 * unit, c3 * unit
@@ -579,7 +584,7 @@
 
     n, ext_z, ext_n, moments = pl.pallas_call(
         boundary_kernel,
-        out_shape=[field, pair_of, pair_of, held(tiles, systems, 128)],
+        out_shape=[field, pair_of, pair_of, held(tiles, 1, 128)],
         in_specs=[IN_VMEM] * 13,
         out_specs=[IN_VMEM] * 4,
         input_output_aliases={11: 0},

time: 78.3 us -> 77.4 us (0.989)
  blocking collectives: 21.8 us -> 20.9 us
    all_to_all x1, blocking collectives: 21.8 us -> 20.9 us  [local(): parts = lax.all_to_all(moments, 'tile', 0, 0)]
  transfers between devices with their start and end apart: 9 -> 9, of which waited for: 6 -> 6; matrix products, arithmetic and copies ran while one was open for 0% -> 0% of each run, Pallas kernels for 24% -> 23%
where the time goes in v5:
time: 77.4 us; the launch traced here: 77.1 us
  Pallas kernels  23 us (30%)
  blocking collectives  20.9 us (27%)
  starting transfers between devices  19.1 us (25%)
  waiting for transfers between devices  13.3 us (17%)
    all_to_all x1, blocking collectives, local(): parts = lax.all_to_all(moments, 'tile', 0, 0)  20.9 us
    ppermute x4, starting transfers between devices, opposite(): return lax.ppermute(value, ('grp', 'tile'), pairs)  11.3 us
    pallas_call x1, Pallas kernels, local(): pl.pallas_call(interior_kernel, out_shape=[field, field, held(systems, 4,...  8.94 us
    ppermute x4, waiting for transfers between devices, opposite(): return lax.ppermute(value, ('grp', 'tile'), pairs)  8.37 us
    ppermute x4, starting transfers between devices, swapped(): return lax.ppermute(value, 'grp', [(g, g ^ by) for g in range(groups)])  6.5 us
    pallas_call x1, Pallas kernels, local(): pl.pallas_call(edges_kernel, out_shape=[message, message, field, held(slo...  5.22 us
    ppermute x4, waiting for transfers between devices, swapped(): return lax.ppermute(value, 'grp', [(g, g ^ by) for g in range(groups)])  4.94 us
    pallas_call x1, Pallas kernels, local(): pl.pallas_call(correlate_kernel, out_shape=[blocks, blocks], in_specs=[IN...  2.82 us
  transfers between devices with their start and end apart: 9, of which 6 were waited for; matrix products, arithmetic and copies ran while one was open for 0% of the time, Pallas kernels for 23%

profile of v5, /device:TPU:1, one launch (start us, length us, event | category | flops | bytes accessed | tf_op | source)
XLA Modules:
  0.0 77.1 jit_solution(13124114540117470005)
XLA Ops:
  0.0 1.5 %head.1 = (f32[11,64,256]{2,1,0:T(8,128)S(1)}, f32[11,64,256]{2,1,0:T(8,128)S(1)}) custom-call(f32[8]{0:T(128)} %table_in.3, f32[1,4,8,64,256]{4,3,2,1,0:T(8,128)} %fwd.3, f32[1,4,8,64,256]{4,3,2,1,0:T(8,128)} %adj.3, s32[8,64,256]{2,1,0:T(8,128)} %label.3, s32[8,64,256]{2,1,0:T(8,128)} %cut.3), custom_call_target="tpu_custom_call" | custom-call | flops 2621440 | bytes 2621440 | tf_op jit(solution)/shard_map/head/pallas_call | solution.py:510
  1.5 1.3 %collective-permute-start.2 = (f32[11,64,256]{2,1,0:T(8,128)S(1)}, f32[11,64,256]{2,1,0:T(8,128)S(1)}, u32[]{:S(2)}, u32[]{:S(2)}) collective-permute-start(f32[11,64,256]{2,1,0:T(8,128)S(1)} %get-tuple-element.41.head_a), channel_id=1, source_target_pairs={{0,1},{1,2},{2,3},{3,4},{4,5},{5,6},{6,7},{7,8},{8,9},{9,10},{10,1... | collective-permute-start | bytes 2162696 | tf_op jit(solution)/shard_map/ppermute | solution.py:508
  2.8 4.7 %collective-permute-start.3 = (f32[11,64,256]{2,1,0:T(8,128)S(1)}, f32[11,64,256]{2,1,0:T(8,128)S(1)}, u32[]{:S(2)}, u32[]{:S(2)}) collective-permute-start(f32[11,64,256]{2,1,0:T(8,128)S(1)} %get-tuple-element.42.head_b), channel_id=1, source_target_pairs={{1,0},{2,1},{3,2},{4,3},{5,4},{6,5},{7,6},{8,7},{9,8},{10,9},{11,1... | collective-permute-start | bytes 2162696 | tf_op jit(solution)/shard_map/ppermute | solution.py:508
  8.2 5.2 %edges.1 = (f32[12,64,256]{2,1,0:T(8,128)S(1)}, f32[12,64,256]{2,1,0:T(8,128)S(1)}, f32[8,8,64,256]{3,2,1,0:T(8,128)S(1)}, f32[4,8,64,256]{3,2,1,0:T(8,128)S(1)}...) custom-call(f32[8]{0:T(128)} %table_in.3, ...), custom_call_target="tpu_custom_call" | custom-call | flops 2621440 | bytes 2621440 | tf_op jit(solution)/shard_map/edges/pallas_call | solution.py:529
  13.4 1.3 %collective-permute-start = (f32[12,64,256]{2,1,0:T(8,128)S(1)}, f32[12,64,256]{2,1,0:T(8,128)S(1)}, u32[]{:S(2)}, u32[]{:S(2)}) collective-permute-start(f32[12,64,256]{2,1,0:T(8,128)S(1)} %get-tuple-element.44.msg_a), channel_id=1, source_target_pairs={{0,1},{1,2},{2,3},{3,4},{4,5},{5,6},{6,7},{7,8},{8,9},{9,10},{10,1... | collective-permute-start | bytes 2359304 | tf_op jit(solution)/shard_map/ppermute | solution.py:508
  14.7 4.0 %collective-permute-start.1 = (f32[12,64,256]{2,1,0:T(8,128)S(1)}, f32[12,64,256]{2,1,0:T(8,128)S(1)}, u32[]{:S(2)}, u32[]{:S(2)}) collective-permute-start(f32[12,64,256]{2,1,0:T(8,128)S(1)} %get-tuple-element.45.msg_b), channel_id=1, source_target_pairs={{1,0},{2,1},{3,2},{4,3},{5,4},{6,5},{7,6},{8,7},{9,8},{10,9},{11,1... | collective-permute-start | bytes 2359304 | tf_op jit(solution)/shard_map/ppermute | solution.py:508
  18.8 8.9 %interior.1 = (f32[8,8,64,256]{3,2,1,0:T(8,128)S(1)}, f32[8,8,64,256]{3,2,1,0:T(8,128)S(1)}, f32[8,4,8,128]{3,2,1,0:T(8,128)S(1)}, f32[4,64,256]{2,1,0:T(8,128)S(1)}) custom-call(s32[1,4]{1,0:T(1,128)} %src_in.3, f32[8,8,64,256]{3,2,1,0:T(8,128)S(1)} %get-tuple-element.51.x, f32[4,8,64,256]{3,2,1,0:T(8,128)S(1)} %get-tuple-element.52.rs, ...), custom_call_target="tpu_custom_call" | custom-call | flops 131072 | bytes 131072 | tf_op jit(solution)/shard_map/interior/pallas_call | solution.py:559
  27.7 0.0 collective-permute-done.2.got_a
  27.7 0.0 collective-permute-done.3.got_b
  27.7 2.1 %near.1 = (f32[8,8,64,256]{3,2,1,0:T(8,128)S(1)}, f32[8,8,64,256]{3,2,1,0:T(8,128)S(1)}, f32[2,8,64,256]{3,2,1,0:T(8,128)S(1)}, f32[2,8,64,256]{3,2,1,0:T(8,128)...) custom-call(f32[11,64,256]{2,1,0:T(8,128)S(1)} %collective-permute-d, ...), custom_call_target="tpu_custom_call", output_to_operand_aliasing={{0}: (11, {}), {1}: (12, {})} | custom-call | flops 1310720000 | bytes 1310720000 | tf_op jit(solution)/shard_map/near/pallas_call | solution.py:571
  29.8 1.3 %collective-permute-start.4 = (f32[4,64,256]{2,1,0:T(8,128)S(1)}, f32[4,64,256]{2,1,0:T(8,128)S(1)}, u32[]{:S(2)}, u32[]{:S(2)}) collective-permute-start(f32[4,64,256]{2,1,0:T(8,128)S(1)} %get-tuple-element.70), channel_id=1, source_target_pairs={{1,0},{2,1},{3,2},{4,3},{5,4},{6,5},{7,6},{8,7},{9,8},{10,9},{11,1... | collective-permute-start | bytes 786440 | tf_op jit(solution)/shard_map/ppermute | solution.py:583
  31.1 3.8 %collective-permute-done.got_a = f32[12,64,256]{2,1,0:T(8,128)S(1)} collective-permute-done((f32[12,64,256]{2,1,0:T(8,128)S(1)}, f32[12,64,256]{2,1,0:T(8,128)S(1)}, u32[]{:S(2)}, u32[]{:S(2)}) %collective-permute-start) | collective-permute-done | bytes 786464 | tf_op jit(solution)/shard_map/ppermute | solution.py:508
  34.9 4.6 %collective-permute-done.1.got_b = f32[12,64,256]{2,1,0:T(8,128)S(1)} collective-permute-done((f32[12,64,256]{2,1,0:T(8,128)S(1)}, f32[12,64,256]{2,1,0:T(8,128)S(1)}, u32[]{:S(2)}, u32[]{:S(2)}) %collective-permute-start.1) | collective-permute-done | bytes 786464 | tf_op jit(solution)/shard_map/ppermute | solution.py:508
  39.5 1.6 %boundary.1 = (f32[8,8,64,256]{3,2,1,0:T(8,128)S(1)}, f32[2,8,64,256]{3,2,1,0:T(8,128)S(1)}, f32[2,8,64,256]{3,2,1,0:T(8,128)S(1)}, f32[32,1,128]{2,1,0:T(1,128)S(1)}) custom-call(f32[12,64,256]{2,1,0:T(8,128)S(1)} %collective-permute-done.got_a, f32[12,64,256]{2,1,0:T(8,128)S(1)} %collective-permute-done.1.got_b, ...), custom_call_target="tpu_custom_call", output_to_operand_aliasing={{0}: (11, {})} | custom-call | tf_op jit(solution)/shard_map/boundary/pallas_call | solution.py:585
  41.1 20.9 %all_to_all.5.parts = f32[32,1,128]{2,1,0:T(1,128)S(1)} all-to-all(f32[32,1,128]{2,1,0:T(1,128)S(1)} %get-tuple-element.66), channel_id=1, replica_groups=mesh['grp'=8,'tile'=32] {'tile'}, dimensions={0} | all-to-all | bytes 32768 | tf_op jit(solution)/shard_map/all_to_all | solution.py:596
  62.0 0.1 steps.1.scale
  62.1 0.0 collective-permute-done.4.extra
  62.2 2.8 %correlate.1 = (f32[4,8,8,256]{3,2,1,0:T(8,128)S(1)}, f32[4,8,8,256]{3,2,1,0:T(8,128)S(1)}) custom-call(f32[8,256]{1,0:T(8,128)S(1)} %get-tuple-element.43.weight, f32[2,8,256]{2,1,0:T(8,128)S(1)} %steps.1.scale, f32[8,8,64,256]{3,2,1,0:T(8,128)S(1)} %get-tuple-element.51.x, f32[8,8,64,256]{3,2,1,0:T(8,128)S(1)} %get-tuple-element.61.z, ...), custom_call_target="tpu_custom_call" | custom-call | tf_op jit(solution)/shard_map/correlate/pallas_call | solution.py:609
  65.0 2.8 %collective-permute-start.5 = (f32[4,8,8,256]{3,2,1,0:T(8,128)S(1)}, f32[4,8,8,256]{3,2,1,0:T(8,128)S(1)}, u32[]{:S(2)}, u32[]{:S(2)}) collective-permute-start(f32[4,8,8,256]{3,2,1,0:T(8,128)S(1)} %get-tuple-element.72), channel_id=1, source_target_pairs={{0,32},{32,0},{64,96},{96,64},{128,160},{160,128},{192,224},{224,1... | collective-permute-start | bytes 786440 | tf_op jit(solution)/shard_map/ppermute | solution.py:620
  67.8 1.2 %collective-permute-done.5.got = f32[4,8,8,256]{3,2,1,0:T(8,128)S(1)} collective-permute-done((f32[4,8,8,256]{3,2,1,0:T(8,128)S(1)}, f32[4,8,8,256]{3,2,1,0:T(8,128)S(1)}, u32[]{:S(2)}, u32[]{:S(2)}) %collective-permute-start.5) | collective-permute-done | bytes 262176 | tf_op jit(solution)/shard_map/ppermute | solution.py:620
  69.0 2.8 %collective-permute-start.6 = (f32[8,8,256]{2,1,0:T(8,128)S(1)}, f32[8,8,256]{2,1,0:T(8,128)S(1)}, u32[]{:S(2)}, u32[]{:S(2)}) collective-permute-start(f32[8,8,256]{2,1,0:T(8,128)S(1)} %get-tuple-element.74), channel_id=1, source_target_pairs={{0,128},{32,160},{64,192},{96,224},{128,0},{160,32},{192,64},{224,... | collective-permute-start | bytes 196616 | tf_op jit(solution)/shard_map/ppermute | solution.py:620
  71.8 0.3 collective-permute-start.7
  72.1 0.6 collective-permute-start.8
  72.7 1.0 %collective-permute-done.6.one = f32[8,8,256]{2,1,0:T(8,128)S(1)} collective-permute-done((f32[8,8,256]{2,1,0:T(8,128)S(1)}, f32[8,8,256]{2,1,0:T(8,128)S(1)}, u32[]{:S(2)}, u32[]{:S(2)}) %collective-permute-start.6) | collective-permute-done | bytes 65568 | tf_op jit(solution)/shard_map/ppermute | solution.py:620
  73.7 1.6 %collective-permute-done.7.two = f32[8,8,256]{2,1,0:T(8,128)S(1)} collective-permute-done((f32[8,8,256]{2,1,0:T(8,128)S(1)}, f32[8,8,256]{2,1,0:T(8,128)S(1)}, u32[]{:S(2)}, u32[]{:S(2)}) %collective-permute-start.7) | collective-permute-done | bytes 65568 | tf_op jit(solution)/shard_map/ppermute | solution.py:620
  75.3 1.1 %collective-permute-done.8.three = f32[8,8,256]{2,1,0:T(8,128)S(1)} collective-permute-done((f32[8,8,256]{2,1,0:T(8,128)S(1)}, f32[8,8,256]{2,1,0:T(8,128)S(1)}, u32[]{:S(2)}, u32[]{:S(2)}) %collective-permute-start.8) | collective-permute-done | bytes 65568 | tf_op jit(solution)/shard_map/ppermute | solution.py:620
  76.4 0.6 total.1
  (1 shorter events, 0.0 us)
Async XLA Ops:
  1.5 26.2 %collective-permute-start.2 = (f32[11,64,256]{2,1,0:T(8,128)S(1)}, f32[11,64,256]{2,1,0:T(8,128)S(1)}, u32[]{:S(2)}, u32[]{:S(2)}) collective-permute-start(f32[11,64,256]{2,1,0:T(8,128)S(1)} %get-tuple-element.41.head_a), channel_id=1, source_target_pairs={{0,1},{1,2},{2,3},{3,4},{4,5},{5,6},{6,7},{7,8},{8,9},{9,10},{10,1... | collective-permute-start | bytes 2162696 | tf_op jit(solution)/shard_map/ppermute | solution.py:508
  2.8 24.9 %collective-permute-start.3 = (f32[11,64,256]{2,1,0:T(8,128)S(1)}, f32[11,64,256]{2,1,0:T(8,128)S(1)}, u32[]{:S(2)}, u32[]{:S(2)}) collective-permute-start(f32[11,64,256]{2,1,0:T(8,128)S(1)} %get-tuple-element.42.head_b), channel_id=1, source_target_pairs={{1,0},{2,1},{3,2},{4,3},{5,4},{6,5},{7,6},{8,7},{9,8},{10,9},{11,1... | collective-permute-start | bytes 2162696 | tf_op jit(solution)/shard_map/ppermute | solution.py:508
  13.4 21.5 %collective-permute-start = (f32[12,64,256]{2,1,0:T(8,128)S(1)}, f32[12,64,256]{2,1,0:T(8,128)S(1)}, u32[]{:S(2)}, u32[]{:S(2)}) collective-permute-start(f32[12,64,256]{2,1,0:T(8,128)S(1)} %get-tuple-element.44.msg_a), channel_id=1, source_target_pairs={{0,1},{1,2},{2,3},{3,4},{4,5},{5,6},{6,7},{7,8},{8,9},{9,10},{10,1... | collective-permute-start | bytes 2359304 | tf_op jit(solution)/shard_map/ppermute | solution.py:508
  14.7 24.8 %collective-permute-start.1 = (f32[12,64,256]{2,1,0:T(8,128)S(1)}, f32[12,64,256]{2,1,0:T(8,128)S(1)}, u32[]{:S(2)}, u32[]{:S(2)}) collective-permute-start(f32[12,64,256]{2,1,0:T(8,128)S(1)} %get-tuple-element.45.msg_b), channel_id=1, source_target_pairs={{1,0},{2,1},{3,2},{4,3},{5,4},{6,5},{7,6},{8,7},{9,8},{10,9},{11,1... | collective-permute-start | bytes 2359304 | tf_op jit(solution)/shard_map/ppermute | solution.py:508
  29.8 32.3 %collective-permute-start.4 = (f32[4,64,256]{2,1,0:T(8,128)S(1)}, f32[4,64,256]{2,1,0:T(8,128)S(1)}, u32[]{:S(2)}, u32[]{:S(2)}) collective-permute-start(f32[4,64,256]{2,1,0:T(8,128)S(1)} %get-tuple-element.70), channel_id=1, source_target_pairs={{1,0},{2,1},{3,2},{4,3},{5,4},{6,5},{7,6},{8,7},{9,8},{10,9},{11,1... | collective-permute-start | bytes 786440 | tf_op jit(solution)/shard_map/ppermute | solution.py:583
  65.0 4.0 %collective-permute-start.5 = (f32[4,8,8,256]{3,2,1,0:T(8,128)S(1)}, f32[4,8,8,256]{3,2,1,0:T(8,128)S(1)}, u32[]{:S(2)}, u32[]{:S(2)}) collective-permute-start(f32[4,8,8,256]{3,2,1,0:T(8,128)S(1)} %get-tuple-element.72), channel_id=1, source_target_pairs={{0,32},{32,0},{64,96},{96,64},{128,160},{160,128},{192,224},{224,1... | collective-permute-start | bytes 786440 | tf_op jit(solution)/shard_map/ppermute | solution.py:620
  69.0 4.7 %collective-permute-start.6 = (f32[8,8,256]{2,1,0:T(8,128)S(1)}, f32[8,8,256]{2,1,0:T(8,128)S(1)}, u32[]{:S(2)}, u32[]{:S(2)}) collective-permute-start(f32[8,8,256]{2,1,0:T(8,128)S(1)} %get-tuple-element.74), channel_id=1, source_target_pairs={{0,128},{32,160},{64,192},{96,224},{128,0},{160,32},{192,64},{224,... | collective-permute-start | bytes 196616 | tf_op jit(solution)/shard_map/ppermute | solution.py:620
  71.8 3.5 %collective-permute-start.7 = (f32[8,8,256]{2,1,0:T(8,128)S(1)}, f32[8,8,256]{2,1,0:T(8,128)S(1)}, u32[]{:S(2)}, u32[]{:S(2)}) collective-permute-start(f32[8,8,256]{2,1,0:T(8,128)S(1)} %get-tuple-element.75), channel_id=1, source_target_pairs={{0,64},{32,96},{64,0},{96,32},{128,192},{160,224},{192,128},{224,1... | collective-permute-start | bytes 196616 | tf_op jit(solution)/shard_map/ppermute | solution.py:620
  72.1 4.3 %collective-permute-start.8 = (f32[8,8,256]{2,1,0:T(8,128)S(1)}, f32[8,8,256]{2,1,0:T(8,128)S(1)}, u32[]{:S(2)}, u32[]{:S(2)}) collective-permute-start(f32[8,8,256]{2,1,0:T(8,128)S(1)} %get-tuple-element.76), channel_id=1, source_target_pairs={{0,192},{32,224},{64,128},{96,160},{128,64},{160,96},{192,0},{224,... | collective-permute-start | bytes 196616 | tf_op jit(solution)/shard_map/ppermute | solution.py:620

commit v6 on v5

--- a/solution.py
+++ b/solution.py
@@ -86,7 +86,7 @@
     return 1.0 - 0.5 * flags.astype(F32)
 
 
-def head_kernel(table_in, fwd, adj, label, cut, msg_a, msg_b, table, lab, flag, shared, sems):
+def head_kernel(table_in, fwd, adj, label, cut, msg_a, msg_b, table, lab, flag, sems):
     slots = fwd.shape[1]
     planes = label.shape[0]
     last = planes - 1
@@ -116,14 +116,10 @@
     sigma = [conductivity(table, lab[at]) for at in range(4)]
     factor = [cut_factor(flag[at]) for at in range(4)]
     faces = [harmonic(sigma[at], sigma[at + 1]) * factor[at] for at in (0, 2)]
-    for side, at in enumerate((0, 3)):
-        shared[side, 0] = sigma[at]
-        shared[side, 1] = factor[at]
-        shared[side, 2] = faces[side]
     for msg, up in edges:
-        side = jnp.where(up, 1, 0)
-        for at in range(3):
-            msg[systems + at] = shared[side, at]
+        msg[systems] = jnp.where(up, sigma[3], sigma[0])
+        msg[systems + 1] = jnp.where(up, factor[3], factor[0])
+        msg[systems + 2] = jnp.where(up, faces[1], faces[0])
     for copy in copies[5:]:
         copy.wait()
 
@@ -156,7 +152,7 @@
     for copy in copies[:4]:
         copy.wait()
 
-    @pl.loop(0, planes)
+    @pl.loop(0, planes, unroll=2)
     def _(p):
         value = conductivity(table, lab[p])
         factor = cut_factor(flag[p])
@@ -175,7 +171,7 @@
     def _(p):
         kxf[p] = harmonic(sig[p - 1], sig[p]) * fac[p - 1]
 
-    @pl.loop(0, planes)
+    @pl.loop(0, planes, unroll=2)
     def _(p):
         face_y = ky[p]
         diag = mass[p] + kxf[p] + kxf[p + 1] + face_y + prev_y(face_y) + kz[p] + kzb[p]
@@ -202,12 +198,12 @@
             total = total + kxf[face] * (x[s, edge] - x1) + kxf[face_next] * (x[s, third] - x1)
             msg[systems + at] = inv[inner] * total
 
-        @pl.loop(0, slots)
+        @pl.loop(0, slots, unroll=2)
         def _(s):
             partial(s, plane_source(src, s, edge, (rows, lanes)))
             partial(slots + s, rhs[s, edge])
 
-        @pl.loop(0, half)
+        @pl.loop(0, half, unroll=2)
         def _(s):
             slot = lead + s
             onward(s, slot, plane_source(src, slot, inner, (rows, lanes)))
@@ -309,7 +305,7 @@
         far[side, 6] = beyond
         far[side, 7] = back_z
 
-    @pl.loop(0, systems, unroll=2)
+    @pl.loop(0, systems, unroll=4)
     def _(s):
         c0, c1, c2, c3 = [moments_in[s, at] for at in range(4)]
         for at, (got, head, msg), _, side, edge, inner, third, face, face_next, _ in sides:
@@ -356,7 +352,7 @@
     half = slots // 2
     sides = both_sides(planes, slots, ((got_a, head_b), (got_b, head_a)))
 
-    @pl.loop(0, systems, unroll=2)
+    @pl.loop(0, systems, unroll=4)
     def _(s):
         c0, c1, c2, c3 = [moments[s, at] for at in range(4)]
         for _, (got, head), _, side, edge, inner, _, face, _, _ in sides:
@@ -516,7 +512,6 @@
             pltpu.SMEM(region_sigma.shape, F32),
             VMEM((4, rows, lanes), jnp.int32),
             VMEM((4, rows, lanes), jnp.int32),
-            VMEM((2, 3, rows, lanes), F32),
             pltpu.SemaphoreType.DMA((9,)),
         ],
         compiler_params=params(),

time: 77.4 us -> 78.2 us (1.010)
  Pallas kernels: 23 us -> 22.1 us
  starting transfers between devices: 19.1 us -> 20 us
  waiting for transfers between devices: 13.3 us -> 14.2 us
    ppermute x4, waiting for transfers between devices: 8.37 us -> 9.27 us  [opposite(): return lax.ppermute(value, ('grp', 'tile'), pairs)]
    ppermute x4, starting transfers between devices: 6.5 us -> 7.4 us  [swapped(): return lax.ppermute(value, 'grp', [(g, g ^ by) for g in range(groups)])]
    pallas_call x1, Pallas kernels: 5.22 us -> 4.35 us  [local(): pl.pallas_call(edges_kernel, out_shape=[message, message, field, held(slo...]
  transfers between devices with their start and end apart: 9 -> 9, of which waited for: 6 -> 6; matrix products, arithmetic and copies ran while one was open for 0% -> 0% of each run, Pallas kernels for 23% -> 22%
where the time goes in v6:
time: 78.2 us; the launch traced here: 77.9 us
  Pallas kernels  22.1 us (28%)
  blocking collectives  20.9 us (27%)
  starting transfers between devices  20 us (26%)
  waiting for transfers between devices  14.2 us (18%)
    all_to_all x1, blocking collectives, local(): parts = lax.all_to_all(moments, 'tile', 0, 0)  20.9 us
    ppermute x4, starting transfers between devices, opposite(): return lax.ppermute(value, ('grp', 'tile'), pairs)  11.3 us
    ppermute x4, waiting for transfers between devices, opposite(): return lax.ppermute(value, ('grp', 'tile'), pairs)  9.27 us
    pallas_call x1, Pallas kernels, local(): pl.pallas_call(interior_kernel, out_shape=[field, field, held(systems, 4,...  8.94 us
    ppermute x4, starting transfers between devices, swapped(): return lax.ppermute(value, 'grp', [(g, g ^ by) for g in range(groups)])  7.4 us
    ppermute x4, waiting for transfers between devices, swapped(): return lax.ppermute(value, 'grp', [(g, g ^ by) for g in range(groups)])  4.94 us
    pallas_call x1, Pallas kernels, local(): pl.pallas_call(edges_kernel, out_shape=[message, message, field, held(slo...  4.35 us
    pallas_call x1, Pallas kernels, local(): pl.pallas_call(correlate_kernel, out_shape=[blocks, blocks], in_specs=[IN...  2.82 us
  transfers between devices with their start and end apart: 9, of which 6 were waited for; matrix products, arithmetic and copies ran while one was open for 0% of the time, Pallas kernels for 22%

profile of v6, /device:TPU:1, one launch (start us, length us, event | category | flops | bytes accessed | tf_op | source)
XLA Modules:
  0.0 77.9 jit_solution(5423118849585987066)
XLA Ops:
  0.0 1.5 %head.1 = (f32[11,64,256]{2,1,0:T(8,128)S(1)}, f32[11,64,256]{2,1,0:T(8,128)S(1)}) custom-call(f32[8]{0:T(128)} %table_in.3, f32[1,4,8,64,256]{4,3,2,1,0:T(8,128)} %fwd.3, f32[1,4,8,64,256]{4,3,2,1,0:T(8,128)} %adj.3, s32[8,64,256]{2,1,0:T(8,128)} %label.3, s32[8,64,256]{2,1,0:T(8,128)} %cut.3), custom_call_target="tpu_custom_call" | custom-call | flops 2621440 | bytes 2621440 | tf_op jit(solution)/shard_map/head/pallas_call | solution.py:506
  1.5 1.3 %collective-permute-start.2 = (f32[11,64,256]{2,1,0:T(8,128)S(1)}, f32[11,64,256]{2,1,0:T(8,128)S(1)}, u32[]{:S(2)}, u32[]{:S(2)}) collective-permute-start(f32[11,64,256]{2,1,0:T(8,128)S(1)} %get-tuple-element.41.head_a), channel_id=1, source_target_pairs={{0,1},{1,2},{2,3},{3,4},{4,5},{5,6},{6,7},{7,8},{8,9},{9,10},{10,1... | collective-permute-start | bytes 2162696 | tf_op jit(solution)/shard_map/ppermute | solution.py:504
  2.8 4.7 %collective-permute-start.3 = (f32[11,64,256]{2,1,0:T(8,128)S(1)}, f32[11,64,256]{2,1,0:T(8,128)S(1)}, u32[]{:S(2)}, u32[]{:S(2)}) collective-permute-start(f32[11,64,256]{2,1,0:T(8,128)S(1)} %get-tuple-element.42.head_b), channel_id=1, source_target_pairs={{1,0},{2,1},{3,2},{4,3},{5,4},{6,5},{7,6},{8,7},{9,8},{10,9},{11,1... | collective-permute-start | bytes 2162696 | tf_op jit(solution)/shard_map/ppermute | solution.py:504
  8.2 4.3 %edges.1 = (f32[12,64,256]{2,1,0:T(8,128)S(1)}, f32[12,64,256]{2,1,0:T(8,128)S(1)}, f32[8,8,64,256]{3,2,1,0:T(8,128)S(1)}, f32[4,8,64,256]{3,2,1,0:T(8,128)S(1)}...) custom-call(f32[8]{0:T(128)} %table_in.3, ...), custom_call_target="tpu_custom_call" | custom-call | flops 2621440 | bytes 2621440 | tf_op jit(solution)/shard_map/edges/pallas_call | solution.py:524
  12.5 1.3 %collective-permute-start = (f32[12,64,256]{2,1,0:T(8,128)S(1)}, f32[12,64,256]{2,1,0:T(8,128)S(1)}, u32[]{:S(2)}, u32[]{:S(2)}) collective-permute-start(f32[12,64,256]{2,1,0:T(8,128)S(1)} %get-tuple-element.44.msg_a), channel_id=1, source_target_pairs={{0,1},{1,2},{2,3},{3,4},{4,5},{5,6},{6,7},{7,8},{8,9},{9,10},{10,1... | collective-permute-start | bytes 2359304 | tf_op jit(solution)/shard_map/ppermute | solution.py:504
  13.8 4.0 %collective-permute-start.1 = (f32[12,64,256]{2,1,0:T(8,128)S(1)}, f32[12,64,256]{2,1,0:T(8,128)S(1)}, u32[]{:S(2)}, u32[]{:S(2)}) collective-permute-start(f32[12,64,256]{2,1,0:T(8,128)S(1)} %get-tuple-element.45.msg_b), channel_id=1, source_target_pairs={{1,0},{2,1},{3,2},{4,3},{5,4},{6,5},{7,6},{8,7},{9,8},{10,9},{11,1... | collective-permute-start | bytes 2359304 | tf_op jit(solution)/shard_map/ppermute | solution.py:504
  17.9 8.9 %interior.1 = (f32[8,8,64,256]{3,2,1,0:T(8,128)S(1)}, f32[8,8,64,256]{3,2,1,0:T(8,128)S(1)}, f32[8,4,8,128]{3,2,1,0:T(8,128)S(1)}, f32[4,64,256]{2,1,0:T(8,128)S(1)}) custom-call(s32[1,4]{1,0:T(1,128)} %src_in.3, f32[8,8,64,256]{3,2,1,0:T(8,128)S(1)} %get-tuple-element.51.x, f32[4,8,64,256]{3,2,1,0:T(8,128)S(1)} %get-tuple-element.52.rs, ...), custom_call_target="tpu_custom_call" | custom-call | flops 131072 | bytes 131072 | tf_op jit(solution)/shard_map/interior/pallas_call | solution.py:554
  26.8 0.0 collective-permute-done.2.got_a
  26.8 0.0 collective-permute-done.3.got_b
  26.9 2.1 %near.1 = (f32[8,8,64,256]{3,2,1,0:T(8,128)S(1)}, f32[8,8,64,256]{3,2,1,0:T(8,128)S(1)}, f32[2,8,64,256]{3,2,1,0:T(8,128)S(1)}, f32[2,8,64,256]{3,2,1,0:T(8,128)...) custom-call(f32[11,64,256]{2,1,0:T(8,128)S(1)} %collective-permute-d, ...), custom_call_target="tpu_custom_call", output_to_operand_aliasing={{0}: (11, {}), {1}: (12, {})} | custom-call | flops 1310720000 | bytes 1310720000 | tf_op jit(solution)/shard_map/near/pallas_call | solution.py:566
  28.9 1.3 %collective-permute-start.4 = (f32[4,64,256]{2,1,0:T(8,128)S(1)}, f32[4,64,256]{2,1,0:T(8,128)S(1)}, u32[]{:S(2)}, u32[]{:S(2)}) collective-permute-start(f32[4,64,256]{2,1,0:T(8,128)S(1)} %get-tuple-element.70), channel_id=1, source_target_pairs={{1,0},{2,1},{3,2},{4,3},{5,4},{6,5},{7,6},{8,7},{9,8},{10,9},{11,1... | collective-permute-start | bytes 786440 | tf_op jit(solution)/shard_map/ppermute | solution.py:578
  30.2 4.0 %collective-permute-done.got_a = f32[12,64,256]{2,1,0:T(8,128)S(1)} collective-permute-done((f32[12,64,256]{2,1,0:T(8,128)S(1)}, f32[12,64,256]{2,1,0:T(8,128)S(1)}, u32[]{:S(2)}, u32[]{:S(2)}) %collective-permute-start) | collective-permute-done | bytes 786464 | tf_op jit(solution)/shard_map/ppermute | solution.py:504
  34.2 5.3 %collective-permute-done.1.got_b = f32[12,64,256]{2,1,0:T(8,128)S(1)} collective-permute-done((f32[12,64,256]{2,1,0:T(8,128)S(1)}, f32[12,64,256]{2,1,0:T(8,128)S(1)}, u32[]{:S(2)}, u32[]{:S(2)}) %collective-permute-start.1) | collective-permute-done | bytes 786464 | tf_op jit(solution)/shard_map/ppermute | solution.py:504
  39.5 1.6 %boundary.1 = (f32[8,8,64,256]{3,2,1,0:T(8,128)S(1)}, f32[2,8,64,256]{3,2,1,0:T(8,128)S(1)}, f32[2,8,64,256]{3,2,1,0:T(8,128)S(1)}, f32[32,1,128]{2,1,0:T(1,128)S(1)}) custom-call(f32[12,64,256]{2,1,0:T(8,128)S(1)} %collective-permute-done.got_a, f32[12,64,256]{2,1,0:T(8,128)S(1)} %collective-permute-done.1.got_b, ...), custom_call_target="tpu_custom_call", output_to_operand_aliasing={{0}: (11, {})} | custom-call | tf_op jit(solution)/shard_map/boundary/pallas_call | solution.py:580
  41.1 20.9 %all_to_all.5.parts = f32[32,1,128]{2,1,0:T(1,128)S(1)} all-to-all(f32[32,1,128]{2,1,0:T(1,128)S(1)} %get-tuple-element.66), channel_id=1, replica_groups=mesh['grp'=8,'tile'=32] {'tile'}, dimensions={0} | all-to-all | bytes 32768 | tf_op jit(solution)/shard_map/all_to_all | solution.py:591
  62.0 0.1 steps.1.scale
  62.1 0.0 collective-permute-done.4.extra
  62.1 2.8 %correlate.1 = (f32[4,8,8,256]{3,2,1,0:T(8,128)S(1)}, f32[4,8,8,256]{3,2,1,0:T(8,128)S(1)}) custom-call(f32[8,256]{1,0:T(8,128)S(1)} %get-tuple-element.43.weight, f32[2,8,256]{2,1,0:T(8,128)S(1)} %steps.1.scale, f32[8,8,64,256]{3,2,1,0:T(8,128)S(1)} %get-tuple-element.51.x, f32[8,8,64,256]{3,2,1,0:T(8,128)S(1)} %get-tuple-element.61.z, ...), custom_call_target="tpu_custom_call" | custom-call | tf_op jit(solution)/shard_map/correlate/pallas_call | solution.py:604
  64.9 3.7 %collective-permute-start.5 = (f32[4,8,8,256]{3,2,1,0:T(8,128)S(1)}, f32[4,8,8,256]{3,2,1,0:T(8,128)S(1)}, u32[]{:S(2)}, u32[]{:S(2)}) collective-permute-start(f32[4,8,8,256]{3,2,1,0:T(8,128)S(1)} %get-tuple-element.72), channel_id=1, source_target_pairs={{0,32},{32,0},{64,96},{96,64},{128,160},{160,128},{192,224},{224,1... | collective-permute-start | bytes 786440 | tf_op jit(solution)/shard_map/ppermute | solution.py:615
  68.6 1.2 %collective-permute-done.5.got = f32[4,8,8,256]{3,2,1,0:T(8,128)S(1)} collective-permute-done((f32[4,8,8,256]{3,2,1,0:T(8,128)S(1)}, f32[4,8,8,256]{3,2,1,0:T(8,128)S(1)}, u32[]{:S(2)}, u32[]{:S(2)}) %collective-permute-start.5) | collective-permute-done | bytes 262176 | tf_op jit(solution)/shard_map/ppermute | solution.py:615
  69.8 2.8 %collective-permute-start.6 = (f32[8,8,256]{2,1,0:T(8,128)S(1)}, f32[8,8,256]{2,1,0:T(8,128)S(1)}, u32[]{:S(2)}, u32[]{:S(2)}) collective-permute-start(f32[8,8,256]{2,1,0:T(8,128)S(1)} %get-tuple-element.74), channel_id=1, source_target_pairs={{0,128},{32,160},{64,192},{96,224},{128,0},{160,32},{192,64},{224,... | collective-permute-start | bytes 196616 | tf_op jit(solution)/shard_map/ppermute | solution.py:615
  72.7 0.3 collective-permute-start.7
  73.0 0.6 collective-permute-start.8
  73.5 1.0 %collective-permute-done.6.one = f32[8,8,256]{2,1,0:T(8,128)S(1)} collective-permute-done((f32[8,8,256]{2,1,0:T(8,128)S(1)}, f32[8,8,256]{2,1,0:T(8,128)S(1)}, u32[]{:S(2)}, u32[]{:S(2)}) %collective-permute-start.6) | collective-permute-done | bytes 65568 | tf_op jit(solution)/shard_map/ppermute | solution.py:615
  74.5 1.6 %collective-permute-done.7.two = f32[8,8,256]{2,1,0:T(8,128)S(1)} collective-permute-done((f32[8,8,256]{2,1,0:T(8,128)S(1)}, f32[8,8,256]{2,1,0:T(8,128)S(1)}, u32[]{:S(2)}, u32[]{:S(2)}) %collective-permute-start.7) | collective-permute-done | bytes 65568 | tf_op jit(solution)/shard_map/ppermute | solution.py:615
  76.1 1.1 %collective-permute-done.8.three = f32[8,8,256]{2,1,0:T(8,128)S(1)} collective-permute-done((f32[8,8,256]{2,1,0:T(8,128)S(1)}, f32[8,8,256]{2,1,0:T(8,128)S(1)}, u32[]{:S(2)}, u32[]{:S(2)}) %collective-permute-start.8) | collective-permute-done | bytes 65568 | tf_op jit(solution)/shard_map/ppermute | solution.py:615
  77.3 0.6 total.1
  (1 shorter events, 0.0 us)
Async XLA Ops:
  1.5 25.3 %collective-permute-start.2 = (f32[11,64,256]{2,1,0:T(8,128)S(1)}, f32[11,64,256]{2,1,0:T(8,128)S(1)}, u32[]{:S(2)}, u32[]{:S(2)}) collective-permute-start(f32[11,64,256]{2,1,0:T(8,128)S(1)} %get-tuple-element.41.head_a), channel_id=1, source_target_pairs={{0,1},{1,2},{2,3},{3,4},{4,5},{5,6},{6,7},{7,8},{8,9},{9,10},{10,1... | collective-permute-start | bytes 2162696 | tf_op jit(solution)/shard_map/ppermute | solution.py:504
  2.8 24.0 %collective-permute-start.3 = (f32[11,64,256]{2,1,0:T(8,128)S(1)}, f32[11,64,256]{2,1,0:T(8,128)S(1)}, u32[]{:S(2)}, u32[]{:S(2)}) collective-permute-start(f32[11,64,256]{2,1,0:T(8,128)S(1)} %get-tuple-element.42.head_b), channel_id=1, source_target_pairs={{1,0},{2,1},{3,2},{4,3},{5,4},{6,5},{7,6},{8,7},{9,8},{10,9},{11,1... | collective-permute-start | bytes 2162696 | tf_op jit(solution)/shard_map/ppermute | solution.py:504
  12.5 21.7 %collective-permute-start = (f32[12,64,256]{2,1,0:T(8,128)S(1)}, f32[12,64,256]{2,1,0:T(8,128)S(1)}, u32[]{:S(2)}, u32[]{:S(2)}) collective-permute-start(f32[12,64,256]{2,1,0:T(8,128)S(1)} %get-tuple-element.44.msg_a), channel_id=1, source_target_pairs={{0,1},{1,2},{2,3},{3,4},{4,5},{5,6},{6,7},{7,8},{8,9},{9,10},{10,1... | collective-permute-start | bytes 2359304 | tf_op jit(solution)/shard_map/ppermute | solution.py:504
  13.8 25.7 %collective-permute-start.1 = (f32[12,64,256]{2,1,0:T(8,128)S(1)}, f32[12,64,256]{2,1,0:T(8,128)S(1)}, u32[]{:S(2)}, u32[]{:S(2)}) collective-permute-start(f32[12,64,256]{2,1,0:T(8,128)S(1)} %get-tuple-element.45.msg_b), channel_id=1, source_target_pairs={{1,0},{2,1},{3,2},{4,3},{5,4},{6,5},{7,6},{8,7},{9,8},{10,9},{11,1... | collective-permute-start | bytes 2359304 | tf_op jit(solution)/shard_map/ppermute | solution.py:504
  28.9 33.2 %collective-permute-start.4 = (f32[4,64,256]{2,1,0:T(8,128)S(1)}, f32[4,64,256]{2,1,0:T(8,128)S(1)}, u32[]{:S(2)}, u32[]{:S(2)}) collective-permute-start(f32[4,64,256]{2,1,0:T(8,128)S(1)} %get-tuple-element.70), channel_id=1, source_target_pairs={{1,0},{2,1},{3,2},{4,3},{5,4},{6,5},{7,6},{8,7},{9,8},{10,9},{11,1... | collective-permute-start | bytes 786440 | tf_op jit(solution)/shard_map/ppermute | solution.py:578
  64.9 4.9 %collective-permute-start.5 = (f32[4,8,8,256]{3,2,1,0:T(8,128)S(1)}, f32[4,8,8,256]{3,2,1,0:T(8,128)S(1)}, u32[]{:S(2)}, u32[]{:S(2)}) collective-permute-start(f32[4,8,8,256]{3,2,1,0:T(8,128)S(1)} %get-tuple-element.72), channel_id=1, source_target_pairs={{0,32},{32,0},{64,96},{96,64},{128,160},{160,128},{192,224},{224,1... | collective-permute-start | bytes 786440 | tf_op jit(solution)/shard_map/ppermute | solution.py:615
  69.8 4.7 %collective-permute-start.6 = (f32[8,8,256]{2,1,0:T(8,128)S(1)}, f32[8,8,256]{2,1,0:T(8,128)S(1)}, u32[]{:S(2)}, u32[]{:S(2)}) collective-permute-start(f32[8,8,256]{2,1,0:T(8,128)S(1)} %get-tuple-element.74), channel_id=1, source_target_pairs={{0,128},{32,160},{64,192},{96,224},{128,0},{160,32},{192,64},{224,... | collective-permute-start | bytes 196616 | tf_op jit(solution)/shard_map/ppermute | solution.py:615
  72.7 3.5 %collective-permute-start.7 = (f32[8,8,256]{2,1,0:T(8,128)S(1)}, f32[8,8,256]{2,1,0:T(8,128)S(1)}, u32[]{:S(2)}, u32[]{:S(2)}) collective-permute-start(f32[8,8,256]{2,1,0:T(8,128)S(1)} %get-tuple-element.75), channel_id=1, source_target_pairs={{0,64},{32,96},{64,0},{96,32},{128,192},{160,224},{192,128},{224,1... | collective-permute-start | bytes 196616 | tf_op jit(solution)/shard_map/ppermute | solution.py:615
  73.0 4.3 %collective-permute-start.8 = (f32[8,8,256]{2,1,0:T(8,128)S(1)}, f32[8,8,256]{2,1,0:T(8,128)S(1)}, u32[]{:S(2)}, u32[]{:S(2)}) collective-permute-start(f32[8,8,256]{2,1,0:T(8,128)S(1)} %get-tuple-element.76), channel_id=1, source_target_pairs={{0,192},{32,224},{64,128},{96,160},{128,64},{160,96},{192,0},{224,... | collective-permute-start | bytes 196616 | tf_op jit(solution)/shard_map/ppermute | solution.py:615
